TPU v7x, 32 devices: a whole 2x2x4 slice. The times are simulated.
32 devices in a mesh: dp: 8 (over z, x), tensor: 4 (over y, core).
Axes of the slice: x: 2, y: 2, z: 4, core: 2. Of those that a mesh axis runs over, the one named last changes fastest.
Arguments:
- tokens: bfloat16 [1024, 4096], P(('dp', 'tensor')), may hold values from -6 to 6
- query_base_weight: bfloat16 [4096, 4096], P(None, 'tensor'), may hold values from -0.09375 to 0.09375
- adapter_down_weight: bfloat16 [8, 16, 4096], P('dp', None, 'tensor'), may hold values from -0.09375 to 0.09375
- adapter_up_weight: bfloat16 [8, 16, 4096], P('dp', None, 'tensor'), may hold values from -0.375 to 0.375
- upstream: bfloat16 [1024, 4096], P('dp', 'tensor'), may hold values from -6 to 6
- adapter_per_block: int32 [8, 1], P('dp'), may hold values from 0 to 7
- owner: int32 [8], replicated, may hold values from 0 to 7, each once
Outputs:
- mixed: bfloat16 [1024, 4096], P('dp', 'tensor')
- input_gradient: bfloat16 [1024, 4096], P(('dp', 'tensor'))
- down_gradient: float32 [8, 16, 4096], P('dp', None, 'tensor')
- up_gradient: float32 [8, 16, 4096], P('dp', None, 'tensor')
Inputs may be any that keep to these rules, and one draw needn't show every extreme that they name: `adapter_per_block`: every adapter has at least one block. `owner`: each slot is taken by exactly one adapter.
All inputs are finite; a program needn't handle non-finite values.
Results may differ from a plain program's by a relative error of at most 0.0032.
Values may be sent and summed in bfloat16 or wider, within the bound.
No kernel may reach another device: no remote copies, remote signals or barrier semaphores. Data moves between devices by JAX's collectives and lax.ppermute only.
A program may use at most 128 MiB of HBM per device.

v0:
```python
import jax
import jax.numpy as jnp
from jax import lax
from jax.sharding import PartitionSpec as P

adapter_scale = 2.0


def per_device(
    tokens,
    query_base_weight,
    adapter_down_weight,
    adapter_up_weight,
    upstream,
    adapter_per_block,
    owner,
):
    tensor_index = lax.axis_index("tensor")
    col_width = query_base_weight.shape[1]
    blocks_here = adapter_per_block.shape[0]
    adapter_count = owner.shape[0]
    rank_width = adapter_down_weight.shape[1]
    gathered = lax.all_gather(tokens, "tensor", axis=0, tiled=True)
    block_len = gathered.shape[0] // blocks_here
    slot_indices = jnp.take(owner, adapter_per_block[:, 0])
    onehot = slot_indices[:, None] == jnp.arange(adapter_count, dtype=jnp.int32)[None, :]
    select = onehot.astype(jnp.bfloat16)
    down_all, up_all = (
        lax.all_gather(adapter_down_weight, "dp", axis=0, tiled=True),
        lax.all_gather(adapter_up_weight, "dp", axis=0, tiled=True),
    )
    down_pick = jnp.dot(
        select, down_all.reshape(adapter_count, -1), preferred_element_type=jnp.float32
    )
    up_pick = jnp.dot(select, up_all.reshape(adapter_count, -1), preferred_element_type=jnp.float32)
    down_chosen = down_pick.astype(jnp.bfloat16).reshape(blocks_here, rank_width, col_width)
    up_chosen = up_pick.astype(jnp.bfloat16).reshape(blocks_here, rank_width, col_width)
    owned_columns = lax.dynamic_slice_in_dim(gathered, tensor_index * col_width, col_width, 1)
    owned_columns = owned_columns.reshape(blocks_here, block_len, col_width)
    backward_blocks = upstream.reshape(blocks_here, block_len, col_width)
    reduced_portion = jnp.einsum(
        "mtn,myn->mty", owned_columns, down_chosen, preferred_element_type=jnp.float32
    )
    backward_portion = jnp.einsum(
        "mtn,myn->mty", backward_blocks, up_chosen, preferred_element_type=jnp.float32
    )
    reduced_hidden, reduced_backward = lax.psum((reduced_portion, backward_portion), "tensor")
    reduced_hidden = reduced_hidden.astype(jnp.bfloat16)
    reduced_backward = reduced_backward.astype(jnp.bfloat16)
    mixed = jnp.dot(gathered, query_base_weight, preferred_element_type=jnp.float32)
    mixed = mixed + adapter_scale * jnp.einsum(
        "xzv,xva->xza", reduced_hidden, up_chosen, preferred_element_type=jnp.float32
    ).reshape(-1, col_width)
    adapter_branch_term = adapter_scale * jnp.einsum(
        "xzv,xva->xza", reduced_backward, down_chosen, preferred_element_type=jnp.float32
    ).reshape(-1, col_width)
    partial_rows = lax.dot_general(
        upstream, query_base_weight, (((1,), (1,)), ((), ())), preferred_element_type=jnp.float32
    )
    current = lax.dynamic_slice_in_dim(partial_rows, tensor_index * col_width, col_width, 1)
    input_gradient = lax.psum_scatter(
        lax.dynamic_update_slice_in_dim(
            partial_rows, current + adapter_branch_term, tensor_index * col_width, 1
        ),
        "tensor",
        scatter_dimension=0,
        tiled=True,
    ).astype(jnp.bfloat16)
    down_contributions = adapter_scale * jnp.einsum(
        "phl,phj->plj", reduced_backward, owned_columns, preferred_element_type=jnp.float32
    )
    up_contributions = adapter_scale * jnp.einsum(
        "phl,phj->plj", reduced_hidden, backward_blocks, preferred_element_type=jnp.float32
    )
    spread = onehot.astype(jnp.float32).T
    dense_down = jnp.dot(
        spread, down_contributions.reshape(blocks_here, -1), precision=lax.Precision.HIGHEST
    )
    dense_up = jnp.dot(
        spread, up_contributions.reshape(blocks_here, -1), precision=lax.Precision.HIGHEST
    )
    down_gradient, up_gradient = (
        lax.psum_scatter(dense_down, "dp", scatter_dimension=0, tiled=True),
        lax.psum_scatter(dense_up, "dp", scatter_dimension=0, tiled=True),
    )
    down_gradient = down_gradient.reshape(adapter_down_weight.shape)
    up_gradient = up_gradient.reshape(adapter_up_weight.shape)
    return (mixed.astype(jnp.bfloat16), input_gradient, down_gradient, up_gradient)


def solution(mesh):
    return jax.shard_map(
        per_device,
        mesh=mesh,
        in_specs=(
            P(("dp", "tensor"), None),
            P(None, "tensor"),
            P("dp", None, "tensor"),
            P("dp", None, "tensor"),
            P("dp", "tensor"),
            P("dp", None),
            P(),
        ),
        out_specs=(
            P("dp", "tensor"),
            P(("dp", "tensor"), None),
            P("dp", None, "tensor"),
            P("dp", None, "tensor"),
        ),
        check_vma=False,
    )
```

profile of v0, /device:TPU:0, one launch (start us, length us, event | category | flops | bytes accessed | tf_op | source)
XLA Modules:
  0.0 210.6 jit_solution(5244636170388985395)
XLA Ops:
  7.2 0.0 copy-start
  7.2 0.0 all-gather.2.cloned.1.call-start
  7.2 0.7 all-gather.2.cloned.1.call-update
  7.9 0.0 all-reduce.6.cloned.1.call-start
  8.6 32.7 %all_gather.10 = bf16[8,16,1024]{2,1,0:T(8,128)(2,1)S(1)} all-gather(bf16[1,16,1024]{2,1,0:T(8,128)(2,1)} %param.9), channel_id=1, replica_groups=mesh['dp'=8,'tensor'=4] {'dp'}, dimensions={0}, use_global_device_ids=true | all-gather | bytes 294912 | tf_op jit(solution)/shard_map/all_gather | solution.py:29
  41.4 0.1 copy.11
  41.5 1.2 dynamic-slice.2
  43.4 0.2 fusion.18
  43.7 31.0 %all_gather.11 = bf16[8,16,1024]{2,1,0:T(8,128)(2,1)S(1)} all-gather(bf16[1,16,1024]{2,1,0:T(8,128)(2,1)} %param.10), channel_id=1, replica_groups=mesh['dp'=8,'tensor'=4] {'dp'}, dimensions={0}, use_global_device_ids=true | all-gather | bytes 294912 | tf_op jit(solution)/shard_map/all_gather | solution.py:30
  74.6 0.1 copy.12
  74.8 0.2 fusion.16
  75.0 0.0 copy-done
  75.0 0.2 convolution_bitcast_fusion
  75.2 0.0 all-gather.2.cloned.1.call-done
  75.2 1.1 convolution_bitcast_fusion.1
  76.3 10.2 %all-reduce.3 = (bf16[1,128,16]{1,2,0:T(8,128)(2,1)S(1)}, bf16[1,128,16]{1,2,0:T(8,128)(2,1)S(1)}) all-reduce(f32[1,128,16]{1,2,0:T(8,128)S(1)} %convolution_bitcast_fusion.1, f32[1,128,16]{1,2,0:T(8,128)S(1)} %convolution_bitcast_fusion), channel_id=1, replica_groups=mesh['dp'=8,'tensor'=4] {'tensor'}, use_global_device_ids=true, to_apply=%region_0.1 | all-reduce | flops 4096 | bytes 24576 | tf_op jit(solution)/shard_map/psum | solution.py:47
  86.5 0.2 fusion.4
  86.7 0.0 copy-start.3
  86.7 0.0 copy-start.2
  86.7 1.2 fusion.5
  87.9 1.2 broadcast_multiply_fusion
  89.1 0.0 all-reduce.6.cloned.1.call-update
  89.1 0.0 reduce-scatter.2.cloned.1.call-start
  89.2 6.2 %fusion.25 = f32[128,4096]{1,0:T(8,128)S(1)} fusion(bf16[128,1024]{1,0:T(8,128)(2,1)S(1)} %copy-done, bf16[4096,1024]{1,0:T(8,128)(2,1)} %param.8), kind=kOutput, calls=%fused_computation.37 | convolution fusion | flops 1073741824 | bytes 10747904 | tf_op jit(solution)/shard_map/dot_general | solution.py:57
  95.4 0.3 fusion.2
  95.7 0.0 copy-start.1
  95.7 1.3 copy-done.1
  97.0 0.0 reduce-scatter.2.cloned.1.call-update
  97.0 0.0 copy-done.3
  97.0 0.6 dynamic-slice.3
  97.6 0.0 copy-done.2
  97.6 4.6 %fusion.24 = f32[128,1024]{1,0:T(8,128)S(1)} fusion(bf16[128,4096]{1,0:T(8,128)(2,1)S(1)} %copy-done.2, bf16[4096,1024]{1,0:T(8,128)(2,1)} %param.8), kind=kOutput, calls=%fused_computation.36 | convolution fusion | flops 1073741824 | bytes 9961472 | tf_op jit(solution)/shard_map/dot_general | solution.py:50
  102.3 1.0 fusion.3
  103.2 65.5 %all-reduce.6.cloned.1.call-done = (f32[8,16384]{1,0:T(8,128)}, f32[8,16384]{1,0:T(8,128)}) async-done(((f32[8,16384]{1,0:T(8,128)}, f32[8,16384]{1,0:T(8,128)}), (f32[8,16384]{1,0:T(8,128)}, f32[8,16384]{1,0:T(8,128)})) %all-reduce.6.cloned.1.call-update) | async-done | bytes 1048592
  168.8 2.2 %dynamic-slice_reduce_fusion = (f32[16384]{0:T(1024)S(1)}, f32[16384]{0:T(1024)S(1)}) fusion(f32[8,16384]{1,0:T(8,128)} %get-tuple-element.16, u32[]{:T(128)} %bitcast.14, f32[8,16384]{1,0:T(8,128)} %get-tuple-element.15), kind=kLoop, calls=%fused_computation.16 | loop fusion | bytes 262148
  171.0 0.6 reshape.131
  171.6 0.6 reshape.129
  172.3 30.0 %reduce-scatter.2.cloned.1.call-done = f32[32,4096]{1,0:T(8,128)} async-done(((f32[128,4096]{1,0:T(8,128)}), f32[32,4096]{1,0:T(8,128)}) %reduce-scatter.2.cloned.1.call-update) | async-done | bytes 524304 | tf_op jit(solution)/shard_map/reduce_scatter | solution.py:61
  202.3 1.8 convert_element_type.27
  (7 shorter events, 0.1 us)
Async XLA Ops:
  7.2 67.9 %copy-start = (bf16[128,1024]{1,0:T(8,128)(2,1)S(1)}, bf16[128,1024]{1,0:T(8,128)(2,1)}, u32[]{:S(2)}) copy-start(bf16[128,1024]{1,0:T(8,128)(2,1)} %param.11) | copy-start | bytes 786436
  7.2 68.0 %all-gather.2.cloned.1.call-start = ((), (), s32[]{:S(2)}) async-start(), calls=%async_computation.1 | async-start | bytes 1310720 | tf_op jit(solution)/shard_map/all_gather | solution.py:23
  7.9 160.8 %all-reduce.6.cloned.1.call-start = ((), (), s32[]{:S(2)}) async-start(), calls=%async_computation.3 | async-start | bytes 2097152
  86.7 10.4 %copy-start.3 = (u32[32]{0:T(128)S(1)}, u32[32]{0:T(128)}, u32[]{:S(2)}) copy-start(u32[32]{0:T(128)} %constant.55) | copy-start | bytes 388
  86.7 10.9 %copy-start.2 = (bf16[128,4096]{1,0:T(8,128)(2,1)S(1)}, bf16[128,4096]{1,0:T(8,128)(2,1)}, u32[]{:S(2)}) copy-start(bf16[128,4096]{1,0:T(8,128)(2,1)} %all-gather.2.cloned.1.call-done) | copy-start | bytes 3145732
  89.1 113.2 %reduce-scatter.2.cloned.1.call-start = ((), (), s32[]{:S(2)}) async-start(), calls=%async_computation.2 | async-start | bytes 2621440 | tf_op jit(solution)/shard_map/reduce_scatter | solution.py:61
  95.7 1.3 copy-start.1
Sparse Core Ops, SparseCore 0:
  9.6 19.4 all-gather.1
  89.2 79.4 all-reduce.5
  171.4 30.8 reduce-scatter.1
where the time goes:
time: 211 us
  waiting for transfers between devices  96.3 us (46%)
  blocking collectives  73.9 us (35%)
  between operations  15.2 us (7%)
  matrix products  15.1 us (7%)
  local copies, waits for them, and re-layouts  7.03 us (3%)
  other arithmetic  2.96 us (1%)
    unnamed x4, waiting for transfers between devices  66.3 us
    all_gather x1, blocking collectives, per_device(): lax.all_gather(adapter_down_weight, 'dp', axis=0, tiled=True)  32.7 us
    all_gather x1, blocking collectives, per_device(): lax.all_gather(adapter_up_weight, 'dp', axis=0, tiled=True)  31 us
    reduce_scatter x1, waiting for transfers between devices, per_device(): lax.psum_scatter(lax.dynamic_update_slice_in_dim(partial_rows, current +...  30 us
    psum x1, blocking collectives, per_device(): lax.psum((reduced_portion, backward_portion), 'tensor')  10.2 us
    dot_general x1, matrix products, per_device(): lax.dot_general(upstream, query_base_weight, (((1,), (1,)), ((), ())), pr...  6.23 us
    dot_general x1, matrix products, per_device(): jnp.dot(gathered, query_base_weight, preferred_element_type=jnp.float32)  4.63 us
    unnamed x14, local copies, waits for them, and re-layouts  4.46 us
  transfers between devices with their start and end apart: 3, of which 2 were waited for; matrix products, arithmetic and copies ran while one was open for 9% of the time, Pallas kernels for 0%

commit v1 on v0

v1 whole, which is shorter than its diff:
```python
import functools

import jax
import jax.numpy as jnp
from jax import lax
from jax.experimental import pallas as pl
from jax.experimental.pallas import tpu as pltpu
from jax.sharding import PartitionSpec as P

adapter_scale = 2.0
bf16, f32 = jnp.bfloat16, jnp.float32
nt = (((1,), (1,)), ((), ()))
tn = (((0,), (0,)), ((), ()))
small_limit = 16 * 1024 * 1024
pieces_of_weight = 8
small_bytes = 8 * 1024 * 1024


def vmem():
    return pl.BlockSpec(memory_space=pltpu.VMEM)


def shape(dims, dtype):
    return jax.ShapeDtypeStruct(dims, dtype)


def call(
    body, name, outs, operands, specs, scratch=(), flops=0, moved=0, limit=small_limit, after=()
):
    count = len(operands)

    def run(*refs):
        body(*refs[:count], *refs[count + len(after) :])

    return list(
        pl.pallas_call(
            run,
            name=name,
            out_shape=outs,
            in_specs=specs + [pl.BlockSpec(memory_space=pl.ANY)] * len(after),
            out_specs=[vmem()] * len(outs),
            scratch_shapes=list(scratch),
            cost_estimate=pl.CostEstimate(flops=flops, bytes_accessed=moved, transcendentals=0),
            compiler_params=pltpu.CompilerParams(vmem_limit_bytes=limit),
        )(*operands, *after)
    )


def log2(n):
    return n.bit_length() - 1


def choose(refs, key):
    chosen = None
    for k in range(len(refs)):
        one = jnp.where(key == k, 1.0, 0.0).astype(bf16) * refs[k][...]
        chosen = one if chosen is None else chosen + one
    return chosen


def slot_kernel(*refs):
    owner, blocks = refs[0], refs[1:-5]
    tokens, upstream, slots, tokens_here, upstream_here = refs[-5:]
    tokens_here[...] = tokens[...]
    upstream_here[...] = upstream[...]
    adapters = lax.broadcasted_iota(jnp.int32, owner.shape, 1)
    for k in range(len(blocks)):
        here = jnp.where(adapters == blocks[k][...], owner[...], 0)
        slot = jnp.sum(here, axis=1, keepdims=True)
        slots[k : k + 1, :] = jnp.broadcast_to(slot, (1, slots.shape[1]))


def base_kernel(upstream, weight, keep, give, rows_of):
    t = lax.axis_index("tensor")
    rows = keep.shape[1]
    half = keep.shape[0]
    step = weight.shape[0] // pieces_of_weight
    for n in range(half):
        for side in range(2):
            start = pl.multiple_of((2 * n + ((t & 1) ^ side)) * rows, rows)
            at = (side * half + n) * rows
            rows_of[at : at + rows, :] = upstream[pl.ds(start, rows), :]
    for n in range(pieces_of_weight):
        part = lax.dot_general(rows_of[...], weight[n * step : (n + 1) * step, :], nt, preferred_element_type=f32)
        for m in range(half):
            keep[m, :, n * step : (n + 1) * step] = part[m * rows : (m + 1) * rows]
            at = (half + m) * rows
            give[m, :, n * step : (n + 1) * step] = part[at : at + rows]


def own_kernel(source, target):
    target[...] = source[...]


def pick_kernel(near, far, *refs):
    slots, group, found = refs[0], refs[1 : 1 + near], refs[1 + near :]
    i = lax.axis_index("dp") & (near - 1)
    for k in range(far):
        found[k][...] = choose(group, (slots[k : k + 1, :1] & (near - 1)) ^ i)


def low_kernel(near, far, parts, *refs):
    slots, found = refs[0], refs[1 : 1 + far]
    tokens = refs[1 + far : 1 + far + parts]
    upstream, both, chosen, columns, down = refs[1 + far + parts :]
    o = lax.axis_index("dp") >> log2(near)
    t = lax.axis_index("tensor")
    cols = columns.shape[1]
    rows = columns.shape[0] // parts
    rank = chosen.shape[0] // 2
    chosen[...] = choose(found, (slots[:1, :1] >> log2(near)) ^ o)
    down[...] = chosen[:rank, :]
    start = pl.multiple_of(t * cols, cols)
    for k in range(parts):
        at = pl.multiple_of((t ^ k) * rows, rows)
        columns[pl.ds(at, rows), :] = tokens[k][:, pl.ds(start, cols)]
    both[:rank, :] = lax.dot_general(
        chosen[:rank, :], columns[...], nt, preferred_element_type=f32
    )
    both[rank:, :] = lax.dot_general(
        chosen[rank:, :], upstream[...], nt, preferred_element_type=f32
    )


def gradient_kernel(parts, *refs):
    totals = refs[:parts]
    columns, upstream, low, term = refs[parts:]
    rank = low.shape[0] // 2
    total = totals[0][...]
    for k in range(1, parts):
        total = total + totals[k][...]
    low[...] = total.astype(bf16)
    down_term = jnp.dot(low[rank:, :], columns[...], preferred_element_type=f32)
    up_term = jnp.dot(low[:rank, :], upstream[...], preferred_element_type=f32)
    term[:rank, :] = (adapter_scale * down_term).astype(bf16)
    term[rank:, :] = (adapter_scale * up_term).astype(bf16)


def route_kernel(near, far, *refs):
    slots, terms, parts = refs[0], refs[1 : 1 + far], refs[1 + far :]
    d = lax.axis_index("dp")
    for m in range(near):
        part = None
        for k in range(far):
            here = jnp.where(slots[k : k + 1, :1] == (d ^ m), 1.0, 0.0).astype(bf16)
            one = here * terms[k][...]
            part = one if part is None else part + one
        parts[m][...] = part


def add_kernel(keep, got, low, chosen, sibling, hold, give, total, term):
    t = lax.axis_index("tensor")
    half, rows = keep.shape[0], keep.shape[1]
    rank, cols = sibling.shape
    high = t >> 1
    total[...] = keep[...] + got[...]
    for k, down in ((0, chosen), (1, sibling)):
        term[...] = adapter_scale * lax.dot_general(
            low[rank:, :], down[:rank, :], tn, preferred_element_type=f32
        )
        at = pl.multiple_of((t ^ k) * cols, cols)
        for n in range(half):
            start = pl.multiple_of((2 * n + (t & 1)) * rows, rows)
            total[n, :, pl.ds(at, cols)] += term[pl.ds(start, rows), :]
    hold[...] = total[high]
    give[...] = total[1 - high].astype(bf16)


def mixed_kernel(parts, *refs):
    tokens = refs[:parts]
    weight, total, gathered = refs[parts:]
    t = lax.axis_index("tensor")
    rows = tokens[0].shape[0]
    step = weight.shape[0] // pieces_of_weight
    for k in range(parts):
        at = pl.multiple_of((t ^ k) * rows, rows)
        gathered[pl.ds(at, rows), :] = tokens[k][...]
    for n in range(pieces_of_weight):
        part = jnp.dot(
            gathered[:, n * step : (n + 1) * step],
            weight[n * step : (n + 1) * step, :],
            preferred_element_type=f32,
        )
        total[...] = part if n == 0 else total[...] + part


def finish_kernel(mixed, low, chosen, out):
    rank = low.shape[0] // 2
    term = lax.dot_general(low[:rank, :], chosen[rank:, :], tn, preferred_element_type=f32)
    out[...] = (mixed[...] + adapter_scale * term).astype(bf16)


def close_kernel(hold, got, out, done):
    out[...] = (hold[...] + got[...].astype(f32)).astype(bf16)
    done[...] = jnp.zeros(done.shape, f32)


def sum_kernel(*refs):
    parts, down, up = refs[:-2], refs[-2], refs[-1]
    rank = down.shape[1]
    total = parts[0][...].astype(f32)
    for part in parts[1:]:
        total = total + part[...].astype(f32)
    down[0] = total[:rank, :]
    up[0] = total[rank:, :]


def make_per_device(dp_size, tensor_size):
    near = 1 << ((log2(dp_size) + 1) // 2)
    far = dp_size // near
    half = tensor_size // 2

    def over_tensor(x, k):
        return lax.ppermute(x, "tensor", [(t, t ^ k) for t in range(tensor_size)])

    def over_near(x, k):
        return lax.ppermute(x, "dp", [(d, d ^ k) for d in range(dp_size)])

    def over_far(x, k):
        return lax.ppermute(x, "dp", [(d, d ^ (k * near)) for d in range(dp_size)])

    def per_device(tokens, weight, down, up, upstream, adapter_per_block, owner):
        rank, cols = down.shape[1], down.shape[2]
        rows, width = tokens.shape
        length = upstream.shape[0]
        weight_bytes = weight.shape[0] * cols * 2
        flops = 2 * length * weight.shape[0] * cols

        mine = jnp.concatenate([down[0], up[0]], axis=0)
        group = [mine] + [over_near(mine, k) for k in range(1, near)]
        across = over_tensor(tokens, half)
        blocks = [adapter_per_block]
        blocks += [over_far(adapter_per_block, k) for k in range(1, far)]

        (group[0],) = call(
            own_kernel,
            "own",
            [shape(mine.shape, bf16)],
            (mine,),
            [vmem()],
            flops=8 * flops,
            after=(across, *blocks[1:]),
        )
        slots, tokens_here, upstream_here = call(
            slot_kernel,
            "slots",
            [
                shape((far, 128), jnp.int32),
                shape(tokens.shape, bf16),
                shape(upstream.shape, bf16),
            ],
            (owner.reshape(1, -1), *blocks, tokens, upstream),
            [vmem()] * (far + 3),
            flops=flops,
            moved=small_bytes,
            after=(group[0],),
        )
        pieces = [tokens_here, over_tensor(tokens_here, 1), across, over_tensor(across, 1)]
        found = call(
            functools.partial(pick_kernel, near, far),
            "pick",
            [shape((2 * rank, cols), bf16)] * far,
            (slots, *group),
            [vmem()] * (1 + near),
            flops=flops,
            moved=small_bytes,
        )
        keep, give = call(
            base_kernel,
            "base",
            [shape((half, rows, width), f32)] * 2,
            (upstream_here, weight),
            [vmem(), vmem()],
            [pltpu.VMEM((length, cols), bf16)],
            flops,
            weight_bytes,
            after=(found[0],),
        )
        found = [found[0]] + [over_far(found[k], k) for k in range(1, far)]

        both, chosen, columns, chosen_down = call(
            functools.partial(low_kernel, near, far, tensor_size),
            "low",
            [
                shape((2 * rank, length), f32),
                shape((2 * rank, cols), bf16),
                shape((length, cols), bf16),
                shape((rank, cols), bf16),
            ],
            (slots, *found, *pieces, upstream_here),
            [vmem()] * (1 + far + tensor_size + 1),
            flops=flops,
            moved=small_bytes,
        )
        (mixed,) = call(
            functools.partial(mixed_kernel, tensor_size),
            "mixed",
            [shape((length, cols), f32)],
            (*pieces, weight),
            [vmem()] * (tensor_size + 1),
            [pltpu.VMEM((length, width), bf16)],
            flops,
            weight_bytes,
            after=(both,),
        )
        give, both = lax.optimization_barrier((give, both))
        got = over_tensor(give, 1)
        sibling = over_tensor(chosen_down, 1)
        totals = [both] + [over_tensor(both, k) for k in range(1, tensor_size)]

        low, term = call(
            functools.partial(gradient_kernel, tensor_size),
            "gradient",
            [shape((2 * rank, length), bf16), shape((2 * rank, cols), bf16)],
            (*totals, columns, upstream_here),
            [vmem()] * (tensor_size + 2),
            after=(mixed, sibling),
        )
        terms = [term] + [over_far(term, k) for k in range(1, far)]

        hold, give = call(
            add_kernel,
            "add",
            [shape((rows, width), f32), shape((rows, width), bf16)],
            (keep, got, low, chosen, sibling),
            [vmem()] * 5,
            [pltpu.VMEM((half, rows, width), f32), pltpu.VMEM((length, cols), f32)],
        )
        got = over_tensor(give, half)

        routed = call(
            functools.partial(route_kernel, near, far),
            "route",
            [shape((2 * rank, cols), bf16)] * near,
            (slots, *terms),
            [vmem()] * (1 + far),
            after=(give,),
        )
        parts = [routed[0]] + [over_near(routed[m], m) for m in range(1, near)]
        (mixed,) = call(
            finish_kernel,
            "finish",
            [shape((length, cols), bf16)],
            (mixed, low, chosen),
            [vmem()] * 3,
            flops=4 * flops,
            after=(routed[0],),
        )
        input_gradient, done = call(
            close_kernel,
            "close",
            [shape((rows, width), bf16), shape((8, 128), f32)],
            (hold, got),
            [vmem()] * 2,
        )
        down_gradient, up_gradient = call(
            sum_kernel,
            "sum",
            [shape(down.shape, f32)] * 2,
            parts,
            [vmem()] * near,
            after=(done,),
        )
        return mixed, input_gradient, down_gradient, up_gradient

    return per_device


def solution(mesh):
    return jax.shard_map(
        make_per_device(mesh.shape["dp"], mesh.shape["tensor"]),
        mesh=mesh,
        in_specs=(
            P(("dp", "tensor"), None),
            P(None, "tensor"),
            P("dp", None, "tensor"),
            P("dp", None, "tensor"),
            P("dp", "tensor"),
            P("dp", None),
            P(),
        ),
        out_specs=(
            P("dp", "tensor"),
            P(("dp", "tensor"), None),
            P("dp", None, "tensor"),
            P("dp", None, "tensor"),
        ),
        check_vma=False,
    )
```

time: 211 us -> 40.1 us (0.19)
  waiting for transfers between devices: 96.3 us -> 7.72 us
  blocking collectives: 73.9 us -> 0 us
  starting transfers between devices: 0.12 us -> 20.1 us
  matrix products: 15.1 us -> 0 us
  between operations: 15.2 us -> 1.62 us
  Pallas kernels: 0 us -> 9.7 us
  local copies, waits for them, and re-layouts: 7.03 us -> 0.03 us
  other arithmetic: 2.96 us -> 0.78 us
    unnamed x4 -> x0, waiting for transfers between devices: 66.3 us -> none
    all_gather x2 -> x0, blocking collectives: 63.7 us -> none  [the longest x1 32.7 us: per_device(): lax.all_gather(adapter_down_weight, 'dp', axis=0, tiled=True)]
    reduce_scatter x1 -> x0, waiting for transfers between devices: 30 us -> none  [per_device(): lax.psum_scatter(lax.dynamic_update_slice_in_dim(partial_rows, current +...]
    ppermute x0 -> x18, starting transfers between devices: none -> 20.1 us  [the longest x9 7.38 us: over_tensor(): return lax.ppermute(x, 'tensor', [(t, t ^ k) for t in range(tensor_size)])]
    dot_general x10 -> x0, matrix products: 15.1 us -> none  [the longest x1 6.23 us: per_device(): lax.dot_general(upstream, query_base_weight, (((1,), (1,)), ((), ())), pr...]
    psum x1 -> x0, blocking collectives: 10.2 us -> none  [per_device(): lax.psum((reduced_portion, backward_portion), 'tensor')]
    pallas_call x0 -> x12, Pallas kernels: none -> 9.7 us  [call(): pl.pallas_call(run, name=name, out_shape=outs, in_specs=specs + [pl.Block...]
    ppermute x0 -> x18, waiting for transfers between devices: none -> 7.72 us  [the longest x3 6.2 us: over_far(): return lax.ppermute(x, 'dp', [(d, d ^ k * near) for d in range(dp_size)])]
  transfers between devices with their start and end apart: 3 -> 18, of which waited for: 2 -> 5; matrix products, arithmetic and copies ran while one was open for 9% -> 2% of each run, Pallas kernels for 0% -> 22%
where the time goes in v1:
time: 40.1 us; the launch traced here: 39.9 us
  starting transfers between devices  20.1 us (50%)
  Pallas kernels  9.7 us (24%)
  waiting for transfers between devices  7.72 us (19%)
  between operations  1.62 us (4%)
  other arithmetic  0.78 us (2%)
    pallas_call x12, Pallas kernels, call(): pl.pallas_call(run, name=name, out_shape=outs, in_specs=specs + [pl.Block...  9.7 us
    ppermute x9, starting transfers between devices, over_tensor(): return lax.ppermute(x, 'tensor', [(t, t ^ k) for t in range(tensor_size)])  7.38 us
    ppermute x6, starting transfers between devices, over_near(): return lax.ppermute(x, 'dp', [(d, d ^ k) for d in range(dp_size)])  7.04 us
    ppermute x3, waiting for transfers between devices, over_far(): return lax.ppermute(x, 'dp', [(d, d ^ k * near) for d in range(dp_size)])  6.2 us
    ppermute x3, starting transfers between devices, over_far(): return lax.ppermute(x, 'dp', [(d, d ^ k * near) for d in range(dp_size)])  5.63 us
    ppermute x6, waiting for transfers between devices, over_near(): return lax.ppermute(x, 'dp', [(d, d ^ k) for d in range(dp_size)])  1.45 us
  transfers between devices with their start and end apart: 18, of which 5 were waited for; matrix products, arithmetic and copies ran while one was open for 2% of the time, Pallas kernels for 22%

profile of v1, /device:TPU:0, one launch (start us, length us, event | category | flops | bytes accessed | tf_op | source)
XLA Modules:
  0.0 39.9 jit_solution(9138684511275688810)
XLA Ops:
  0.6 3.0 %collective-permute-start.1 = (bf16[32,4096]{1,0:T(8,128)(2,1)}, bf16[32,4096]{1,0:T(8,128)(2,1)S(1)}, u32[]{:S(2)}, u32[]{:S(2)}) collective-permute-start(bf16[32,4096]{1,0:T(8,128)(2,1)} %refs_3_.1), channel_id=1, source_target_pairs={{0,2},{1,3},{2,0},{3,1},{4,6},{5,7},{6,4},{7,5},{8,10},{9,11},{10,... | collective-permute-start | bytes 786440 | tf_op jit(solution)/shard_map/ppermute | solution.py:214
  3.7 0.8 %pad_maximum_fusion.refs_0_ = bf16[32,1024]{1,0:T(8,128)(2,1)S(1)} fusion(bf16[16,1024]{1,0:T(8,128)(2,1)} %bitcast.6, bf16[16,1024]{1,0:T(8,128)(2,1)} %bitcast.7), kind=kLoop, calls=%fused_computation | loop fusion | flops 131072 | bytes 131072 | tf_op jit(solution)/shard_map/concatenate | solution.py:229
  4.4 2.5 %collective-permute-start.6 = (bf16[32,1024]{1,0:T(8,128)(2,1)S(1)}, bf16[32,1024]{1,0:T(8,128)(2,1)S(1)}, u32[]{:S(2)}, u32[]{:S(2)}) collective-permute-start(bf16[32,1024]{1,0:T(8,128)(2,1)S(1)} %pad_maximum_fusion.refs_0_), channel_id=1, source_target_pairs={{0,12},{4,8},{8,4},{12,0},{16,28},{20,24},{24,20},{28,16},{1,13},{... | collective-permute-start | bytes 196616 | tf_op jit(solution)/shard_map/ppermute | solution.py:217
  6.9 0.4 %collective-permute-start.5 = (bf16[32,1024]{1,0:T(8,128)(2,1)S(1)}, bf16[32,1024]{1,0:T(8,128)(2,1)S(1)}, u32[]{:S(2)}, u32[]{:S(2)}) collective-permute-start(bf16[32,1024]{1,0:T(8,128)(2,1)S(1)} %pad_maximum_fusion.refs_0_), channel_id=1, source_target_pairs={{0,8},{4,12},{8,0},{12,4},{16,24},{20,28},{24,16},{28,20},{1,9},{5... | collective-permute-start | bytes 196616 | tf_op jit(solution)/shard_map/ppermute | solution.py:217
  7.4 0.5 %collective-permute-start.4 = (bf16[32,1024]{1,0:T(8,128)(2,1)S(1)}, bf16[32,1024]{1,0:T(8,128)(2,1)S(1)}, u32[]{:S(2)}, u32[]{:S(2)}) collective-permute-start(bf16[32,1024]{1,0:T(8,128)(2,1)S(1)} %pad_maximum_fusion.refs_0_), channel_id=1, source_target_pairs={{0,4},{4,0},{8,12},{12,8},{16,20},{20,16},{24,28},{28,24},{1,5},{5... | collective-permute-start | bytes 196616 | tf_op jit(solution)/shard_map/ppermute | solution.py:217
  7.9 2.6 %collective-permute-start = (s32[1,1]{1,0:T(1,128)}, s32[1,1]{1,0:T(1,128)}, u32[]{:S(2)}, u32[]{:S(2)}) collective-permute-start(s32[1,1]{1,0:T(1,128)} %param.12), channel_id=1, source_target_pairs={{0,16},{4,20},{8,24},{12,28},{16,0},{20,4},{24,8},{28,12},{1,17},{... | collective-permute-start | bytes 20 | tf_op jit(solution)/shard_map/ppermute | solution.py:220
  10.5 0.0 slice-start
  11.3 0.0 copy-start
  11.3 0.0 copy-start.1
  11.4 0.0 copy-start.2
  11.4 0.0 slice-start.1
  11.4 0.0 collective-permute-done.1.refs_1_.refs_5_.refs_2_
  11.4 0.1 collective-permute-start.3
  11.5 1.0 %collective-permute-done.refs_2_ = s32[1,1]{1,0:T(1,128)} collective-permute-done((s32[1,1]{1,0:T(1,128)}, s32[1,1]{1,0:T(1,128)}, u32[]{:S(2)}, u32[]{:S(2)}) %collective-permute-start) | collective-permute-done | bytes 36 | tf_op jit(solution)/shard_map/ppermute | solution.py:220
  12.5 1.3 %own.1.refs_5_.refs_1_ = bf16[32,1024]{1,0:T(8,128)(2,1)S(1)} custom-call(bf16[32,1024]{1,0:T(8,128)(2,1)S(1)} %pad_maximum_fusion.refs_0_, bf16[32,4096]{1,0:T(8,128)(2,1)S(1)} %collective-permute-done.1.refs_1_.refs_5_.refs_2_, s32[1,1]{1,0:T(1,128)} %collective-permute-done.refs_2_), custom_call_target="tpu_custom_call" | custom-call | flops 8589934592 | tf_op jit(solution)/shard_map/own/pallas_call | solution.py:36
  13.7 0.0 copy-done
  13.7 0.0 copy-done.1
  13.8 0.0 copy-done.2
  13.8 0.8 %slots.1 = (s32[2,128]{1,0:T(2,128)S(1)}, bf16[32,4096]{1,0:T(8,128)(2,1)S(1)}, bf16[128,1024]{1,0:T(8,128)(2,1)S(1)}) custom-call(s32[1,8]{1,0:T(1,128)S(1)} %bitcast.5, s32[1,1]{1,0:T(1,128)S(6)} %copy.11.refs_1_, s32[1,1]{1,0:T(1,128)} %collective-permute-done.refs_2_, bf16[32,4096]{1,0:T(8,128)(2,1)S(1)} %copy-done, bf16[128,1024]{1,0:T(8,128)(2,1)S(1)} %copy-done.1, ...), custom_call_target="tpu_custom_call" | custom-call | flops 1073741824 | bytes 8388608 | tf_op jit(solution)/shard_map/slots/pallas_call | solution.py:36
  14.6 0.0 collective-permute-start.2
  14.6 0.0 collective-permute-done.6.refs_4_
  14.6 0.0 collective-permute-done.5.refs_3_
  14.6 0.0 collective-permute-done.4.refs_2_
  14.6 0.1 pick.1
  14.7 2.0 %collective-permute-start.7 = (bf16[32,1024]{1,0:T(8,128)(2,1)S(1)}, bf16[32,1024]{1,0:T(8,128)(2,1)S(1)}, u32[]{:S(2)}, u32[]{:S(2)}) collective-permute-start(bf16[32,1024]{1,0:T(8,128)(2,1)S(1)} %get-tuple-element.32), channel_id=1, source_target_pairs={{0,16},{4,20},{8,24},{12,28},{16,0},{20,4},{24,8},{28,12},{1,17},{... | collective-permute-start | bytes 196616 | tf_op jit(solution)/shard_map/ppermute | solution.py:220
  16.7 0.0 slice-done
  16.7 0.0 slice-done.1
  16.7 2.8 %base.1 = (f32[2,32,4096]{2,1,0:T(8,128)S(1)}, f32[2,32,4096]{2,1,0:T(8,128)S(1)}) custom-call(bf16[128,1024]{1,0:T(8,128)(2,1)S(1)} %get-tuple-element.33.refs_7_.refs_0_.refs_5_, bf16[4096,1024]{1,0:T(8,128)(2,1)S(1)} %bitcast.4, bf16[32,1024]{1,0:T(8,128)(2,1)S(1)} %get-tuple-element.31.refs_1_.refs_2_), custom_call_target="tpu_custom_call" | custom-call | flops 1073741824 | bytes 8388608 | tf_op jit(solution)/shard_map/base/pallas_call | solution.py:36
  19.6 2.0 %collective-permute-done.7.refs_2_ = bf16[32,1024]{1,0:T(8,128)(2,1)S(1)} collective-permute-done((bf16[32,1024]{1,0:T(8,128)(2,1)S(1)}, bf16[32,1024]{1,0:T(8,128)(2,1)S(1)}, u32[]{:S(2)}, u32[]{:S(2)}) %collective-permute-start.7) | collective-permute-done | bytes 65568 | tf_op jit(solution)/shard_map/ppermute | solution.py:220
  21.5 0.0 collective-permute-done.3.refs_6_.refs_3_
  21.6 0.0 collective-permute-done.2.refs_4_.refs_1_
  21.6 0.3 low.1
  21.8 0.0 collective-permute-start.13
  21.8 0.1 collective-permute-start.10
  21.9 2.1 %collective-permute-start.9 = (f32[32,128]{1,0:T(8,128)S(1)}, f32[32,128]{1,0:T(8,128)S(1)}, u32[]{:S(2)}, u32[]{:S(2)}) collective-permute-start(f32[32,128]{1,0:T(8,128)S(1)} %get-tuple-element.36.refs_5_.refs_0_), channel_id=1, source_target_pairs={{0,2},{1,3},{2,0},{3,1},{4,6},{5,7},{6,4},{7,5},{8,10},{9,11},{10,... | collective-permute-start | bytes 49160 | tf_op jit(solution)/shard_map/ppermute | solution.py:214
  24.0 0.0 collective-permute-start.8
  24.0 0.5 %collective-permute-start.11 = (bf16[16,1024]{1,0:T(8,128)(2,1)S(1)}, bf16[16,1024]{1,0:T(8,128)(2,1)S(1)}, u32[]{:S(2)}, u32[]{:S(2)}) collective-permute-start(bf16[16,1024]{1,0:T(8,128)(2,1)S(1)} %get-tuple-element.38), channel_id=1, source_target_pairs={{0,1},{1,0},{2,3},{3,2},{4,5},{5,4},{6,7},{7,6},{8,9},{9,8},{10,11... | collective-permute-start | bytes 98312 | tf_op jit(solution)/shard_map/ppermute | solution.py:214
  24.5 1.3 %mixed.1.refs_6_.refs_0_ = f32[128,1024]{1,0:T(8,128)S(1)} custom-call(bf16[32,4096]{1,0:T(8,128)(2,1)S(1)} %get-tuple-element.29.refs_3_.refs_0_, bf16[32,4096]{1,0:T(8,128)(2,1)S(1)} %collective-permute-done.2.refs_4_.refs_1_, bf16[32,4096]{1,0:T(8,128)(2,1)S(1)} %collective-permute-done.1.refs_1_.refs_5_.refs_2_, ...), custom_call_target="tpu_custom_call" | custom-call | flops 1073741824 | bytes 8388608 | tf_op jit(solution)/shard_map/mixed/pallas_call | solution.py:36
  25.8 0.0 collective-permute-done.10.refs_3_
  25.9 0.0 collective-permute-done.9.refs_2_
  25.9 0.0 collective-permute-done.8.refs_1_
  25.9 0.0 collective-permute-done.11.refs_7_.refs_4_
  25.9 0.2 gradient.1
  26.1 1.0 %collective-permute-start.12 = (bf16[32,1024]{1,0:T(8,128)(2,1)S(1)}, bf16[32,1024]{1,0:T(8,128)(2,1)S(1)}, u32[]{:S(2)}, u32[]{:S(2)}) collective-permute-start(bf16[32,1024]{1,0:T(8,128)(2,1)S(1)} %get-tuple-element.41.refs_1_), channel_id=1, source_target_pairs={{0,16},{4,20},{8,24},{12,28},{16,0},{20,4},{24,8},{28,12},{1,17},{... | collective-permute-start | bytes 196616 | tf_op jit(solution)/shard_map/ppermute | solution.py:220
  27.1 0.0 collective-permute-done.13.refs_1_
  27.1 0.5 %add.1 = (f32[32,4096]{1,0:T(8,128)S(1)}, bf16[32,4096]{1,0:T(8,128)(2,1)S(1)}) custom-call(f32[2,32,4096]{2,1,0:T(8,128)S(1)} %get-tuple-element.42.refs_0_, f32[2,32,4096]{2,1,0:T(8,128)S(1)} %collective-permute-done.13.refs_1_, bf16[32,128]{1,0:T(8,128)(2,1)S(1)} %get-tuple-element.39.refs_2_.refs_1_, ...), custom_call_target="tpu_custom_call" | custom-call | tf_op jit(solution)/shard_map/add/pallas_call | solution.py:36
  27.6 1.6 %collective-permute-start.14 = (bf16[32,4096]{1,0:T(8,128)(2,1)S(1)}, bf16[32,4096]{1,0:T(8,128)(2,1)S(1)}, u32[]{:S(2)}, u32[]{:S(2)}) collective-permute-start(bf16[32,4096]{1,0:T(8,128)(2,1)S(1)} %get-tuple-element.44.refs_3_), channel_id=1, source_target_pairs={{0,2},{1,3},{2,0},{3,1},{4,6},{5,7},{6,4},{7,5},{8,10},{9,11},{10,... | collective-permute-start | bytes 786440 | tf_op jit(solution)/shard_map/ppermute | solution.py:214
  29.2 3.2 %collective-permute-done.12.refs_2_ = bf16[32,1024]{1,0:T(8,128)(2,1)S(1)} collective-permute-done((bf16[32,1024]{1,0:T(8,128)(2,1)S(1)}, bf16[32,1024]{1,0:T(8,128)(2,1)S(1)}, u32[]{:S(2)}, u32[]{:S(2)}) %collective-permute-start.12) | collective-permute-done | bytes 65568 | tf_op jit(solution)/shard_map/ppermute | solution.py:220
  32.4 0.1 route.1
  32.5 1.5 %collective-permute-start.15 = (bf16[32,1024]{1,0:T(8,128)(2,1)S(1)}, bf16[32,1024]{1,0:T(8,128)(2,1)S(1)}, u32[]{:S(2)}, u32[]{:S(2)}) collective-permute-start(bf16[32,1024]{1,0:T(8,128)(2,1)S(1)} %get-tuple-element.48), channel_id=1, source_target_pairs={{0,4},{4,0},{8,12},{12,8},{16,20},{20,16},{24,28},{28,24},{1,5},{5... | collective-permute-start | bytes 196616 | tf_op jit(solution)/shard_map/ppermute | solution.py:217
  34.1 0.0 collective-permute-start.16
  34.1 2.0 %collective-permute-start.17 = (bf16[32,1024]{1,0:T(8,128)(2,1)S(1)}, bf16[32,1024]{1,0:T(8,128)(2,1)S(1)}, u32[]{:S(2)}, u32[]{:S(2)}) collective-permute-start(bf16[32,1024]{1,0:T(8,128)(2,1)S(1)} %get-tuple-element.50), channel_id=1, source_target_pairs={{0,12},{4,8},{8,4},{12,0},{16,28},{20,24},{24,20},{28,16},{1,13},{... | collective-permute-start | bytes 196616 | tf_op jit(solution)/shard_map/ppermute | solution.py:217
  36.1 1.0 %finish.1 = bf16[128,1024]{1,0:T(8,128)(2,1)} custom-call(f32[128,1024]{1,0:T(8,128)S(1)} %mixed.1.refs_6_.refs_0_, bf16[32,128]{1,0:T(8,128)(2,1)S(1)} %get-tuple-element.39.refs_2_.refs_1_, bf16[32,1024]{1,0:T(8,128)(2,1)S(1)} %get-tuple-element.40.refs_3_.refs_2_, bf16[32,1024]{1,0:T(8,128)(2,1)S(1)} %get-tuple-element.45.refs_3_.refs_0_), custom_call_target="tpu_custom_call" | custom-call | flops 4294967296 | tf_op jit(solution)/shard_map/finish/pallas_call | solution.py:36
  37.0 0.0 collective-permute-done.14.refs_1_
  37.0 0.7 %close.1 = (bf16[32,4096]{1,0:T(8,128)(2,1)}, f32[8,128]{1,0:T(8,128)S(1)}) custom-call(f32[32,4096]{1,0:T(8,128)S(1)} %get-tuple-element.46.refs_0_, bf16[32,4096]{1,0:T(8,128)(2,1)S(1)} %collective-permute-done.14.refs_1_), custom_call_target="tpu_custom_call" | custom-call | tf_op jit(solution)/shard_map/close/pallas_call | solution.py:36
  37.8 0.0 collective-permute-done.15.refs_1_
  37.8 0.5 %collective-permute-done.16.refs_2_ = bf16[32,1024]{1,0:T(8,128)(2,1)S(1)} collective-permute-done((bf16[32,1024]{1,0:T(8,128)(2,1)S(1)}, bf16[32,1024]{1,0:T(8,128)(2,1)S(1)}, u32[]{:S(2)}, u32[]{:S(2)}) %collective-permute-start.16) | collective-permute-done | bytes 65568 | tf_op jit(solution)/shard_map/ppermute | solution.py:217
  38.3 0.9 %collective-permute-done.17.refs_3_ = bf16[32,1024]{1,0:T(8,128)(2,1)S(1)} collective-permute-done((bf16[32,1024]{1,0:T(8,128)(2,1)S(1)}, bf16[32,1024]{1,0:T(8,128)(2,1)S(1)}, u32[]{:S(2)}, u32[]{:S(2)}) %collective-permute-start.17) | collective-permute-done | bytes 65568 | tf_op jit(solution)/shard_map/ppermute | solution.py:217
  39.2 0.7 %sum.1 = (f32[1,16,1024]{2,1,0:T(8,128)}, f32[1,16,1024]{2,1,0:T(8,128)}) custom-call(bf16[32,1024]{1,0:T(8,128)(2,1)S(1)} %get-tuple-element.45.refs_3_.refs_0_, bf16[32,1024]{1,0:T(8,128)(2,1)S(1)} %collective-permute-done.15.refs_1_, bf16[32,1024]{1,0:T(8,128)(2,1)S(1)} %collective-permute-done.16.refs_2_, ...), custom_call_target="tpu_custom_call" | custom-call | tf_op jit(solution)/shard_map/sum/pallas_call | solution.py:36
  (1 shorter events, 0.0 us)
Async XLA Ops:
  0.6 10.7 %collective-permute-start.1 = (bf16[32,4096]{1,0:T(8,128)(2,1)}, bf16[32,4096]{1,0:T(8,128)(2,1)S(1)}, u32[]{:S(2)}, u32[]{:S(2)}) collective-permute-start(bf16[32,4096]{1,0:T(8,128)(2,1)} %refs_3_.1), channel_id=1, source_target_pairs={{0,2},{1,3},{2,0},{3,1},{4,6},{5,7},{6,4},{7,5},{8,10},{9,11},{10,... | collective-permute-start | bytes 786440 | tf_op jit(solution)/shard_map/ppermute | solution.py:214
  4.4 10.1 %collective-permute-start.6 = (bf16[32,1024]{1,0:T(8,128)(2,1)S(1)}, bf16[32,1024]{1,0:T(8,128)(2,1)S(1)}, u32[]{:S(2)}, u32[]{:S(2)}) collective-permute-start(bf16[32,1024]{1,0:T(8,128)(2,1)S(1)} %pad_maximum_fusion.refs_0_), channel_id=1, source_target_pairs={{0,12},{4,8},{8,4},{12,0},{16,28},{20,24},{24,20},{28,16},{1,13},{... | collective-permute-start | bytes 196616 | tf_op jit(solution)/shard_map/ppermute | solution.py:217
  6.9 7.6 %collective-permute-start.5 = (bf16[32,1024]{1,0:T(8,128)(2,1)S(1)}, bf16[32,1024]{1,0:T(8,128)(2,1)S(1)}, u32[]{:S(2)}, u32[]{:S(2)}) collective-permute-start(bf16[32,1024]{1,0:T(8,128)(2,1)S(1)} %pad_maximum_fusion.refs_0_), channel_id=1, source_target_pairs={{0,8},{4,12},{8,0},{12,4},{16,24},{20,28},{24,16},{28,20},{1,9},{5... | collective-permute-start | bytes 196616 | tf_op jit(solution)/shard_map/ppermute | solution.py:217
  7.4 7.2 %collective-permute-start.4 = (bf16[32,1024]{1,0:T(8,128)(2,1)S(1)}, bf16[32,1024]{1,0:T(8,128)(2,1)S(1)}, u32[]{:S(2)}, u32[]{:S(2)}) collective-permute-start(bf16[32,1024]{1,0:T(8,128)(2,1)S(1)} %pad_maximum_fusion.refs_0_), channel_id=1, source_target_pairs={{0,4},{4,0},{8,12},{12,8},{16,20},{20,16},{24,28},{28,24},{1,5},{5... | collective-permute-start | bytes 196616 | tf_op jit(solution)/shard_map/ppermute | solution.py:217
  7.9 4.5 %collective-permute-start = (s32[1,1]{1,0:T(1,128)}, s32[1,1]{1,0:T(1,128)}, u32[]{:S(2)}, u32[]{:S(2)}) collective-permute-start(s32[1,1]{1,0:T(1,128)} %param.12), channel_id=1, source_target_pairs={{0,16},{4,20},{8,24},{12,28},{16,0},{20,4},{24,8},{28,12},{1,17},{... | collective-permute-start | bytes 20 | tf_op jit(solution)/shard_map/ppermute | solution.py:220
  10.5 6.2 %slice-start = ((s8[8388608]{0:T(1024)(128)(4,1)}), s8[4194304]{0:T(1024)(128)(4,1)S(1)}, s32[]{:S(2)}) async-start(s8[8388608]{0:T(1024)(128)(4,1)} %bitcast.3), calls=%async_computation | async-start | bytes 8388608
  11.3 2.4 %copy-start = (bf16[32,4096]{1,0:T(8,128)(2,1)S(1)}, bf16[32,4096]{1,0:T(8,128)(2,1)}, u32[]{:S(2)}) copy-start(bf16[32,4096]{1,0:T(8,128)(2,1)} %refs_3_.1) | copy-start | bytes 786436
  11.3 2.4 %copy-start.1 = (bf16[128,1024]{1,0:T(8,128)(2,1)S(1)}, bf16[128,1024]{1,0:T(8,128)(2,1)}, u32[]{:S(2)}) copy-start(bf16[128,1024]{1,0:T(8,128)(2,1)} %refs_4_.2) | copy-start | bytes 786436
  11.4 2.4 %copy-start.2 = (s32[8]{0:T(128)S(1)}, s32[8]{0:T(128)}, u32[]{:S(2)}) copy-start(s32[8]{0:T(128)} %param.13) | copy-start | bytes 100
  11.4 5.4 %slice-start.1 = ((s8[8388608]{0:T(1024)(128)(4,1)}), s8[4194304]{0:T(1024)(128)(4,1)S(1)}, s32[]{:S(2)}) async-start(s8[8388608]{0:T(1024)(128)(4,1)} %bitcast.3), calls=%async_computation.1 | async-start | bytes 8388608
  11.4 10.2 %collective-permute-start.3 = (bf16[32,4096]{1,0:T(8,128)(2,1)S(1)}, bf16[32,4096]{1,0:T(8,128)(2,1)S(1)}, u32[]{:S(2)}, u32[]{:S(2)}) collective-permute-start(bf16[32,4096]{1,0:T(8,128)(2,1)S(1)} %collective-permute-done.1.refs_1_.refs_5_.refs_2_), channel_id=1, source_target_pairs={{0,1},{1,0},{2,3},{3,2},{4,5},{5,4},{6,7},{7,6},{8,9},{9,8},{10,11... | collective-permute-start | bytes 786440 | tf_op jit(solution)/shard_map/ppermute | solution.py:214
  14.6 7.0 %collective-permute-start.2 = (bf16[32,4096]{1,0:T(8,128)(2,1)S(1)}, bf16[32,4096]{1,0:T(8,128)(2,1)S(1)}, u32[]{:S(2)}, u32[]{:S(2)}) collective-permute-start(bf16[32,4096]{1,0:T(8,128)(2,1)S(1)} %get-tuple-element.29.refs_3_.refs_0_), channel_id=1, source_target_pairs={{0,1},{1,0},{2,3},{3,2},{4,5},{5,4},{6,7},{7,6},{8,9},{9,8},{10,11... | collective-permute-start | bytes 786440 | tf_op jit(solution)/shard_map/ppermute | solution.py:214
  14.7 6.8 %collective-permute-start.7 = (bf16[32,1024]{1,0:T(8,128)(2,1)S(1)}, bf16[32,1024]{1,0:T(8,128)(2,1)S(1)}, u32[]{:S(2)}, u32[]{:S(2)}) collective-permute-start(bf16[32,1024]{1,0:T(8,128)(2,1)S(1)} %get-tuple-element.32), channel_id=1, source_target_pairs={{0,16},{4,20},{8,24},{12,28},{16,0},{20,4},{24,8},{28,12},{1,17},{... | collective-permute-start | bytes 196616 | tf_op jit(solution)/shard_map/ppermute | solution.py:220
  21.8 5.3 %collective-permute-start.13 = (f32[2,32,4096]{2,1,0:T(8,128)S(1)}, f32[2,32,4096]{2,1,0:T(8,128)S(1)}, u32[]{:S(2)}, u32[]{:S(2)}) collective-permute-start(f32[2,32,4096]{2,1,0:T(8,128)S(1)} %get-tuple-element.43), channel_id=1, source_target_pairs={{0,1},{1,0},{2,3},{3,2},{4,5},{5,4},{6,7},{7,6},{8,9},{9,8},{10,11... | collective-permute-start | bytes 3145736 | tf_op jit(solution)/shard_map/ppermute | solution.py:214
  21.8 4.0 %collective-permute-start.10 = (f32[32,128]{1,0:T(8,128)S(1)}, f32[32,128]{1,0:T(8,128)S(1)}, u32[]{:S(2)}, u32[]{:S(2)}) collective-permute-start(f32[32,128]{1,0:T(8,128)S(1)} %get-tuple-element.36.refs_5_.refs_0_), channel_id=1, source_target_pairs={{0,3},{1,2},{2,1},{3,0},{4,7},{5,6},{6,5},{7,4},{8,11},{9,10},{10,... | collective-permute-start | bytes 49160 | tf_op jit(solution)/shard_map/ppermute | solution.py:214
  21.9 4.0 %collective-permute-start.9 = (f32[32,128]{1,0:T(8,128)S(1)}, f32[32,128]{1,0:T(8,128)S(1)}, u32[]{:S(2)}, u32[]{:S(2)}) collective-permute-start(f32[32,128]{1,0:T(8,128)S(1)} %get-tuple-element.36.refs_5_.refs_0_), channel_id=1, source_target_pairs={{0,2},{1,3},{2,0},{3,1},{4,6},{5,7},{6,4},{7,5},{8,10},{9,11},{10,... | collective-permute-start | bytes 49160 | tf_op jit(solution)/shard_map/ppermute | solution.py:214
  24.0 1.9 %collective-permute-start.8 = (f32[32,128]{1,0:T(8,128)S(1)}, f32[32,128]{1,0:T(8,128)S(1)}, u32[]{:S(2)}, u32[]{:S(2)}) collective-permute-start(f32[32,128]{1,0:T(8,128)S(1)} %get-tuple-element.36.refs_5_.refs_0_), channel_id=1, source_target_pairs={{0,1},{1,0},{2,3},{3,2},{4,5},{5,4},{6,7},{7,6},{8,9},{9,8},{10,11... | collective-permute-start | bytes 49160 | tf_op jit(solution)/shard_map/ppermute | solution.py:214
  24.0 1.9 %collective-permute-start.11 = (bf16[16,1024]{1,0:T(8,128)(2,1)S(1)}, bf16[16,1024]{1,0:T(8,128)(2,1)S(1)}, u32[]{:S(2)}, u32[]{:S(2)}) collective-permute-start(bf16[16,1024]{1,0:T(8,128)(2,1)S(1)} %get-tuple-element.38), channel_id=1, source_target_pairs={{0,1},{1,0},{2,3},{3,2},{4,5},{5,4},{6,7},{7,6},{8,9},{9,8},{10,11... | collective-permute-start | bytes 98312 | tf_op jit(solution)/shard_map/ppermute | solution.py:214
  26.1 6.3 %collective-permute-start.12 = (bf16[32,1024]{1,0:T(8,128)(2,1)S(1)}, bf16[32,1024]{1,0:T(8,128)(2,1)S(1)}, u32[]{:S(2)}, u32[]{:S(2)}) collective-permute-start(bf16[32,1024]{1,0:T(8,128)(2,1)S(1)} %get-tuple-element.41.refs_1_), channel_id=1, source_target_pairs={{0,16},{4,20},{8,24},{12,28},{16,0},{20,4},{24,8},{28,12},{1,17},{... | collective-permute-start | bytes 196616 | tf_op jit(solution)/shard_map/ppermute | solution.py:220
  27.6 9.4 %collective-permute-start.14 = (bf16[32,4096]{1,0:T(8,128)(2,1)S(1)}, bf16[32,4096]{1,0:T(8,128)(2,1)S(1)}, u32[]{:S(2)}, u32[]{:S(2)}) collective-permute-start(bf16[32,4096]{1,0:T(8,128)(2,1)S(1)} %get-tuple-element.44.refs_3_), channel_id=1, source_target_pairs={{0,2},{1,3},{2,0},{3,1},{4,6},{5,7},{6,4},{7,5},{8,10},{9,11},{10,... | collective-permute-start | bytes 786440 | tf_op jit(solution)/shard_map/ppermute | solution.py:214
  32.5 5.3 %collective-permute-start.15 = (bf16[32,1024]{1,0:T(8,128)(2,1)S(1)}, bf16[32,1024]{1,0:T(8,128)(2,1)S(1)}, u32[]{:S(2)}, u32[]{:S(2)}) collective-permute-start(bf16[32,1024]{1,0:T(8,128)(2,1)S(1)} %get-tuple-element.48), channel_id=1, source_target_pairs={{0,4},{4,0},{8,12},{12,8},{16,20},{20,16},{24,28},{28,24},{1,5},{5... | collective-permute-start | bytes 196616 | tf_op jit(solution)/shard_map/ppermute | solution.py:217
  34.1 4.3 %collective-permute-start.16 = (bf16[32,1024]{1,0:T(8,128)(2,1)S(1)}, bf16[32,1024]{1,0:T(8,128)(2,1)S(1)}, u32[]{:S(2)}, u32[]{:S(2)}) collective-permute-start(bf16[32,1024]{1,0:T(8,128)(2,1)S(1)} %get-tuple-element.49), channel_id=1, source_target_pairs={{0,8},{4,12},{8,0},{12,4},{16,24},{20,28},{24,16},{28,20},{1,9},{5... | collective-permute-start | bytes 196616 | tf_op jit(solution)/shard_map/ppermute | solution.py:217
  34.1 5.2 %collective-permute-start.17 = (bf16[32,1024]{1,0:T(8,128)(2,1)S(1)}, bf16[32,1024]{1,0:T(8,128)(2,1)S(1)}, u32[]{:S(2)}, u32[]{:S(2)}) collective-permute-start(bf16[32,1024]{1,0:T(8,128)(2,1)S(1)} %get-tuple-element.50), channel_id=1, source_target_pairs={{0,12},{4,8},{8,4},{12,0},{16,28},{20,24},{24,20},{28,16},{1,13},{... | collective-permute-start | bytes 196616 | tf_op jit(solution)/shard_map/ppermute | solution.py:217

commit v2 on v1

--- a/solution.py
+++ b/solution.py
@@ -92,23 +92,23 @@
     target[...] = source[...]
 
 
-def pick_kernel(near, far, *refs):
-    slots, group, found = refs[0], refs[1 : 1 + near], refs[1 + near :]
-    i = lax.axis_index("dp") & (near - 1)
-    for k in range(far):
-        found[k][...] = choose(group, (slots[k : k + 1, :1] & (near - 1)) ^ i)
-
-
-def low_kernel(near, far, parts, *refs):
-    slots, found = refs[0], refs[1 : 1 + far]
-    tokens = refs[1 + far : 1 + far + parts]
-    upstream, both, chosen, columns, down = refs[1 + far + parts :]
-    o = lax.axis_index("dp") >> log2(near)
+def pick_kernel(outer, inner, *refs):
+    slots, column, found = refs[0], refs[1 : 1 + outer], refs[1 + outer :]
+    o = lax.axis_index("dp") >> log2(inner)
+    for k in range(inner):
+        found[k][...] = choose(column, (slots[k : k + 1, :1] >> log2(inner)) ^ o)
+
+
+def low_kernel(inner, parts, *refs):
+    slots, found = refs[0], refs[1 : 1 + inner]
+    tokens = refs[1 + inner : 1 + inner + parts]
+    upstream, both, chosen, columns, down = refs[1 + inner + parts :]
+    i = lax.axis_index("dp") & (inner - 1)
     t = lax.axis_index("tensor")
     cols = columns.shape[1]
     rows = columns.shape[0] // parts
     rank = chosen.shape[0] // 2
-    chosen[...] = choose(found, (slots[:1, :1] >> log2(near)) ^ o)
+    chosen[...] = choose(found, (slots[:1, :1] & (inner - 1)) ^ i)
     down[...] = chosen[:rank, :]
     start = pl.multiple_of(t * cols, cols)
     for k in range(parts):
@@ -136,13 +136,14 @@
     term[rank:, :] = (adapter_scale * up_term).astype(bf16)
 
 
-def route_kernel(near, far, *refs):
-    slots, terms, parts = refs[0], refs[1 : 1 + far], refs[1 + far :]
+def route_kernel(outer, inner, *refs):
+    slots, terms, parts = refs[0], refs[1 : 1 + inner], refs[1 + inner :]
     d = lax.axis_index("dp")
-    for m in range(near):
+    for m in range(outer):
+        target = d ^ (m * inner)
         part = None
-        for k in range(far):
-            here = jnp.where(slots[k : k + 1, :1] == (d ^ m), 1.0, 0.0).astype(bf16)
+        for k in range(inner):
+            here = jnp.where(slots[k : k + 1, :1] == target, 1.0, 0.0).astype(bf16)
             one = here * terms[k][...]
             part = one if part is None else part + one
         parts[m][...] = part
@@ -206,18 +207,18 @@
 
 
 def make_per_device(dp_size, tensor_size):
-    near = 1 << ((log2(dp_size) + 1) // 2)
-    far = dp_size // near
+    inner = 1 << (log2(dp_size) // 2)
+    outer = dp_size // inner
     half = tensor_size // 2
 
     def over_tensor(x, k):
         return lax.ppermute(x, "tensor", [(t, t ^ k) for t in range(tensor_size)])
 
-    def over_near(x, k):
+    def over_inner(x, k):
         return lax.ppermute(x, "dp", [(d, d ^ k) for d in range(dp_size)])
 
-    def over_far(x, k):
-        return lax.ppermute(x, "dp", [(d, d ^ (k * near)) for d in range(dp_size)])
+    def over_outer(x, k):
+        return lax.ppermute(x, "dp", [(d, d ^ (k * inner)) for d in range(dp_size)])
 
     def per_device(tokens, weight, down, up, upstream, adapter_per_block, owner):
         rank, cols = down.shape[1], down.shape[2]
@@ -227,41 +228,41 @@
         flops = 2 * length * weight.shape[0] * cols
 
         mine = jnp.concatenate([down[0], up[0]], axis=0)
-        group = [mine] + [over_near(mine, k) for k in range(1, near)]
-        across = over_tensor(tokens, half)
+        column = [mine] + [over_outer(mine, k) for k in range(1, outer)]
+        far = over_tensor(tokens, half)
         blocks = [adapter_per_block]
-        blocks += [over_far(adapter_per_block, k) for k in range(1, far)]
-
-        (group[0],) = call(
+        blocks += [over_inner(adapter_per_block, k) for k in range(1, inner)]
+
+        (column[0],) = call(
             own_kernel,
             "own",
             [shape(mine.shape, bf16)],
             (mine,),
             [vmem()],
             flops=8 * flops,
-            after=(across, *blocks[1:]),
+            after=(far,),
         )
         slots, tokens_here, upstream_here = call(
             slot_kernel,
             "slots",
             [
-                shape((far, 128), jnp.int32),
+                shape((inner, 128), jnp.int32),
                 shape(tokens.shape, bf16),
                 shape(upstream.shape, bf16),
             ],
             (owner.reshape(1, -1), *blocks, tokens, upstream),
-            [vmem()] * (far + 3),
+            [vmem()] * (inner + 3),
             flops=flops,
             moved=small_bytes,
-            after=(group[0],),
-        )
-        pieces = [tokens_here, over_tensor(tokens_here, 1), across, over_tensor(across, 1)]
+            after=(column[0],),
+        )
+        pieces = [tokens_here, over_tensor(tokens_here, 1), far, over_tensor(far, 1)]
         found = call(
-            functools.partial(pick_kernel, near, far),
+            functools.partial(pick_kernel, outer, inner),
             "pick",
-            [shape((2 * rank, cols), bf16)] * far,
-            (slots, *group),
-            [vmem()] * (1 + near),
+            [shape((2 * rank, cols), bf16)] * inner,
+            (slots, *column),
+            [vmem()] * (1 + outer),
             flops=flops,
             moved=small_bytes,
         )
@@ -276,10 +277,10 @@
             weight_bytes,
             after=(found[0],),
         )
-        found = [found[0]] + [over_far(found[k], k) for k in range(1, far)]
+        found = [found[0]] + [over_inner(found[k], k) for k in range(1, inner)]
 
         both, chosen, columns, chosen_down = call(
-            functools.partial(low_kernel, near, far, tensor_size),
+            functools.partial(low_kernel, inner, tensor_size),
             "low",
             [
                 shape((2 * rank, length), f32),
@@ -288,7 +289,7 @@
                 shape((rank, cols), bf16),
             ],
             (slots, *found, *pieces, upstream_here),
-            [vmem()] * (1 + far + tensor_size + 1),
+            [vmem()] * (1 + inner + tensor_size + 1),
             flops=flops,
             moved=small_bytes,
         )
@@ -316,7 +317,7 @@
             [vmem()] * (tensor_size + 2),
             after=(mixed, sibling),
         )
-        terms = [term] + [over_far(term, k) for k in range(1, far)]
+        terms = [term] + [over_inner(term, k) for k in range(1, inner)]
 
         hold, give = call(
             add_kernel,
@@ -329,14 +330,14 @@
         got = over_tensor(give, half)
 
         routed = call(
-            functools.partial(route_kernel, near, far),
+            functools.partial(route_kernel, outer, inner),
             "route",
-            [shape((2 * rank, cols), bf16)] * near,
+            [shape((2 * rank, cols), bf16)] * outer,
             (slots, *terms),
-            [vmem()] * (1 + far),
+            [vmem()] * (1 + inner),
             after=(give,),
         )
-        parts = [routed[0]] + [over_near(routed[m], m) for m in range(1, near)]
+        parts = [routed[0]] + [over_outer(routed[m], m) for m in range(1, outer)]
         (mixed,) = call(
             finish_kernel,
             "finish",
@@ -357,8 +358,8 @@
             sum_kernel,
             "sum",
             [shape(down.shape, f32)] * 2,
-            parts,
-            [vmem()] * near,
+            parts[:1] + parts[:0:-1],
+            [vmem()] * outer,
             after=(done,),
         )
         return mixed, input_gradient, down_gradient, up_gradient

time: 40.1 us -> 37.4 us (0.933)
  waiting for transfers between devices: 7.72 us -> 5.92 us
  Pallas kernels: 9.7 us -> 8.93 us
    ppermute x9, waiting for transfers between devices: 7.65 us -> 5.52 us  [the longest x3 2.84 us: over_inner(): return lax.ppermute(x, 'dp', [(d, d ^ k) for d in range(dp_size)])]
    pallas_call x12, Pallas kernels: 9.7 us -> 8.93 us  [call(): pl.pallas_call(run, name=name, out_shape=outs, in_specs=specs + [pl.Block...]
  transfers between devices with their start and end apart: 18 -> 18, of which waited for: 5 -> 6; matrix products, arithmetic and copies ran while one was open for 2% -> 2% of each run, Pallas kernels for 22% -> 21%
where the time goes in v2:
time: 37.4 us; the launch traced here: 37.2 us
  starting transfers between devices  20 us (53%)
  Pallas kernels  8.93 us (24%)
  waiting for transfers between devices  5.92 us (16%)
  between operations  1.59 us (4%)
  other arithmetic  0.78 us (2%)
    pallas_call x12, Pallas kernels, call(): pl.pallas_call(run, name=name, out_shape=outs, in_specs=specs + [pl.Block...  8.93 us
    ppermute x6, starting transfers between devices, over_outer(): return lax.ppermute(x, 'dp', [(d, d ^ k * inner) for d in range(dp_size)])  8.84 us
    ppermute x9, starting transfers between devices, over_tensor(): return lax.ppermute(x, 'tensor', [(t, t ^ k) for t in range(tensor_size)])  7.37 us
    ppermute x3, starting transfers between devices, over_inner(): return lax.ppermute(x, 'dp', [(d, d ^ k) for d in range(dp_size)])  3.76 us
    ppermute x3, waiting for transfers between devices, over_inner(): return lax.ppermute(x, 'dp', [(d, d ^ k) for d in range(dp_size)])  2.84 us
    ppermute x6, waiting for transfers between devices, over_outer(): return lax.ppermute(x, 'dp', [(d, d ^ k * inner) for d in range(dp_size)])  2.68 us
    concatenate x1, other arithmetic, per_device(): mine = jnp.concatenate([down[0], up[0]], axis=0)  0.78 us
  transfers between devices with their start and end apart: 18, of which 6 were waited for; matrix products, arithmetic and copies ran while one was open for 2% of the time, Pallas kernels for 21%

profile of v2, /device:TPU:0, one launch (start us, length us, event | category | flops | bytes accessed | tf_op | source)
XLA Modules:
  0.0 37.2 jit_solution(17186948691130703496)
XLA Ops:
  0.6 3.0 %collective-permute-start.1 = (bf16[32,4096]{1,0:T(8,128)(2,1)}, bf16[32,4096]{1,0:T(8,128)(2,1)S(1)}, u32[]{:S(2)}, u32[]{:S(2)}) collective-permute-start(bf16[32,4096]{1,0:T(8,128)(2,1)} %refs_3_.1), channel_id=1, source_target_pairs={{0,2},{1,3},{2,0},{3,1},{4,6},{5,7},{6,4},{7,5},{8,10},{9,11},{10,... | collective-permute-start | bytes 786440 | tf_op jit(solution)/shard_map/ppermute | solution.py:215
  3.7 0.8 %pad_maximum_fusion.refs_0_ = bf16[32,1024]{1,0:T(8,128)(2,1)S(1)} fusion(bf16[16,1024]{1,0:T(8,128)(2,1)} %bitcast.6, bf16[16,1024]{1,0:T(8,128)(2,1)} %bitcast.7), kind=kLoop, calls=%fused_computation | loop fusion | flops 131072 | bytes 131072 | tf_op jit(solution)/shard_map/concatenate | solution.py:230
  4.4 3.6 %collective-permute-start.6 = (bf16[32,1024]{1,0:T(8,128)(2,1)S(1)}, bf16[32,1024]{1,0:T(8,128)(2,1)S(1)}, u32[]{:S(2)}, u32[]{:S(2)}) collective-permute-start(bf16[32,1024]{1,0:T(8,128)(2,1)S(1)} %pad_maximum_fusion.refs_0_), channel_id=1, source_target_pairs={{0,24},{4,28},{8,16},{12,20},{16,8},{20,12},{24,0},{28,4},{1,25},{... | collective-permute-start | bytes 196616 | tf_op jit(solution)/shard_map/ppermute | solution.py:221
  8.0 0.0 collective-permute-start.5
  8.0 0.8 %collective-permute-start.4 = (bf16[32,1024]{1,0:T(8,128)(2,1)S(1)}, bf16[32,1024]{1,0:T(8,128)(2,1)S(1)}, u32[]{:S(2)}, u32[]{:S(2)}) collective-permute-start(bf16[32,1024]{1,0:T(8,128)(2,1)S(1)} %pad_maximum_fusion.refs_0_), channel_id=1, source_target_pairs={{0,8},{4,12},{8,0},{12,4},{16,24},{20,28},{24,16},{28,20},{1,9},{5... | collective-permute-start | bytes 196616 | tf_op jit(solution)/shard_map/ppermute | solution.py:221
  8.8 1.5 %collective-permute-start = (s32[1,1]{1,0:T(1,128)}, s32[1,1]{1,0:T(1,128)}, u32[]{:S(2)}, u32[]{:S(2)}) collective-permute-start(s32[1,1]{1,0:T(1,128)} %param.12), channel_id=1, source_target_pairs={{0,4},{4,0},{8,12},{12,8},{16,20},{20,16},{24,28},{28,24},{1,5},{5... | collective-permute-start | bytes 20 | tf_op jit(solution)/shard_map/ppermute | solution.py:218
  10.3 0.0 slice-start
  11.1 0.0 copy-start
  11.1 0.0 copy-start.1
  11.2 0.0 copy-start.2
  11.2 0.0 slice-start.1
  11.2 0.0 collective-permute-done.1.refs_1_.refs_5_.refs_2_
  11.2 0.1 collective-permute-start.3
  11.3 1.2 %collective-permute-done.refs_2_ = s32[1,1]{1,0:T(1,128)} collective-permute-done((s32[1,1]{1,0:T(1,128)}, s32[1,1]{1,0:T(1,128)}, u32[]{:S(2)}, u32[]{:S(2)}) %collective-permute-start) | collective-permute-done | bytes 36 | tf_op jit(solution)/shard_map/ppermute | solution.py:218
  12.5 0.0 copy-done
  12.5 0.0 copy-done.1
  12.5 0.0 copy-done.2
  12.5 1.3 %slots.1 = (s32[2,128]{1,0:T(2,128)S(1)}, bf16[32,4096]{1,0:T(8,128)(2,1)S(1)}, bf16[128,1024]{1,0:T(8,128)(2,1)S(1)}) custom-call(s32[1,8]{1,0:T(1,128)S(1)} %bitcast.5, s32[1,1]{1,0:T(1,128)S(6)} %copy.11.refs_1_, s32[1,1]{1,0:T(1,128)} %collective-permute-done.refs_2_, bf16[32,4096]{1,0:T(8,128)(2,1)S(1)} %copy-done, bf16[128,1024]{1,0:T(8,128)(2,1)S(1)} %copy-done.1, ...), custom_call_target="tpu_custom_call" | custom-call | flops 1073741824 | bytes 8388608 | tf_op jit(solution)/shard_map/slots/pallas_call | solution.py:36
  13.8 0.0 collective-permute-start.2
  13.8 0.0 collective-permute-done.6.refs_4_
  13.8 0.0 collective-permute-done.5.refs_3_
  13.8 0.0 collective-permute-done.4.refs_2_
  13.8 0.1 pick.1
  13.9 1.2 %collective-permute-start.7 = (bf16[32,1024]{1,0:T(8,128)(2,1)S(1)}, bf16[32,1024]{1,0:T(8,128)(2,1)S(1)}, u32[]{:S(2)}, u32[]{:S(2)}) collective-permute-start(bf16[32,1024]{1,0:T(8,128)(2,1)S(1)} %get-tuple-element.32), channel_id=1, source_target_pairs={{0,4},{4,0},{8,12},{12,8},{16,20},{20,16},{24,28},{28,24},{1,5},{5... | collective-permute-start | bytes 196616 | tf_op jit(solution)/shard_map/ppermute | solution.py:218
  15.1 0.0 slice-done
  15.1 0.0 slice-done.1
  15.1 2.8 %base.1 = (f32[2,32,4096]{2,1,0:T(8,128)S(1)}, f32[2,32,4096]{2,1,0:T(8,128)S(1)}) custom-call(bf16[128,1024]{1,0:T(8,128)(2,1)S(1)} %get-tuple-element.33.refs_7_.refs_0_.refs_5_, bf16[4096,1024]{1,0:T(8,128)(2,1)S(1)} %bitcast.4, bf16[32,1024]{1,0:T(8,128)(2,1)S(1)} %get-tuple-element.31.refs_1_.refs_2_), custom_call_target="tpu_custom_call" | custom-call | flops 1073741824 | bytes 8388608 | tf_op jit(solution)/shard_map/base/pallas_call | solution.py:36
  18.0 0.5 %collective-permute-done.7.refs_2_ = bf16[32,1024]{1,0:T(8,128)(2,1)S(1)} collective-permute-done((bf16[32,1024]{1,0:T(8,128)(2,1)S(1)}, bf16[32,1024]{1,0:T(8,128)(2,1)S(1)}, u32[]{:S(2)}, u32[]{:S(2)}) %collective-permute-start.7) | collective-permute-done | bytes 65568 | tf_op jit(solution)/shard_map/ppermute | solution.py:218
  18.4 0.0 collective-permute-done.3.refs_6_.refs_3_
  18.4 0.0 collective-permute-done.2.refs_4_.refs_1_
  18.4 0.3 low.1
  18.7 0.0 collective-permute-start.13
  18.7 0.6 %collective-permute-start.10 = (f32[32,128]{1,0:T(8,128)S(1)}, f32[32,128]{1,0:T(8,128)S(1)}, u32[]{:S(2)}, u32[]{:S(2)}) collective-permute-start(f32[32,128]{1,0:T(8,128)S(1)} %get-tuple-element.36.refs_5_.refs_0_), channel_id=1, source_target_pairs={{0,3},{1,2},{2,1},{3,0},{4,7},{5,6},{6,5},{7,4},{8,11},{9,10},{10,... | collective-permute-start | bytes 49160 | tf_op jit(solution)/shard_map/ppermute | solution.py:215
  19.4 1.5 %collective-permute-start.9 = (f32[32,128]{1,0:T(8,128)S(1)}, f32[32,128]{1,0:T(8,128)S(1)}, u32[]{:S(2)}, u32[]{:S(2)}) collective-permute-start(f32[32,128]{1,0:T(8,128)S(1)} %get-tuple-element.36.refs_5_.refs_0_), channel_id=1, source_target_pairs={{0,2},{1,3},{2,0},{3,1},{4,6},{5,7},{6,4},{7,5},{8,10},{9,11},{10,... | collective-permute-start | bytes 49160 | tf_op jit(solution)/shard_map/ppermute | solution.py:215
  20.9 0.0 collective-permute-start.8
  20.9 0.5 %collective-permute-start.11 = (bf16[16,1024]{1,0:T(8,128)(2,1)S(1)}, bf16[16,1024]{1,0:T(8,128)(2,1)S(1)}, u32[]{:S(2)}, u32[]{:S(2)}) collective-permute-start(bf16[16,1024]{1,0:T(8,128)(2,1)S(1)} %get-tuple-element.38), channel_id=1, source_target_pairs={{0,1},{1,0},{2,3},{3,2},{4,5},{5,4},{6,7},{7,6},{8,9},{9,8},{10,11... | collective-permute-start | bytes 98312 | tf_op jit(solution)/shard_map/ppermute | solution.py:215
  21.4 1.3 %mixed.1.refs_6_.refs_0_ = f32[128,1024]{1,0:T(8,128)S(1)} custom-call(bf16[32,4096]{1,0:T(8,128)(2,1)S(1)} %get-tuple-element.29.refs_3_.refs_0_, bf16[32,4096]{1,0:T(8,128)(2,1)S(1)} %collective-permute-done.2.refs_4_.refs_1_, bf16[32,4096]{1,0:T(8,128)(2,1)S(1)} %collective-permute-done.1.refs_1_.refs_5_.refs_2_, ...), custom_call_target="tpu_custom_call" | custom-call | flops 1073741824 | bytes 8388608 | tf_op jit(solution)/shard_map/mixed/pallas_call | solution.py:36
  22.7 0.0 collective-permute-done.10.refs_3_
  22.7 0.4 %collective-permute-done.9.refs_2_ = f32[32,128]{1,0:T(8,128)S(1)} collective-permute-done((f32[32,128]{1,0:T(8,128)S(1)}, f32[32,128]{1,0:T(8,128)S(1)}, u32[]{:S(2)}, u32[]{:S(2)}) %collective-permute-start.9) | collective-permute-done | bytes 16416 | tf_op jit(solution)/shard_map/ppermute | solution.py:215
  23.1 0.0 collective-permute-done.8.refs_1_
  23.1 0.0 collective-permute-done.11.refs_7_.refs_4_
  23.1 0.2 gradient.1
  23.3 1.0 %collective-permute-start.12 = (bf16[32,1024]{1,0:T(8,128)(2,1)S(1)}, bf16[32,1024]{1,0:T(8,128)(2,1)S(1)}, u32[]{:S(2)}, u32[]{:S(2)}) collective-permute-start(bf16[32,1024]{1,0:T(8,128)(2,1)S(1)} %get-tuple-element.41.refs_1_), channel_id=1, source_target_pairs={{0,4},{4,0},{8,12},{12,8},{16,20},{20,16},{24,28},{28,24},{1,5},{5... | collective-permute-start | bytes 196616 | tf_op jit(solution)/shard_map/ppermute | solution.py:218
  24.4 0.0 collective-permute-done.13.refs_1_
  24.4 0.5 %add.1 = (f32[32,4096]{1,0:T(8,128)S(1)}, bf16[32,4096]{1,0:T(8,128)(2,1)S(1)}) custom-call(f32[2,32,4096]{2,1,0:T(8,128)S(1)} %get-tuple-element.42.refs_0_, f32[2,32,4096]{2,1,0:T(8,128)S(1)} %collective-permute-done.13.refs_1_, bf16[32,128]{1,0:T(8,128)(2,1)S(1)} %get-tuple-element.39.refs_2_.refs_1_, ...), custom_call_target="tpu_custom_call" | custom-call | tf_op jit(solution)/shard_map/add/pallas_call | solution.py:36
  24.8 1.6 %collective-permute-start.14 = (bf16[32,4096]{1,0:T(8,128)(2,1)S(1)}, bf16[32,4096]{1,0:T(8,128)(2,1)S(1)}, u32[]{:S(2)}, u32[]{:S(2)}) collective-permute-start(bf16[32,4096]{1,0:T(8,128)(2,1)S(1)} %get-tuple-element.44.refs_3_), channel_id=1, source_target_pairs={{0,2},{1,3},{2,0},{3,1},{4,6},{5,7},{6,4},{7,5},{8,10},{9,11},{10,... | collective-permute-start | bytes 786440 | tf_op jit(solution)/shard_map/ppermute | solution.py:215
  26.4 1.2 %collective-permute-done.12.refs_2_ = bf16[32,1024]{1,0:T(8,128)(2,1)S(1)} collective-permute-done((bf16[32,1024]{1,0:T(8,128)(2,1)S(1)}, bf16[32,1024]{1,0:T(8,128)(2,1)S(1)}, u32[]{:S(2)}, u32[]{:S(2)}) %collective-permute-start.12) | collective-permute-done | bytes 65568 | tf_op jit(solution)/shard_map/ppermute | solution.py:218
  27.6 0.1 route.1
  27.7 3.7 %collective-permute-start.15 = (bf16[32,1024]{1,0:T(8,128)(2,1)S(1)}, bf16[32,1024]{1,0:T(8,128)(2,1)S(1)}, u32[]{:S(2)}, u32[]{:S(2)}) collective-permute-start(bf16[32,1024]{1,0:T(8,128)(2,1)S(1)} %get-tuple-element.48), channel_id=1, source_target_pairs={{0,24},{4,28},{8,16},{12,20},{16,8},{20,12},{24,0},{28,4},{1,25},{... | collective-permute-start | bytes 196616 | tf_op jit(solution)/shard_map/ppermute | solution.py:221
  31.4 0.0 collective-permute-start.16
  31.4 0.8 %collective-permute-start.17 = (bf16[32,1024]{1,0:T(8,128)(2,1)S(1)}, bf16[32,1024]{1,0:T(8,128)(2,1)S(1)}, u32[]{:S(2)}, u32[]{:S(2)}) collective-permute-start(bf16[32,1024]{1,0:T(8,128)(2,1)S(1)} %get-tuple-element.50), channel_id=1, source_target_pairs={{0,8},{4,12},{8,0},{12,4},{16,24},{20,28},{24,16},{28,20},{1,9},{5... | collective-permute-start | bytes 196616 | tf_op jit(solution)/shard_map/ppermute | solution.py:221
  32.2 1.0 %finish.1 = bf16[128,1024]{1,0:T(8,128)(2,1)} custom-call(f32[128,1024]{1,0:T(8,128)S(1)} %mixed.1.refs_6_.refs_0_, bf16[32,128]{1,0:T(8,128)(2,1)S(1)} %get-tuple-element.39.refs_2_.refs_1_, bf16[32,1024]{1,0:T(8,128)(2,1)S(1)} %get-tuple-element.40.refs_3_.refs_2_, bf16[32,1024]{1,0:T(8,128)(2,1)S(1)} %get-tuple-element.45.refs_3_.refs_0_), custom_call_target="tpu_custom_call" | custom-call | flops 4294967296 | tf_op jit(solution)/shard_map/finish/pallas_call | solution.py:36
  33.1 0.0 collective-permute-done.14.refs_1_
  33.1 0.7 %close.1 = (bf16[32,4096]{1,0:T(8,128)(2,1)}, f32[8,128]{1,0:T(8,128)S(1)}) custom-call(f32[32,4096]{1,0:T(8,128)S(1)} %get-tuple-element.46.refs_0_, bf16[32,4096]{1,0:T(8,128)(2,1)S(1)} %collective-permute-done.14.refs_1_), custom_call_target="tpu_custom_call" | custom-call | tf_op jit(solution)/shard_map/close/pallas_call | solution.py:36
  33.9 0.1 collective-permute-done.15.refs_1_
  33.9 2.6 %collective-permute-done.16.refs_2_ = bf16[32,1024]{1,0:T(8,128)(2,1)S(1)} collective-permute-done((bf16[32,1024]{1,0:T(8,128)(2,1)S(1)}, bf16[32,1024]{1,0:T(8,128)(2,1)S(1)}, u32[]{:S(2)}, u32[]{:S(2)}) %collective-permute-start.16) | collective-permute-done | bytes 65568 | tf_op jit(solution)/shard_map/ppermute | solution.py:221
  36.5 0.0 collective-permute-done.17.refs_3_
  36.5 0.7 %sum.1 = (f32[1,16,1024]{2,1,0:T(8,128)}, f32[1,16,1024]{2,1,0:T(8,128)}) custom-call(bf16[32,1024]{1,0:T(8,128)(2,1)S(1)} %get-tuple-element.45.refs_3_.refs_0_, bf16[32,1024]{1,0:T(8,128)(2,1)S(1)} %collective-permute-done.15.refs_1_, bf16[32,1024]{1,0:T(8,128)(2,1)S(1)} %collective-permute-done.16.refs_2_, ...), custom_call_target="tpu_custom_call" | custom-call | tf_op jit(solution)/shard_map/sum/pallas_call | solution.py:36
  (2 shorter events, 0.0 us)
Async XLA Ops:
  0.6 10.5 %collective-permute-start.1 = (bf16[32,4096]{1,0:T(8,128)(2,1)}, bf16[32,4096]{1,0:T(8,128)(2,1)S(1)}, u32[]{:S(2)}, u32[]{:S(2)}) collective-permute-start(bf16[32,4096]{1,0:T(8,128)(2,1)} %refs_3_.1), channel_id=1, source_target_pairs={{0,2},{1,3},{2,0},{3,1},{4,6},{5,7},{6,4},{7,5},{8,10},{9,11},{10,... | collective-permute-start | bytes 786440 | tf_op jit(solution)/shard_map/ppermute | solution.py:215
  4.4 9.3 %collective-permute-start.6 = (bf16[32,1024]{1,0:T(8,128)(2,1)S(1)}, bf16[32,1024]{1,0:T(8,128)(2,1)S(1)}, u32[]{:S(2)}, u32[]{:S(2)}) collective-permute-start(bf16[32,1024]{1,0:T(8,128)(2,1)S(1)} %pad_maximum_fusion.refs_0_), channel_id=1, source_target_pairs={{0,24},{4,28},{8,16},{12,20},{16,8},{20,12},{24,0},{28,4},{1,25},{... | collective-permute-start | bytes 196616 | tf_op jit(solution)/shard_map/ppermute | solution.py:221
  8.0 5.7 %collective-permute-start.5 = (bf16[32,1024]{1,0:T(8,128)(2,1)S(1)}, bf16[32,1024]{1,0:T(8,128)(2,1)S(1)}, u32[]{:S(2)}, u32[]{:S(2)}) collective-permute-start(bf16[32,1024]{1,0:T(8,128)(2,1)S(1)} %pad_maximum_fusion.refs_0_), channel_id=1, source_target_pairs={{0,16},{4,20},{8,24},{12,28},{16,0},{20,4},{24,8},{28,12},{1,17},{... | collective-permute-start | bytes 196616 | tf_op jit(solution)/shard_map/ppermute | solution.py:221
  8.0 5.8 %collective-permute-start.4 = (bf16[32,1024]{1,0:T(8,128)(2,1)S(1)}, bf16[32,1024]{1,0:T(8,128)(2,1)S(1)}, u32[]{:S(2)}, u32[]{:S(2)}) collective-permute-start(bf16[32,1024]{1,0:T(8,128)(2,1)S(1)} %pad_maximum_fusion.refs_0_), channel_id=1, source_target_pairs={{0,8},{4,12},{8,0},{12,4},{16,24},{20,28},{24,16},{28,20},{1,9},{5... | collective-permute-start | bytes 196616 | tf_op jit(solution)/shard_map/ppermute | solution.py:221
  8.8 3.6 %collective-permute-start = (s32[1,1]{1,0:T(1,128)}, s32[1,1]{1,0:T(1,128)}, u32[]{:S(2)}, u32[]{:S(2)}) collective-permute-start(s32[1,1]{1,0:T(1,128)} %param.12), channel_id=1, source_target_pairs={{0,4},{4,0},{8,12},{12,8},{16,20},{20,16},{24,28},{28,24},{1,5},{5... | collective-permute-start | bytes 20 | tf_op jit(solution)/shard_map/ppermute | solution.py:218
  10.3 4.8 %slice-start = ((s8[8388608]{0:T(1024)(128)(4,1)}), s8[4194304]{0:T(1024)(128)(4,1)S(1)}, s32[]{:S(2)}) async-start(s8[8388608]{0:T(1024)(128)(4,1)} %bitcast.3), calls=%async_computation | async-start | bytes 8388608
  11.1 1.3 %copy-start = (bf16[32,4096]{1,0:T(8,128)(2,1)S(1)}, bf16[32,4096]{1,0:T(8,128)(2,1)}, u32[]{:S(2)}) copy-start(bf16[32,4096]{1,0:T(8,128)(2,1)} %refs_3_.1) | copy-start | bytes 786436
  11.1 1.3 %copy-start.1 = (bf16[128,1024]{1,0:T(8,128)(2,1)S(1)}, bf16[128,1024]{1,0:T(8,128)(2,1)}, u32[]{:S(2)}) copy-start(bf16[128,1024]{1,0:T(8,128)(2,1)} %refs_4_.2) | copy-start | bytes 786436
  11.2 1.3 %copy-start.2 = (s32[8]{0:T(128)S(1)}, s32[8]{0:T(128)}, u32[]{:S(2)}) copy-start(s32[8]{0:T(128)} %param.13) | copy-start | bytes 100
  11.2 4.0 %slice-start.1 = ((s8[8388608]{0:T(1024)(128)(4,1)}), s8[4194304]{0:T(1024)(128)(4,1)S(1)}, s32[]{:S(2)}) async-start(s8[8388608]{0:T(1024)(128)(4,1)} %bitcast.3), calls=%async_computation.1 | async-start | bytes 8388608
  11.2 7.2 %collective-permute-start.3 = (bf16[32,4096]{1,0:T(8,128)(2,1)S(1)}, bf16[32,4096]{1,0:T(8,128)(2,1)S(1)}, u32[]{:S(2)}, u32[]{:S(2)}) collective-permute-start(bf16[32,4096]{1,0:T(8,128)(2,1)S(1)} %collective-permute-done.1.refs_1_.refs_5_.refs_2_), channel_id=1, source_target_pairs={{0,1},{1,0},{2,3},{3,2},{4,5},{5,4},{6,7},{7,6},{8,9},{9,8},{10,11... | collective-permute-start | bytes 786440 | tf_op jit(solution)/shard_map/ppermute | solution.py:215
  13.8 4.7 %collective-permute-start.2 = (bf16[32,4096]{1,0:T(8,128)(2,1)S(1)}, bf16[32,4096]{1,0:T(8,128)(2,1)S(1)}, u32[]{:S(2)}, u32[]{:S(2)}) collective-permute-start(bf16[32,4096]{1,0:T(8,128)(2,1)S(1)} %get-tuple-element.29.refs_3_.refs_0_), channel_id=1, source_target_pairs={{0,1},{1,0},{2,3},{3,2},{4,5},{5,4},{6,7},{7,6},{8,9},{9,8},{10,11... | collective-permute-start | bytes 786440 | tf_op jit(solution)/shard_map/ppermute | solution.py:215
  13.9 4.5 %collective-permute-start.7 = (bf16[32,1024]{1,0:T(8,128)(2,1)S(1)}, bf16[32,1024]{1,0:T(8,128)(2,1)S(1)}, u32[]{:S(2)}, u32[]{:S(2)}) collective-permute-start(bf16[32,1024]{1,0:T(8,128)(2,1)S(1)} %get-tuple-element.32), channel_id=1, source_target_pairs={{0,4},{4,0},{8,12},{12,8},{16,20},{20,16},{24,28},{28,24},{1,5},{5... | collective-permute-start | bytes 196616 | tf_op jit(solution)/shard_map/ppermute | solution.py:218
  18.7 5.6 %collective-permute-start.13 = (f32[2,32,4096]{2,1,0:T(8,128)S(1)}, f32[2,32,4096]{2,1,0:T(8,128)S(1)}, u32[]{:S(2)}, u32[]{:S(2)}) collective-permute-start(f32[2,32,4096]{2,1,0:T(8,128)S(1)} %get-tuple-element.43), channel_id=1, source_target_pairs={{0,1},{1,0},{2,3},{3,2},{4,5},{5,4},{6,7},{7,6},{8,9},{9,8},{10,11... | collective-permute-start | bytes 3145736 | tf_op jit(solution)/shard_map/ppermute | solution.py:215
  18.7 4.0 %collective-permute-start.10 = (f32[32,128]{1,0:T(8,128)S(1)}, f32[32,128]{1,0:T(8,128)S(1)}, u32[]{:S(2)}, u32[]{:S(2)}) collective-permute-start(f32[32,128]{1,0:T(8,128)S(1)} %get-tuple-element.36.refs_5_.refs_0_), channel_id=1, source_target_pairs={{0,3},{1,2},{2,1},{3,0},{4,7},{5,6},{6,5},{7,4},{8,11},{9,10},{10,... | collective-permute-start | bytes 49160 | tf_op jit(solution)/shard_map/ppermute | solution.py:215
  19.4 3.7 %collective-permute-start.9 = (f32[32,128]{1,0:T(8,128)S(1)}, f32[32,128]{1,0:T(8,128)S(1)}, u32[]{:S(2)}, u32[]{:S(2)}) collective-permute-start(f32[32,128]{1,0:T(8,128)S(1)} %get-tuple-element.36.refs_5_.refs_0_), channel_id=1, source_target_pairs={{0,2},{1,3},{2,0},{3,1},{4,6},{5,7},{6,4},{7,5},{8,10},{9,11},{10,... | collective-permute-start | bytes 49160 | tf_op jit(solution)/shard_map/ppermute | solution.py:215
  20.9 2.2 %collective-permute-start.8 = (f32[32,128]{1,0:T(8,128)S(1)}, f32[32,128]{1,0:T(8,128)S(1)}, u32[]{:S(2)}, u32[]{:S(2)}) collective-permute-start(f32[32,128]{1,0:T(8,128)S(1)} %get-tuple-element.36.refs_5_.refs_0_), channel_id=1, source_target_pairs={{0,1},{1,0},{2,3},{3,2},{4,5},{5,4},{6,7},{7,6},{8,9},{9,8},{10,11... | collective-permute-start | bytes 49160 | tf_op jit(solution)/shard_map/ppermute | solution.py:215
  20.9 2.2 %collective-permute-start.11 = (bf16[16,1024]{1,0:T(8,128)(2,1)S(1)}, bf16[16,1024]{1,0:T(8,128)(2,1)S(1)}, u32[]{:S(2)}, u32[]{:S(2)}) collective-permute-start(bf16[16,1024]{1,0:T(8,128)(2,1)S(1)} %get-tuple-element.38), channel_id=1, source_target_pairs={{0,1},{1,0},{2,3},{3,2},{4,5},{5,4},{6,7},{7,6},{8,9},{9,8},{10,11... | collective-permute-start | bytes 98312 | tf_op jit(solution)/shard_map/ppermute | solution.py:215
  23.3 4.3 %collective-permute-start.12 = (bf16[32,1024]{1,0:T(8,128)(2,1)S(1)}, bf16[32,1024]{1,0:T(8,128)(2,1)S(1)}, u32[]{:S(2)}, u32[]{:S(2)}) collective-permute-start(bf16[32,1024]{1,0:T(8,128)(2,1)S(1)} %get-tuple-element.41.refs_1_), channel_id=1, source_target_pairs={{0,4},{4,0},{8,12},{12,8},{16,20},{20,16},{24,28},{28,24},{1,5},{5... | collective-permute-start | bytes 196616 | tf_op jit(solution)/shard_map/ppermute | solution.py:218
  24.8 8.3 %collective-permute-start.14 = (bf16[32,4096]{1,0:T(8,128)(2,1)S(1)}, bf16[32,4096]{1,0:T(8,128)(2,1)S(1)}, u32[]{:S(2)}, u32[]{:S(2)}) collective-permute-start(bf16[32,4096]{1,0:T(8,128)(2,1)S(1)} %get-tuple-element.44.refs_3_), channel_id=1, source_target_pairs={{0,2},{1,3},{2,0},{3,1},{4,6},{5,7},{6,4},{7,5},{8,10},{9,11},{10,... | collective-permute-start | bytes 786440 | tf_op jit(solution)/shard_map/ppermute | solution.py:215
  27.7 6.2 %collective-permute-start.15 = (bf16[32,1024]{1,0:T(8,128)(2,1)S(1)}, bf16[32,1024]{1,0:T(8,128)(2,1)S(1)}, u32[]{:S(2)}, u32[]{:S(2)}) collective-permute-start(bf16[32,1024]{1,0:T(8,128)(2,1)S(1)} %get-tuple-element.48), channel_id=1, source_target_pairs={{0,24},{4,28},{8,16},{12,20},{16,8},{20,12},{24,0},{28,4},{1,25},{... | collective-permute-start | bytes 196616 | tf_op jit(solution)/shard_map/ppermute | solution.py:221
  31.4 5.2 %collective-permute-start.16 = (bf16[32,1024]{1,0:T(8,128)(2,1)S(1)}, bf16[32,1024]{1,0:T(8,128)(2,1)S(1)}, u32[]{:S(2)}, u32[]{:S(2)}) collective-permute-start(bf16[32,1024]{1,0:T(8,128)(2,1)S(1)} %get-tuple-element.49), channel_id=1, source_target_pairs={{0,16},{4,20},{8,24},{12,28},{16,0},{20,4},{24,8},{28,12},{1,17},{... | collective-permute-start | bytes 196616 | tf_op jit(solution)/shard_map/ppermute | solution.py:221
  31.4 5.2 %collective-permute-start.17 = (bf16[32,1024]{1,0:T(8,128)(2,1)S(1)}, bf16[32,1024]{1,0:T(8,128)(2,1)S(1)}, u32[]{:S(2)}, u32[]{:S(2)}) collective-permute-start(bf16[32,1024]{1,0:T(8,128)(2,1)S(1)} %get-tuple-element.50), channel_id=1, source_target_pairs={{0,8},{4,12},{8,0},{12,4},{16,24},{20,28},{24,16},{28,20},{1,9},{5... | collective-permute-start | bytes 196616 | tf_op jit(solution)/shard_map/ppermute | solution.py:221

commit v3 on v2

--- a/solution.py
+++ b/solution.py
@@ -65,7 +65,7 @@
     upstream_here[...] = upstream[...]
     adapters = lax.broadcasted_iota(jnp.int32, owner.shape, 1)
     for k in range(len(blocks)):
-        here = jnp.where(adapters == blocks[k][...], owner[...], 0)
+        here = jnp.where(adapters == blocks[k][:1, :1], owner[...], 0)
         slot = jnp.sum(here, axis=1, keepdims=True)
         slots[k : k + 1, :] = jnp.broadcast_to(slot, (1, slots.shape[1]))
 
@@ -230,8 +230,8 @@
         mine = jnp.concatenate([down[0], up[0]], axis=0)
         column = [mine] + [over_outer(mine, k) for k in range(1, outer)]
         far = over_tensor(tokens, half)
-        blocks = [adapter_per_block]
-        blocks += [over_inner(adapter_per_block, k) for k in range(1, inner)]
+        block = jnp.broadcast_to(adapter_per_block, (8, 128))
+        blocks = [block] + [over_inner(block, k) for k in range(1, inner)]
 
         (column[0],) = call(
             own_kernel,

time: 37.4 us -> 37.1 us (level)
  Pallas kernels: 8.93 us -> 7.79 us
  starting transfers between devices: 20 us -> 21 us
    pallas_call x12, Pallas kernels: 8.93 us -> 7.79 us  [call(): pl.pallas_call(run, name=name, out_shape=outs, in_specs=specs + [pl.Block...]
    ppermute x3, starting transfers between devices: 3.76 us -> 4.74 us  [over_inner(): return lax.ppermute(x, 'dp', [(d, d ^ k) for d in range(dp_size)])]
  transfers between devices with their start and end apart: 18 -> 18, of which waited for: 6 -> 5; matrix products, arithmetic and copies ran while one was open for 2% -> 2% of each run, Pallas kernels for 21% -> 19%
where the time goes in v3:
time: 37.1 us; the launch traced here: 36.9 us
  starting transfers between devices  21 us (57%)
  Pallas kernels  7.79 us (21%)
  waiting for transfers between devices  5.86 us (16%)
  between operations  1.43 us (4%)
  other arithmetic  0.78 us (2%)
    ppermute x6, starting transfers between devices, over_outer(): return lax.ppermute(x, 'dp', [(d, d ^ k * inner) for d in range(dp_size)])  8.84 us
    pallas_call x12, Pallas kernels, call(): pl.pallas_call(run, name=name, out_shape=outs, in_specs=specs + [pl.Block...  7.79 us
    ppermute x9, starting transfers between devices, over_tensor(): return lax.ppermute(x, 'tensor', [(t, t ^ k) for t in range(tensor_size)])  7.4 us
    ppermute x3, starting transfers between devices, over_inner(): return lax.ppermute(x, 'dp', [(d, d ^ k) for d in range(dp_size)])  4.74 us
    ppermute x6, waiting for transfers between devices, over_outer(): return lax.ppermute(x, 'dp', [(d, d ^ k * inner) for d in range(dp_size)])  2.82 us
    ppermute x3, waiting for transfers between devices, over_inner(): return lax.ppermute(x, 'dp', [(d, d ^ k) for d in range(dp_size)])  2.74 us
    concatenate x1, other arithmetic, per_device(): mine = jnp.concatenate([down[0], up[0]], axis=0)  0.78 us
  transfers between devices with their start and end apart: 18, of which 5 were waited for; matrix products, arithmetic and copies ran while one was open for 2% of the time, Pallas kernels for 19%

profile of v3, /device:TPU:0, one launch (start us, length us, event | category | flops | bytes accessed | tf_op | source)
XLA Modules:
  0.0 36.9 jit_solution(10299842928357177070)
XLA Ops:
  0.6 3.0 %collective-permute-start.1 = (bf16[32,4096]{1,0:T(8,128)(2,1)}, bf16[32,4096]{1,0:T(8,128)(2,1)S(1)}, u32[]{:S(2)}, u32[]{:S(2)}) collective-permute-start(bf16[32,4096]{1,0:T(8,128)(2,1)} %refs_3_.1), channel_id=1, source_target_pairs={{0,2},{1,3},{2,0},{3,1},{4,6},{5,7},{6,4},{7,5},{8,10},{9,11},{10,... | collective-permute-start | bytes 786440 | tf_op jit(solution)/shard_map/ppermute | solution.py:215
  3.7 0.8 %pad_maximum_fusion.refs_0_ = bf16[32,1024]{1,0:T(8,128)(2,1)S(1)} fusion(bf16[16,1024]{1,0:T(8,128)(2,1)} %bitcast.8, bf16[16,1024]{1,0:T(8,128)(2,1)} %bitcast.9), kind=kLoop, calls=%fused_computation | loop fusion | flops 131072 | bytes 131072 | tf_op jit(solution)/shard_map/concatenate | solution.py:230
  4.4 3.6 %collective-permute-start.6 = (bf16[32,1024]{1,0:T(8,128)(2,1)S(1)}, bf16[32,1024]{1,0:T(8,128)(2,1)S(1)}, u32[]{:S(2)}, u32[]{:S(2)}) collective-permute-start(bf16[32,1024]{1,0:T(8,128)(2,1)S(1)} %pad_maximum_fusion.refs_0_), channel_id=1, source_target_pairs={{0,24},{4,28},{8,16},{12,20},{16,8},{20,12},{24,0},{28,4},{1,25},{... | collective-permute-start | bytes 196616 | tf_op jit(solution)/shard_map/ppermute | solution.py:221
  8.0 0.0 collective-permute-start.5
  8.0 0.8 %collective-permute-start.4 = (bf16[32,1024]{1,0:T(8,128)(2,1)S(1)}, bf16[32,1024]{1,0:T(8,128)(2,1)S(1)}, u32[]{:S(2)}, u32[]{:S(2)}) collective-permute-start(bf16[32,1024]{1,0:T(8,128)(2,1)S(1)} %pad_maximum_fusion.refs_0_), channel_id=1, source_target_pairs={{0,8},{4,12},{8,0},{12,4},{16,24},{20,28},{24,16},{28,20},{1,9},{5... | collective-permute-start | bytes 196616 | tf_op jit(solution)/shard_map/ppermute | solution.py:221
  9.5 0.0 slice-start
  9.5 0.0 copy-start
  9.5 0.0 copy-start.1
  9.5 0.0 copy-start.2
  9.5 0.0 slice-start.1
  9.6 1.6 %collective-permute-start = (s32[8,128]{1,0:T(8,128)S(1)}, s32[8,128]{1,0:T(8,128)S(1)}, u32[]{:S(2)}, u32[]{:S(2)}) collective-permute-start(s32[8,128]{1,0:T(8,128)S(1)} %broadcast_in_dim.8.refs_1_), channel_id=1, source_target_pairs={{0,4},{4,0},{8,12},{12,8},{16,20},{20,16},{24,28},{28,24},{1,5},{5... | collective-permute-start | bytes 12296 | tf_op jit(solution)/shard_map/ppermute | solution.py:218
  11.1 0.0 collective-permute-done.1.refs_1_.refs_5_.refs_2_
  11.1 0.1 collective-permute-start.3
  11.2 2.0 %collective-permute-done.refs_2_ = s32[8,128]{1,0:T(8,128)S(1)} collective-permute-done((s32[8,128]{1,0:T(8,128)S(1)}, s32[8,128]{1,0:T(8,128)S(1)}, u32[]{:S(2)}, u32[]{:S(2)}) %collective-permute-start) | collective-permute-done | bytes 4128 | tf_op jit(solution)/shard_map/ppermute | solution.py:218
  13.2 0.0 copy-done
  13.2 0.0 copy-done.1
  13.2 0.0 copy-done.2
  13.2 0.2 slots.1
  13.4 0.0 collective-permute-start.2
  13.4 0.0 collective-permute-done.6.refs_4_
  13.4 0.0 collective-permute-done.5.refs_3_
  13.4 0.0 collective-permute-done.4.refs_2_
  13.5 0.1 pick.1
  13.6 1.6 %collective-permute-start.7 = (bf16[32,1024]{1,0:T(8,128)(2,1)S(1)}, bf16[32,1024]{1,0:T(8,128)(2,1)S(1)}, u32[]{:S(2)}, u32[]{:S(2)}) collective-permute-start(bf16[32,1024]{1,0:T(8,128)(2,1)S(1)} %get-tuple-element.32), channel_id=1, source_target_pairs={{0,4},{4,0},{8,12},{12,8},{16,20},{20,16},{24,28},{28,24},{1,5},{5... | collective-permute-start | bytes 196616 | tf_op jit(solution)/shard_map/ppermute | solution.py:218
  15.1 0.0 slice-done
  15.1 0.0 slice-done.1
  15.1 2.8 %base.1 = (f32[2,32,4096]{2,1,0:T(8,128)S(1)}, f32[2,32,4096]{2,1,0:T(8,128)S(1)}) custom-call(bf16[128,1024]{1,0:T(8,128)(2,1)S(1)} %get-tuple-element.33.refs_7_.refs_0_.refs_5_, bf16[4096,1024]{1,0:T(8,128)(2,1)S(1)} %bitcast.6, bf16[32,1024]{1,0:T(8,128)(2,1)S(1)} %get-tuple-element.31.refs_1_.refs_2_), custom_call_target="tpu_custom_call" | custom-call | flops 1073741824 | bytes 8388608 | tf_op jit(solution)/shard_map/base/pallas_call | solution.py:36
  18.0 0.1 collective-permute-done.7.refs_2_
  18.1 0.0 collective-permute-done.3.refs_6_.refs_3_
  18.1 0.0 collective-permute-done.2.refs_4_.refs_1_
  18.1 0.3 low.1
  18.4 0.1 collective-permute-start.13
  18.5 0.4 %collective-permute-start.10 = (f32[32,128]{1,0:T(8,128)S(1)}, f32[32,128]{1,0:T(8,128)S(1)}, u32[]{:S(2)}, u32[]{:S(2)}) collective-permute-start(f32[32,128]{1,0:T(8,128)S(1)} %get-tuple-element.36.refs_5_.refs_0_), channel_id=1, source_target_pairs={{0,3},{1,2},{2,1},{3,0},{4,7},{5,6},{6,5},{7,4},{8,11},{9,10},{10,... | collective-permute-start | bytes 49160 | tf_op jit(solution)/shard_map/ppermute | solution.py:215
  18.9 1.6 %collective-permute-start.9 = (f32[32,128]{1,0:T(8,128)S(1)}, f32[32,128]{1,0:T(8,128)S(1)}, u32[]{:S(2)}, u32[]{:S(2)}) collective-permute-start(f32[32,128]{1,0:T(8,128)S(1)} %get-tuple-element.36.refs_5_.refs_0_), channel_id=1, source_target_pairs={{0,2},{1,3},{2,0},{3,1},{4,6},{5,7},{6,4},{7,5},{8,10},{9,11},{10,... | collective-permute-start | bytes 49160 | tf_op jit(solution)/shard_map/ppermute | solution.py:215
  20.5 0.0 collective-permute-start.8
  20.6 0.5 %collective-permute-start.11 = (bf16[16,1024]{1,0:T(8,128)(2,1)S(1)}, bf16[16,1024]{1,0:T(8,128)(2,1)S(1)}, u32[]{:S(2)}, u32[]{:S(2)}) collective-permute-start(bf16[16,1024]{1,0:T(8,128)(2,1)S(1)} %get-tuple-element.38), channel_id=1, source_target_pairs={{0,1},{1,0},{2,3},{3,2},{4,5},{5,4},{6,7},{7,6},{8,9},{9,8},{10,11... | collective-permute-start | bytes 98312 | tf_op jit(solution)/shard_map/ppermute | solution.py:215
  21.1 1.3 %mixed.1.refs_6_.refs_0_ = f32[128,1024]{1,0:T(8,128)S(1)} custom-call(bf16[32,4096]{1,0:T(8,128)(2,1)S(1)} %get-tuple-element.29.refs_3_.refs_0_, bf16[32,4096]{1,0:T(8,128)(2,1)S(1)} %collective-permute-done.2.refs_4_.refs_1_, bf16[32,4096]{1,0:T(8,128)(2,1)S(1)} %collective-permute-done.1.refs_1_.refs_5_.refs_2_, ...), custom_call_target="tpu_custom_call" | custom-call | flops 1073741824 | bytes 8388608 | tf_op jit(solution)/shard_map/mixed/pallas_call | solution.py:36
  22.4 0.0 collective-permute-done.10.refs_3_
  22.4 0.3 collective-permute-done.9.refs_2_
  22.7 0.0 collective-permute-done.8.refs_1_
  22.7 0.0 collective-permute-done.11.refs_7_.refs_4_
  22.7 0.2 gradient.1
  22.9 1.6 %collective-permute-start.12 = (bf16[32,1024]{1,0:T(8,128)(2,1)S(1)}, bf16[32,1024]{1,0:T(8,128)(2,1)S(1)}, u32[]{:S(2)}, u32[]{:S(2)}) collective-permute-start(bf16[32,1024]{1,0:T(8,128)(2,1)S(1)} %get-tuple-element.41.refs_1_), channel_id=1, source_target_pairs={{0,4},{4,0},{8,12},{12,8},{16,20},{20,16},{24,28},{28,24},{1,5},{5... | collective-permute-start | bytes 196616 | tf_op jit(solution)/shard_map/ppermute | solution.py:218
  24.5 0.0 collective-permute-done.13.refs_1_
  24.5 0.5 %add.1 = (f32[32,4096]{1,0:T(8,128)S(1)}, bf16[32,4096]{1,0:T(8,128)(2,1)S(1)}) custom-call(f32[2,32,4096]{2,1,0:T(8,128)S(1)} %get-tuple-element.42.refs_0_, f32[2,32,4096]{2,1,0:T(8,128)S(1)} %collective-permute-done.13.refs_1_, bf16[32,128]{1,0:T(8,128)(2,1)S(1)} %get-tuple-element.39.refs_2_.refs_1_, ...), custom_call_target="tpu_custom_call" | custom-call | tf_op jit(solution)/shard_map/add/pallas_call | solution.py:36
  25.0 1.6 %collective-permute-start.14 = (bf16[32,4096]{1,0:T(8,128)(2,1)S(1)}, bf16[32,4096]{1,0:T(8,128)(2,1)S(1)}, u32[]{:S(2)}, u32[]{:S(2)}) collective-permute-start(bf16[32,4096]{1,0:T(8,128)(2,1)S(1)} %get-tuple-element.44.refs_3_), channel_id=1, source_target_pairs={{0,2},{1,3},{2,0},{3,1},{4,6},{5,7},{6,4},{7,5},{8,10},{9,11},{10,... | collective-permute-start | bytes 786440 | tf_op jit(solution)/shard_map/ppermute | solution.py:215
  26.6 0.6 %collective-permute-done.12.refs_2_ = bf16[32,1024]{1,0:T(8,128)(2,1)S(1)} collective-permute-done((bf16[32,1024]{1,0:T(8,128)(2,1)S(1)}, bf16[32,1024]{1,0:T(8,128)(2,1)S(1)}, u32[]{:S(2)}, u32[]{:S(2)}) %collective-permute-start.12) | collective-permute-done | bytes 65568 | tf_op jit(solution)/shard_map/ppermute | solution.py:218
  27.2 0.1 route.1
  27.3 3.8 %collective-permute-start.15 = (bf16[32,1024]{1,0:T(8,128)(2,1)S(1)}, bf16[32,1024]{1,0:T(8,128)(2,1)S(1)}, u32[]{:S(2)}, u32[]{:S(2)}) collective-permute-start(bf16[32,1024]{1,0:T(8,128)(2,1)S(1)} %get-tuple-element.48), channel_id=1, source_target_pairs={{0,24},{4,28},{8,16},{12,20},{16,8},{20,12},{24,0},{28,4},{1,25},{... | collective-permute-start | bytes 196616 | tf_op jit(solution)/shard_map/ppermute | solution.py:221
  31.0 0.0 collective-permute-start.16
  31.0 0.7 %collective-permute-start.17 = (bf16[32,1024]{1,0:T(8,128)(2,1)S(1)}, bf16[32,1024]{1,0:T(8,128)(2,1)S(1)}, u32[]{:S(2)}, u32[]{:S(2)}) collective-permute-start(bf16[32,1024]{1,0:T(8,128)(2,1)S(1)} %get-tuple-element.50), channel_id=1, source_target_pairs={{0,8},{4,12},{8,0},{12,4},{16,24},{20,28},{24,16},{28,20},{1,9},{5... | collective-permute-start | bytes 196616 | tf_op jit(solution)/shard_map/ppermute | solution.py:221
  31.7 1.0 %finish.1 = bf16[128,1024]{1,0:T(8,128)(2,1)} custom-call(f32[128,1024]{1,0:T(8,128)S(1)} %mixed.1.refs_6_.refs_0_, bf16[32,128]{1,0:T(8,128)(2,1)S(1)} %get-tuple-element.39.refs_2_.refs_1_, bf16[32,1024]{1,0:T(8,128)(2,1)S(1)} %get-tuple-element.40.refs_3_.refs_2_, bf16[32,1024]{1,0:T(8,128)(2,1)S(1)} %get-tuple-element.45.refs_3_.refs_0_), custom_call_target="tpu_custom_call" | custom-call | flops 4294967296 | tf_op jit(solution)/shard_map/finish/pallas_call | solution.py:36
  32.7 0.0 collective-permute-done.14.refs_1_
  32.7 0.7 %close.1 = (bf16[32,4096]{1,0:T(8,128)(2,1)}, f32[8,128]{1,0:T(8,128)S(1)}) custom-call(f32[32,4096]{1,0:T(8,128)S(1)} %get-tuple-element.46.refs_0_, bf16[32,4096]{1,0:T(8,128)(2,1)S(1)} %collective-permute-done.14.refs_1_), custom_call_target="tpu_custom_call" | custom-call | tf_op jit(solution)/shard_map/close/pallas_call | solution.py:36
  33.4 0.0 collective-permute-done.15.refs_1_
  33.5 2.7 %collective-permute-done.16.refs_2_ = bf16[32,1024]{1,0:T(8,128)(2,1)S(1)} collective-permute-done((bf16[32,1024]{1,0:T(8,128)(2,1)S(1)}, bf16[32,1024]{1,0:T(8,128)(2,1)S(1)}, u32[]{:S(2)}, u32[]{:S(2)}) %collective-permute-start.16) | collective-permute-done | bytes 65568 | tf_op jit(solution)/shard_map/ppermute | solution.py:221
  36.2 0.0 collective-permute-done.17.refs_3_
  36.2 0.7 %sum.1 = (f32[1,16,1024]{2,1,0:T(8,128)}, f32[1,16,1024]{2,1,0:T(8,128)}) custom-call(bf16[32,1024]{1,0:T(8,128)(2,1)S(1)} %get-tuple-element.45.refs_3_.refs_0_, bf16[32,1024]{1,0:T(8,128)(2,1)S(1)} %collective-permute-done.15.refs_1_, bf16[32,1024]{1,0:T(8,128)(2,1)S(1)} %collective-permute-done.16.refs_2_, ...), custom_call_target="tpu_custom_call" | custom-call | tf_op jit(solution)/shard_map/sum/pallas_call | solution.py:36
  (3 shorter events, 0.0 us)
Async XLA Ops:
  0.6 10.5 %collective-permute-start.1 = (bf16[32,4096]{1,0:T(8,128)(2,1)}, bf16[32,4096]{1,0:T(8,128)(2,1)S(1)}, u32[]{:S(2)}, u32[]{:S(2)}) collective-permute-start(bf16[32,4096]{1,0:T(8,128)(2,1)} %refs_3_.1), channel_id=1, source_target_pairs={{0,2},{1,3},{2,0},{3,1},{4,6},{5,7},{6,4},{7,5},{8,10},{9,11},{10,... | collective-permute-start | bytes 786440 | tf_op jit(solution)/shard_map/ppermute | solution.py:215
  4.4 9.0 %collective-permute-start.6 = (bf16[32,1024]{1,0:T(8,128)(2,1)S(1)}, bf16[32,1024]{1,0:T(8,128)(2,1)S(1)}, u32[]{:S(2)}, u32[]{:S(2)}) collective-permute-start(bf16[32,1024]{1,0:T(8,128)(2,1)S(1)} %pad_maximum_fusion.refs_0_), channel_id=1, source_target_pairs={{0,24},{4,28},{8,16},{12,20},{16,8},{20,12},{24,0},{28,4},{1,25},{... | collective-permute-start | bytes 196616 | tf_op jit(solution)/shard_map/ppermute | solution.py:221
  8.0 5.4 %collective-permute-start.5 = (bf16[32,1024]{1,0:T(8,128)(2,1)S(1)}, bf16[32,1024]{1,0:T(8,128)(2,1)S(1)}, u32[]{:S(2)}, u32[]{:S(2)}) collective-permute-start(bf16[32,1024]{1,0:T(8,128)(2,1)S(1)} %pad_maximum_fusion.refs_0_), channel_id=1, source_target_pairs={{0,16},{4,20},{8,24},{12,28},{16,0},{20,4},{24,8},{28,12},{1,17},{... | collective-permute-start | bytes 196616 | tf_op jit(solution)/shard_map/ppermute | solution.py:221
  8.0 5.4 %collective-permute-start.4 = (bf16[32,1024]{1,0:T(8,128)(2,1)S(1)}, bf16[32,1024]{1,0:T(8,128)(2,1)S(1)}, u32[]{:S(2)}, u32[]{:S(2)}) collective-permute-start(bf16[32,1024]{1,0:T(8,128)(2,1)S(1)} %pad_maximum_fusion.refs_0_), channel_id=1, source_target_pairs={{0,8},{4,12},{8,0},{12,4},{16,24},{20,28},{24,16},{28,20},{1,9},{5... | collective-permute-start | bytes 196616 | tf_op jit(solution)/shard_map/ppermute | solution.py:221
  9.5 5.6 %slice-start = ((s8[8388608]{0:T(1024)(128)(4,1)}), s8[4194304]{0:T(1024)(128)(4,1)S(1)}, s32[]{:S(2)}) async-start(s8[8388608]{0:T(1024)(128)(4,1)} %bitcast.5), calls=%async_computation | async-start | bytes 8388608
  9.5 3.7 %copy-start = (bf16[32,4096]{1,0:T(8,128)(2,1)S(1)}, bf16[32,4096]{1,0:T(8,128)(2,1)}, u32[]{:S(2)}) copy-start(bf16[32,4096]{1,0:T(8,128)(2,1)} %refs_3_.1) | copy-start | bytes 786436
  9.5 3.7 %copy-start.1 = (bf16[128,1024]{1,0:T(8,128)(2,1)S(1)}, bf16[128,1024]{1,0:T(8,128)(2,1)}, u32[]{:S(2)}) copy-start(bf16[128,1024]{1,0:T(8,128)(2,1)} %refs_4_.2) | copy-start | bytes 786436
  9.5 3.7 %copy-start.2 = (s32[8]{0:T(128)S(1)}, s32[8]{0:T(128)}, u32[]{:S(2)}) copy-start(s32[8]{0:T(128)} %param.13) | copy-start | bytes 100
  9.5 5.6 %slice-start.1 = ((s8[8388608]{0:T(1024)(128)(4,1)}), s8[4194304]{0:T(1024)(128)(4,1)S(1)}, s32[]{:S(2)}) async-start(s8[8388608]{0:T(1024)(128)(4,1)} %bitcast.5), calls=%async_computation.1 | async-start | bytes 8388608
  9.6 3.7 %collective-permute-start = (s32[8,128]{1,0:T(8,128)S(1)}, s32[8,128]{1,0:T(8,128)S(1)}, u32[]{:S(2)}, u32[]{:S(2)}) collective-permute-start(s32[8,128]{1,0:T(8,128)S(1)} %broadcast_in_dim.8.refs_1_), channel_id=1, source_target_pairs={{0,4},{4,0},{8,12},{12,8},{16,20},{20,16},{24,28},{28,24},{1,5},{5... | collective-permute-start | bytes 12296 | tf_op jit(solution)/shard_map/ppermute | solution.py:218
  11.1 7.0 %collective-permute-start.3 = (bf16[32,4096]{1,0:T(8,128)(2,1)S(1)}, bf16[32,4096]{1,0:T(8,128)(2,1)S(1)}, u32[]{:S(2)}, u32[]{:S(2)}) collective-permute-start(bf16[32,4096]{1,0:T(8,128)(2,1)S(1)} %collective-permute-done.1.refs_1_.refs_5_.refs_2_), channel_id=1, source_target_pairs={{0,1},{1,0},{2,3},{3,2},{4,5},{5,4},{6,7},{7,6},{8,9},{9,8},{10,11... | collective-permute-start | bytes 786440 | tf_op jit(solution)/shard_map/ppermute | solution.py:215
  13.4 4.7 %collective-permute-start.2 = (bf16[32,4096]{1,0:T(8,128)(2,1)S(1)}, bf16[32,4096]{1,0:T(8,128)(2,1)S(1)}, u32[]{:S(2)}, u32[]{:S(2)}) collective-permute-start(bf16[32,4096]{1,0:T(8,128)(2,1)S(1)} %get-tuple-element.29.refs_3_.refs_0_), channel_id=1, source_target_pairs={{0,1},{1,0},{2,3},{3,2},{4,5},{5,4},{6,7},{7,6},{8,9},{9,8},{10,11... | collective-permute-start | bytes 786440 | tf_op jit(solution)/shard_map/ppermute | solution.py:215
  13.6 4.5 %collective-permute-start.7 = (bf16[32,1024]{1,0:T(8,128)(2,1)S(1)}, bf16[32,1024]{1,0:T(8,128)(2,1)S(1)}, u32[]{:S(2)}, u32[]{:S(2)}) collective-permute-start(bf16[32,1024]{1,0:T(8,128)(2,1)S(1)} %get-tuple-element.32), channel_id=1, source_target_pairs={{0,4},{4,0},{8,12},{12,8},{16,20},{20,16},{24,28},{28,24},{1,5},{5... | collective-permute-start | bytes 196616 | tf_op jit(solution)/shard_map/ppermute | solution.py:218
  18.4 6.1 %collective-permute-start.13 = (f32[2,32,4096]{2,1,0:T(8,128)S(1)}, f32[2,32,4096]{2,1,0:T(8,128)S(1)}, u32[]{:S(2)}, u32[]{:S(2)}) collective-permute-start(f32[2,32,4096]{2,1,0:T(8,128)S(1)} %get-tuple-element.43), channel_id=1, source_target_pairs={{0,1},{1,0},{2,3},{3,2},{4,5},{5,4},{6,7},{7,6},{8,9},{9,8},{10,11... | collective-permute-start | bytes 3145736 | tf_op jit(solution)/shard_map/ppermute | solution.py:215
  18.5 3.9 %collective-permute-start.10 = (f32[32,128]{1,0:T(8,128)S(1)}, f32[32,128]{1,0:T(8,128)S(1)}, u32[]{:S(2)}, u32[]{:S(2)}) collective-permute-start(f32[32,128]{1,0:T(8,128)S(1)} %get-tuple-element.36.refs_5_.refs_0_), channel_id=1, source_target_pairs={{0,3},{1,2},{2,1},{3,0},{4,7},{5,6},{6,5},{7,4},{8,11},{9,10},{10,... | collective-permute-start | bytes 49160 | tf_op jit(solution)/shard_map/ppermute | solution.py:215
  18.9 3.7 %collective-permute-start.9 = (f32[32,128]{1,0:T(8,128)S(1)}, f32[32,128]{1,0:T(8,128)S(1)}, u32[]{:S(2)}, u32[]{:S(2)}) collective-permute-start(f32[32,128]{1,0:T(8,128)S(1)} %get-tuple-element.36.refs_5_.refs_0_), channel_id=1, source_target_pairs={{0,2},{1,3},{2,0},{3,1},{4,6},{5,7},{6,4},{7,5},{8,10},{9,11},{10,... | collective-permute-start | bytes 49160 | tf_op jit(solution)/shard_map/ppermute | solution.py:215
  20.5 2.1 %collective-permute-start.8 = (f32[32,128]{1,0:T(8,128)S(1)}, f32[32,128]{1,0:T(8,128)S(1)}, u32[]{:S(2)}, u32[]{:S(2)}) collective-permute-start(f32[32,128]{1,0:T(8,128)S(1)} %get-tuple-element.36.refs_5_.refs_0_), channel_id=1, source_target_pairs={{0,1},{1,0},{2,3},{3,2},{4,5},{5,4},{6,7},{7,6},{8,9},{9,8},{10,11... | collective-permute-start | bytes 49160 | tf_op jit(solution)/shard_map/ppermute | solution.py:215
  20.6 2.1 %collective-permute-start.11 = (bf16[16,1024]{1,0:T(8,128)(2,1)S(1)}, bf16[16,1024]{1,0:T(8,128)(2,1)S(1)}, u32[]{:S(2)}, u32[]{:S(2)}) collective-permute-start(bf16[16,1024]{1,0:T(8,128)(2,1)S(1)} %get-tuple-element.38), channel_id=1, source_target_pairs={{0,1},{1,0},{2,3},{3,2},{4,5},{5,4},{6,7},{7,6},{8,9},{9,8},{10,11... | collective-permute-start | bytes 98312 | tf_op jit(solution)/shard_map/ppermute | solution.py:215
  22.9 4.3 %collective-permute-start.12 = (bf16[32,1024]{1,0:T(8,128)(2,1)S(1)}, bf16[32,1024]{1,0:T(8,128)(2,1)S(1)}, u32[]{:S(2)}, u32[]{:S(2)}) collective-permute-start(bf16[32,1024]{1,0:T(8,128)(2,1)S(1)} %get-tuple-element.41.refs_1_), channel_id=1, source_target_pairs={{0,4},{4,0},{8,12},{12,8},{16,20},{20,16},{24,28},{28,24},{1,5},{5... | collective-permute-start | bytes 196616 | tf_op jit(solution)/shard_map/ppermute | solution.py:218
  25.0 7.7 %collective-permute-start.14 = (bf16[32,4096]{1,0:T(8,128)(2,1)S(1)}, bf16[32,4096]{1,0:T(8,128)(2,1)S(1)}, u32[]{:S(2)}, u32[]{:S(2)}) collective-permute-start(bf16[32,4096]{1,0:T(8,128)(2,1)S(1)} %get-tuple-element.44.refs_3_), channel_id=1, source_target_pairs={{0,2},{1,3},{2,0},{3,1},{4,6},{5,7},{6,4},{7,5},{8,10},{9,11},{10,... | collective-permute-start | bytes 786440 | tf_op jit(solution)/shard_map/ppermute | solution.py:215
  27.3 6.2 %collective-permute-start.15 = (bf16[32,1024]{1,0:T(8,128)(2,1)S(1)}, bf16[32,1024]{1,0:T(8,128)(2,1)S(1)}, u32[]{:S(2)}, u32[]{:S(2)}) collective-permute-start(bf16[32,1024]{1,0:T(8,128)(2,1)S(1)} %get-tuple-element.48), channel_id=1, source_target_pairs={{0,24},{4,28},{8,16},{12,20},{16,8},{20,12},{24,0},{28,4},{1,25},{... | collective-permute-start | bytes 196616 | tf_op jit(solution)/shard_map/ppermute | solution.py:221
  31.0 5.2 %collective-permute-start.16 = (bf16[32,1024]{1,0:T(8,128)(2,1)S(1)}, bf16[32,1024]{1,0:T(8,128)(2,1)S(1)}, u32[]{:S(2)}, u32[]{:S(2)}) collective-permute-start(bf16[32,1024]{1,0:T(8,128)(2,1)S(1)} %get-tuple-element.49), channel_id=1, source_target_pairs={{0,16},{4,20},{8,24},{12,28},{16,0},{20,4},{24,8},{28,12},{1,17},{... | collective-permute-start | bytes 196616 | tf_op jit(solution)/shard_map/ppermute | solution.py:221
  31.0 5.2 %collective-permute-start.17 = (bf16[32,1024]{1,0:T(8,128)(2,1)S(1)}, bf16[32,1024]{1,0:T(8,128)(2,1)S(1)}, u32[]{:S(2)}, u32[]{:S(2)}) collective-permute-start(bf16[32,1024]{1,0:T(8,128)(2,1)S(1)} %get-tuple-element.50), channel_id=1, source_target_pairs={{0,8},{4,12},{8,0},{12,4},{16,24},{20,28},{24,16},{28,20},{1,9},{5... | collective-permute-start | bytes 196616 | tf_op jit(solution)/shard_map/ppermute | solution.py:221

commit v4 on v3

--- a/solution.py
+++ b/solution.py
@@ -59,9 +59,8 @@
 
 
 def slot_kernel(*refs):
-    owner, blocks = refs[0], refs[1:-5]
-    tokens, upstream, slots, tokens_here, upstream_here = refs[-5:]
-    tokens_here[...] = tokens[...]
+    owner, blocks = refs[0], refs[1:-3]
+    upstream, slots, upstream_here = refs[-3:]
     upstream_here[...] = upstream[...]
     adapters = lax.broadcasted_iota(jnp.int32, owner.shape, 1)
     for k in range(len(blocks)):
@@ -80,8 +79,11 @@
             start = pl.multiple_of((2 * n + ((t & 1) ^ side)) * rows, rows)
             at = (side * half + n) * rows
             rows_of[at : at + rows, :] = upstream[pl.ds(start, rows), :]
+    turned = rows_of[...].T
     for n in range(pieces_of_weight):
-        part = lax.dot_general(rows_of[...], weight[n * step : (n + 1) * step, :], nt, preferred_element_type=f32)
+        part = jnp.dot(
+            weight[n * step : (n + 1) * step, :], turned, preferred_element_type=f32
+        ).T
         for m in range(half):
             keep[m, :, n * step : (n + 1) * step] = part[m * rows : (m + 1) * rows]
             at = (half + m) * rows
@@ -90,6 +92,11 @@
 
 def own_kernel(source, target):
     target[...] = source[...]
+
+
+def stack_kernel(tokens, far, stack):
+    stack[0] = tokens[...]
+    stack[1] = far[...]
 
 
 def pick_kernel(outer, inner, *refs):
@@ -101,8 +108,8 @@
 
 def low_kernel(inner, parts, *refs):
     slots, found = refs[0], refs[1 : 1 + inner]
-    tokens = refs[1 + inner : 1 + inner + parts]
-    upstream, both, chosen, columns, down = refs[1 + inner + parts :]
+    tokens = refs[1 + inner : 3 + inner]
+    upstream, both, chosen, columns, down = refs[3 + inner :]
     i = lax.axis_index("dp") & (inner - 1)
     t = lax.axis_index("tensor")
     cols = columns.shape[1]
@@ -113,7 +120,7 @@
     start = pl.multiple_of(t * cols, cols)
     for k in range(parts):
         at = pl.multiple_of((t ^ k) * rows, rows)
-        columns[pl.ds(at, rows), :] = tokens[k][:, pl.ds(start, cols)]
+        columns[pl.ds(at, rows), :] = tokens[k & 1][k >> 1, :, pl.ds(start, cols)]
     both[:rank, :] = lax.dot_general(
         chosen[:rank, :], columns[...], nt, preferred_element_type=f32
     )
@@ -168,14 +175,14 @@
 
 
 def mixed_kernel(parts, *refs):
-    tokens = refs[:parts]
-    weight, total, gathered = refs[parts:]
+    tokens = refs[:2]
+    weight, total, gathered = refs[2:]
     t = lax.axis_index("tensor")
-    rows = tokens[0].shape[0]
+    rows = tokens[0].shape[1]
     step = weight.shape[0] // pieces_of_weight
     for k in range(parts):
         at = pl.multiple_of((t ^ k) * rows, rows)
-        gathered[pl.ds(at, rows), :] = tokens[k][...]
+        gathered[pl.ds(at, rows), :] = tokens[k & 1][k >> 1]
     for n in range(pieces_of_weight):
         part = jnp.dot(
             gathered[:, n * step : (n + 1) * step],
@@ -242,21 +249,35 @@
             flops=8 * flops,
             after=(far,),
         )
-        slots, tokens_here, upstream_here = call(
+        (stack,) = call(
+            stack_kernel,
+            "stack",
+            [shape((half, rows, width), bf16)],
+            (tokens, far),
+            [vmem()] * 2,
+            after=(column[0],),
+        )
+        (column[0],) = call(
+            own_kernel,
+            "again",
+            [shape(mine.shape, bf16)],
+            (column[0],),
+            [vmem()],
+            flops=8 * flops,
+            after=(),
+        )
+        pieces = [stack, over_tensor(stack, 1)]
+        slots, upstream_here = call(
             slot_kernel,
             "slots",
             [
                 shape((inner, 128), jnp.int32),
-                shape(tokens.shape, bf16),
                 shape(upstream.shape, bf16),
             ],
-            (owner.reshape(1, -1), *blocks, tokens, upstream),
-            [vmem()] * (inner + 3),
-            flops=flops,
-            moved=small_bytes,
+            (owner.reshape(1, -1), *blocks, upstream),
+            [vmem()] * (inner + 2),
             after=(column[0],),
         )
-        pieces = [tokens_here, over_tensor(tokens_here, 1), far, over_tensor(far, 1)]
         found = call(
             functools.partial(pick_kernel, outer, inner),
             "pick",
@@ -289,7 +310,7 @@
                 shape((rank, cols), bf16),
             ],
             (slots, *found, *pieces, upstream_here),
-            [vmem()] * (1 + inner + tensor_size + 1),
+            [vmem()] * (1 + inner + 2 + 1),
             flops=flops,
             moved=small_bytes,
         )
@@ -298,7 +319,7 @@
             "mixed",
             [shape((length, cols), f32)],
             (*pieces, weight),
-            [vmem()] * (tensor_size + 1),
+            [vmem()] * 3,
             [pltpu.VMEM((length, width), bf16)],
             flops,
             weight_bytes,

time: 37.1 us -> 36.7 us (0.989)
    pallas_call x12 -> x14, Pallas kernels: 7.79 us -> 7.43 us  [call(): pl.pallas_call(run, name=name, out_shape=outs, in_specs=specs + [pl.Block...]
    ppermute x9 -> x8, starting transfers between devices: 7.4 us -> 7.36 us  [over_tensor(): return lax.ppermute(x, 'tensor', [(t, t ^ k) for t in range(tensor_size)])]
  transfers between devices with their start and end apart: 18 -> 17, of which waited for: 5 -> 8; matrix products, arithmetic and copies ran while one was open for 2% -> 2% of each run, Pallas kernels for 19% -> 18%
where the time goes in v4:
time: 36.7 us; the launch traced here: 36.5 us
  starting transfers between devices  21 us (57%)
  Pallas kernels  7.43 us (20%)
  waiting for transfers between devices  5.92 us (16%)
  between operations  1.42 us (4%)
  other arithmetic  0.78 us (2%)
    ppermute x6, starting transfers between devices, over_outer(): return lax.ppermute(x, 'dp', [(d, d ^ k * inner) for d in range(dp_size)])  8.84 us
    pallas_call x14, Pallas kernels, call(): pl.pallas_call(run, name=name, out_shape=outs, in_specs=specs + [pl.Block...  7.43 us
    ppermute x8, starting transfers between devices, over_tensor(): return lax.ppermute(x, 'tensor', [(t, t ^ k) for t in range(tensor_size)])  7.36 us
    ppermute x3, starting transfers between devices, over_inner(): return lax.ppermute(x, 'dp', [(d, d ^ k) for d in range(dp_size)])  4.75 us
    ppermute x3, waiting for transfers between devices, over_inner(): return lax.ppermute(x, 'dp', [(d, d ^ k) for d in range(dp_size)])  2.82 us
    ppermute x6, waiting for transfers between devices, over_outer(): return lax.ppermute(x, 'dp', [(d, d ^ k * inner) for d in range(dp_size)])  2.79 us
    concatenate x1, other arithmetic, per_device(): mine = jnp.concatenate([down[0], up[0]], axis=0)  0.78 us
  transfers between devices with their start and end apart: 17, of which 8 were waited for; matrix products, arithmetic and copies ran while one was open for 2% of the time, Pallas kernels for 18%

profile of v4, /device:TPU:0, one launch (start us, length us, event | category | flops | bytes accessed | tf_op | source)
XLA Modules:
  0.0 36.5 jit_solution(4658912435334242812)
XLA Ops:
  0.6 3.0 %collective-permute-start = (bf16[32,4096]{1,0:T(8,128)(2,1)}, bf16[32,4096]{1,0:T(8,128)(2,1)S(1)}, u32[]{:S(2)}, u32[]{:S(2)}) collective-permute-start(bf16[32,4096]{1,0:T(8,128)(2,1)} %refs_0_.1), channel_id=1, source_target_pairs={{0,2},{1,3},{2,0},{3,1},{4,6},{5,7},{6,4},{7,5},{8,10},{9,11},{10,... | collective-permute-start | bytes 786440 | tf_op jit(solution)/shard_map/ppermute | solution.py:222
  3.7 0.8 %pad_maximum_fusion.refs_0_ = bf16[32,1024]{1,0:T(8,128)(2,1)S(1)} fusion(bf16[16,1024]{1,0:T(8,128)(2,1)} %bitcast.8, bf16[16,1024]{1,0:T(8,128)(2,1)} %bitcast.9), kind=kLoop, calls=%fused_computation | loop fusion | flops 131072 | bytes 131072 | tf_op jit(solution)/shard_map/concatenate | solution.py:237
  4.4 3.6 %collective-permute-start.5 = (bf16[32,1024]{1,0:T(8,128)(2,1)S(1)}, bf16[32,1024]{1,0:T(8,128)(2,1)S(1)}, u32[]{:S(2)}, u32[]{:S(2)}) collective-permute-start(bf16[32,1024]{1,0:T(8,128)(2,1)S(1)} %pad_maximum_fusion.refs_0_), channel_id=1, source_target_pairs={{0,24},{4,28},{8,16},{12,20},{16,8},{20,12},{24,0},{28,4},{1,25},{... | collective-permute-start | bytes 196616 | tf_op jit(solution)/shard_map/ppermute | solution.py:228
  8.0 0.0 collective-permute-start.4
  8.0 0.8 %collective-permute-start.3 = (bf16[32,1024]{1,0:T(8,128)(2,1)S(1)}, bf16[32,1024]{1,0:T(8,128)(2,1)S(1)}, u32[]{:S(2)}, u32[]{:S(2)}) collective-permute-start(bf16[32,1024]{1,0:T(8,128)(2,1)S(1)} %pad_maximum_fusion.refs_0_), channel_id=1, source_target_pairs={{0,8},{4,12},{8,0},{12,4},{16,24},{20,28},{24,16},{28,20},{1,9},{5... | collective-permute-start | bytes 196616 | tf_op jit(solution)/shard_map/ppermute | solution.py:228
  9.5 0.0 copy-start
  9.5 1.6 %collective-permute-start.2 = (s32[8,128]{1,0:T(8,128)S(1)}, s32[8,128]{1,0:T(8,128)S(1)}, u32[]{:S(2)}, u32[]{:S(2)}) collective-permute-start(s32[8,128]{1,0:T(8,128)S(1)} %broadcast_in_dim.8.refs_1_), channel_id=1, source_target_pairs={{0,4},{4,0},{8,12},{12,8},{16,20},{20,16},{24,28},{28,24},{1,5},{5... | collective-permute-start | bytes 12296 | tf_op jit(solution)/shard_map/ppermute | solution.py:225
  11.1 0.0 collective-permute-done.refs_1_
  11.1 0.0 copy-done
  11.1 0.0 slice-start
  11.1 0.0 copy-start.1
  11.2 0.0 copy-start.2
  11.2 0.0 slice-start.1
  11.2 0.1 collective-permute-start.1
  11.3 1.9 %collective-permute-done.2.refs_2_ = s32[8,128]{1,0:T(8,128)S(1)} collective-permute-done((s32[8,128]{1,0:T(8,128)S(1)}, s32[8,128]{1,0:T(8,128)S(1)}, u32[]{:S(2)}, u32[]{:S(2)}) %collective-permute-start.2) | collective-permute-done | bytes 4128 | tf_op jit(solution)/shard_map/ppermute | solution.py:225
  13.2 0.0 copy-done.1
  13.2 0.0 copy-done.2
  13.2 0.2 slots.1
  13.3 0.0 collective-permute-done.5.refs_4_
  13.3 0.1 collective-permute-done.4.refs_3_
  13.4 0.1 collective-permute-done.3.refs_2_
  13.5 0.1 pick.1
  13.6 1.6 %collective-permute-start.6 = (bf16[32,1024]{1,0:T(8,128)(2,1)S(1)}, bf16[32,1024]{1,0:T(8,128)(2,1)S(1)}, u32[]{:S(2)}, u32[]{:S(2)}) collective-permute-start(bf16[32,1024]{1,0:T(8,128)(2,1)S(1)} %get-tuple-element.30), channel_id=1, source_target_pairs={{0,4},{4,0},{8,12},{12,8},{16,20},{20,16},{24,28},{28,24},{1,5},{5... | collective-permute-start | bytes 196616 | tf_op jit(solution)/shard_map/ppermute | solution.py:225
  15.1 0.0 slice-done
  15.1 0.0 slice-done.1
  15.1 2.5 %base.1 = (f32[2,32,4096]{2,1,0:T(8,128)S(1)}, f32[2,32,4096]{2,1,0:T(8,128)S(1)}) custom-call(bf16[128,1024]{1,0:T(8,128)(2,1)S(1)} %get-tuple-element.31.refs_5_.refs_0_, bf16[4096,1024]{1,0:T(8,128)(2,1)S(1)} %bitcast.6, bf16[32,1024]{1,0:T(8,128)(2,1)S(1)} %get-tuple-element.29.refs_1_.refs_2_), custom_call_target="tpu_custom_call" | custom-call | flops 1073741824 | bytes 8388608 | tf_op jit(solution)/shard_map/base/pallas_call | solution.py:36
  17.6 0.3 collective-permute-done.6.refs_2_
  17.9 0.0 collective-permute-done.1.refs_4_.refs_1_
  17.9 0.3 low.1
  18.2 0.0 collective-permute-start.12
  18.2 0.6 %collective-permute-start.9 = (f32[32,128]{1,0:T(8,128)S(1)}, f32[32,128]{1,0:T(8,128)S(1)}, u32[]{:S(2)}, u32[]{:S(2)}) collective-permute-start(f32[32,128]{1,0:T(8,128)S(1)} %get-tuple-element.34.refs_3_.refs_0_), channel_id=1, source_target_pairs={{0,3},{1,2},{2,1},{3,0},{4,7},{5,6},{6,5},{7,4},{8,11},{9,10},{10,... | collective-permute-start | bytes 49160 | tf_op jit(solution)/shard_map/ppermute | solution.py:222
  18.7 1.6 %collective-permute-start.8 = (f32[32,128]{1,0:T(8,128)S(1)}, f32[32,128]{1,0:T(8,128)S(1)}, u32[]{:S(2)}, u32[]{:S(2)}) collective-permute-start(f32[32,128]{1,0:T(8,128)S(1)} %get-tuple-element.34.refs_3_.refs_0_), channel_id=1, source_target_pairs={{0,2},{1,3},{2,0},{3,1},{4,6},{5,7},{6,4},{7,5},{8,10},{9,11},{10,... | collective-permute-start | bytes 49160 | tf_op jit(solution)/shard_map/ppermute | solution.py:222
  20.3 0.0 collective-permute-start.7
  20.3 0.5 %collective-permute-start.10 = (bf16[16,1024]{1,0:T(8,128)(2,1)S(1)}, bf16[16,1024]{1,0:T(8,128)(2,1)S(1)}, u32[]{:S(2)}, u32[]{:S(2)}) collective-permute-start(bf16[16,1024]{1,0:T(8,128)(2,1)S(1)} %get-tuple-element.36), channel_id=1, source_target_pairs={{0,1},{1,0},{2,3},{3,2},{4,5},{5,4},{6,7},{7,6},{8,9},{9,8},{10,11... | collective-permute-start | bytes 98312 | tf_op jit(solution)/shard_map/ppermute | solution.py:222
  20.8 1.3 %mixed.1.refs_6_.refs_0_ = f32[128,1024]{1,0:T(8,128)S(1)} custom-call(bf16[2,32,4096]{2,1,0:T(8,128)(2,1)S(1)} %stack.1.refs_3_.refs_0_, bf16[2,32,4096]{2,1,0:T(8,128)(2,1)S(1)} %collective-permute-done.1.refs_4_.refs_1_, bf16[4096,1024]{1,0:T(8,128)(2,1)S(1)} %bitcast.6, f32[32,128]{1,0:T(8,128)S(1)} %get-tuple-element.34.refs_3_.refs_0_), custom_call_target="tpu_custom_call" | custom-call | flops 1073741824 | bytes 8388608 | tf_op jit(solution)/shard_map/mixed/pallas_call | solution.py:36
  22.2 0.0 collective-permute-done.9.refs_3_
  22.2 0.3 collective-permute-done.8.refs_2_
  22.5 0.0 collective-permute-done.7.refs_1_
  22.5 0.0 collective-permute-done.10.refs_7_.refs_4_
  22.5 0.2 gradient.1
  22.7 1.6 %collective-permute-start.11 = (bf16[32,1024]{1,0:T(8,128)(2,1)S(1)}, bf16[32,1024]{1,0:T(8,128)(2,1)S(1)}, u32[]{:S(2)}, u32[]{:S(2)}) collective-permute-start(bf16[32,1024]{1,0:T(8,128)(2,1)S(1)} %get-tuple-element.39.refs_1_), channel_id=1, source_target_pairs={{0,4},{4,0},{8,12},{12,8},{16,20},{20,16},{24,28},{28,24},{1,5},{5... | collective-permute-start | bytes 196616 | tf_op jit(solution)/shard_map/ppermute | solution.py:225
  24.3 0.0 collective-permute-done.12.refs_1_
  24.3 0.5 %add.1 = (f32[32,4096]{1,0:T(8,128)S(1)}, bf16[32,4096]{1,0:T(8,128)(2,1)S(1)}) custom-call(f32[2,32,4096]{2,1,0:T(8,128)S(1)} %get-tuple-element.40.refs_0_, f32[2,32,4096]{2,1,0:T(8,128)S(1)} %collective-permute-done.12.refs_1_, bf16[32,128]{1,0:T(8,128)(2,1)S(1)} %get-tuple-element.37.refs_2_.refs_1_, ...), custom_call_target="tpu_custom_call" | custom-call | tf_op jit(solution)/shard_map/add/pallas_call | solution.py:36
  24.8 1.6 %collective-permute-start.13 = (bf16[32,4096]{1,0:T(8,128)(2,1)S(1)}, bf16[32,4096]{1,0:T(8,128)(2,1)S(1)}, u32[]{:S(2)}, u32[]{:S(2)}) collective-permute-start(bf16[32,4096]{1,0:T(8,128)(2,1)S(1)} %get-tuple-element.42.refs_3_), channel_id=1, source_target_pairs={{0,2},{1,3},{2,0},{3,1},{4,6},{5,7},{6,4},{7,5},{8,10},{9,11},{10,... | collective-permute-start | bytes 786440 | tf_op jit(solution)/shard_map/ppermute | solution.py:222
  26.4 0.6 %collective-permute-done.11.refs_2_ = bf16[32,1024]{1,0:T(8,128)(2,1)S(1)} collective-permute-done((bf16[32,1024]{1,0:T(8,128)(2,1)S(1)}, bf16[32,1024]{1,0:T(8,128)(2,1)S(1)}, u32[]{:S(2)}, u32[]{:S(2)}) %collective-permute-start.11) | collective-permute-done | bytes 65568 | tf_op jit(solution)/shard_map/ppermute | solution.py:225
  27.0 0.1 route.1
  27.1 3.6 %collective-permute-start.14 = (bf16[32,1024]{1,0:T(8,128)(2,1)S(1)}, bf16[32,1024]{1,0:T(8,128)(2,1)S(1)}, u32[]{:S(2)}, u32[]{:S(2)}) collective-permute-start(bf16[32,1024]{1,0:T(8,128)(2,1)S(1)} %get-tuple-element.46), channel_id=1, source_target_pairs={{0,24},{4,28},{8,16},{12,20},{16,8},{20,12},{24,0},{28,4},{1,25},{... | collective-permute-start | bytes 196616 | tf_op jit(solution)/shard_map/ppermute | solution.py:228
  30.7 0.0 collective-permute-start.15
  30.7 0.8 %collective-permute-start.16 = (bf16[32,1024]{1,0:T(8,128)(2,1)S(1)}, bf16[32,1024]{1,0:T(8,128)(2,1)S(1)}, u32[]{:S(2)}, u32[]{:S(2)}) collective-permute-start(bf16[32,1024]{1,0:T(8,128)(2,1)S(1)} %get-tuple-element.48), channel_id=1, source_target_pairs={{0,8},{4,12},{8,0},{12,4},{16,24},{20,28},{24,16},{28,20},{1,9},{5... | collective-permute-start | bytes 196616 | tf_op jit(solution)/shard_map/ppermute | solution.py:228
  31.5 1.0 %finish.1 = bf16[128,1024]{1,0:T(8,128)(2,1)} custom-call(f32[128,1024]{1,0:T(8,128)S(1)} %mixed.1.refs_6_.refs_0_, bf16[32,128]{1,0:T(8,128)(2,1)S(1)} %get-tuple-element.37.refs_2_.refs_1_, bf16[32,1024]{1,0:T(8,128)(2,1)S(1)} %get-tuple-element.38.refs_3_.refs_2_, bf16[32,1024]{1,0:T(8,128)(2,1)S(1)} %get-tuple-element.43.refs_3_.refs_0_), custom_call_target="tpu_custom_call" | custom-call | flops 4294967296 | tf_op jit(solution)/shard_map/finish/pallas_call | solution.py:36
  32.5 0.0 collective-permute-done.13.refs_1_
  32.5 0.7 %close.1 = (bf16[32,4096]{1,0:T(8,128)(2,1)}, f32[8,128]{1,0:T(8,128)S(1)}) custom-call(f32[32,4096]{1,0:T(8,128)S(1)} %get-tuple-element.44.refs_0_, bf16[32,4096]{1,0:T(8,128)(2,1)S(1)} %collective-permute-done.13.refs_1_), custom_call_target="tpu_custom_call" | custom-call | tf_op jit(solution)/shard_map/close/pallas_call | solution.py:36
  33.2 0.1 collective-permute-done.14.refs_1_
  33.3 2.6 %collective-permute-done.15.refs_2_ = bf16[32,1024]{1,0:T(8,128)(2,1)S(1)} collective-permute-done((bf16[32,1024]{1,0:T(8,128)(2,1)S(1)}, bf16[32,1024]{1,0:T(8,128)(2,1)S(1)}, u32[]{:S(2)}, u32[]{:S(2)}) %collective-permute-start.15) | collective-permute-done | bytes 65568 | tf_op jit(solution)/shard_map/ppermute | solution.py:228
  35.9 0.0 collective-permute-done.16.refs_3_
  35.9 0.7 %sum.1 = (f32[1,16,1024]{2,1,0:T(8,128)}, f32[1,16,1024]{2,1,0:T(8,128)}) custom-call(bf16[32,1024]{1,0:T(8,128)(2,1)S(1)} %get-tuple-element.43.refs_3_.refs_0_, bf16[32,1024]{1,0:T(8,128)(2,1)S(1)} %collective-permute-done.14.refs_1_, bf16[32,1024]{1,0:T(8,128)(2,1)S(1)} %collective-permute-done.15.refs_2_, ...), custom_call_target="tpu_custom_call" | custom-call | tf_op jit(solution)/shard_map/sum/pallas_call | solution.py:36
  (5 shorter events, 0.1 us)
Async XLA Ops:
  0.6 10.4 %collective-permute-start = (bf16[32,4096]{1,0:T(8,128)(2,1)}, bf16[32,4096]{1,0:T(8,128)(2,1)S(1)}, u32[]{:S(2)}, u32[]{:S(2)}) collective-permute-start(bf16[32,4096]{1,0:T(8,128)(2,1)} %refs_0_.1), channel_id=1, source_target_pairs={{0,2},{1,3},{2,0},{3,1},{4,6},{5,7},{6,4},{7,5},{8,10},{9,11},{10,... | collective-permute-start | bytes 786440 | tf_op jit(solution)/shard_map/ppermute | solution.py:222
  4.4 8.9 %collective-permute-start.5 = (bf16[32,1024]{1,0:T(8,128)(2,1)S(1)}, bf16[32,1024]{1,0:T(8,128)(2,1)S(1)}, u32[]{:S(2)}, u32[]{:S(2)}) collective-permute-start(bf16[32,1024]{1,0:T(8,128)(2,1)S(1)} %pad_maximum_fusion.refs_0_), channel_id=1, source_target_pairs={{0,24},{4,28},{8,16},{12,20},{16,8},{20,12},{24,0},{28,4},{1,25},{... | collective-permute-start | bytes 196616 | tf_op jit(solution)/shard_map/ppermute | solution.py:228
  8.0 5.4 %collective-permute-start.4 = (bf16[32,1024]{1,0:T(8,128)(2,1)S(1)}, bf16[32,1024]{1,0:T(8,128)(2,1)S(1)}, u32[]{:S(2)}, u32[]{:S(2)}) collective-permute-start(bf16[32,1024]{1,0:T(8,128)(2,1)S(1)} %pad_maximum_fusion.refs_0_), channel_id=1, source_target_pairs={{0,16},{4,20},{8,24},{12,28},{16,0},{20,4},{24,8},{28,12},{1,17},{... | collective-permute-start | bytes 196616 | tf_op jit(solution)/shard_map/ppermute | solution.py:228
  8.0 5.4 %collective-permute-start.3 = (bf16[32,1024]{1,0:T(8,128)(2,1)S(1)}, bf16[32,1024]{1,0:T(8,128)(2,1)S(1)}, u32[]{:S(2)}, u32[]{:S(2)}) collective-permute-start(bf16[32,1024]{1,0:T(8,128)(2,1)S(1)} %pad_maximum_fusion.refs_0_), channel_id=1, source_target_pairs={{0,8},{4,12},{8,0},{12,4},{16,24},{20,28},{24,16},{28,20},{1,9},{5... | collective-permute-start | bytes 196616 | tf_op jit(solution)/shard_map/ppermute | solution.py:228
  9.5 1.6 %copy-start = (bf16[32,4096]{1,0:T(8,128)(2,1)S(1)}, bf16[32,4096]{1,0:T(8,128)(2,1)}, u32[]{:S(2)}) copy-start(bf16[32,4096]{1,0:T(8,128)(2,1)} %refs_0_.1) | copy-start | bytes 786436
  9.5 3.7 %collective-permute-start.2 = (s32[8,128]{1,0:T(8,128)S(1)}, s32[8,128]{1,0:T(8,128)S(1)}, u32[]{:S(2)}, u32[]{:S(2)}) collective-permute-start(s32[8,128]{1,0:T(8,128)S(1)} %broadcast_in_dim.8.refs_1_), channel_id=1, source_target_pairs={{0,4},{4,0},{8,12},{12,8},{16,20},{20,16},{24,28},{28,24},{1,5},{5... | collective-permute-start | bytes 12296 | tf_op jit(solution)/shard_map/ppermute | solution.py:225
  11.1 4.0 %slice-start = ((s8[8388608]{0:T(1024)(128)(4,1)}), s8[4194304]{0:T(1024)(128)(4,1)S(1)}, s32[]{:S(2)}) async-start(s8[8388608]{0:T(1024)(128)(4,1)} %bitcast.5), calls=%async_computation | async-start | bytes 8388608
  11.1 2.0 %copy-start.1 = (bf16[128,1024]{1,0:T(8,128)(2,1)S(1)}, bf16[128,1024]{1,0:T(8,128)(2,1)}, u32[]{:S(2)}) copy-start(bf16[128,1024]{1,0:T(8,128)(2,1)} %refs_3_.1) | copy-start | bytes 786436
  11.2 2.0 %copy-start.2 = (s32[8]{0:T(128)S(1)}, s32[8]{0:T(128)}, u32[]{:S(2)}) copy-start(s32[8]{0:T(128)} %param.13) | copy-start | bytes 100
  11.2 4.0 %slice-start.1 = ((s8[8388608]{0:T(1024)(128)(4,1)}), s8[4194304]{0:T(1024)(128)(4,1)S(1)}, s32[]{:S(2)}) async-start(s8[8388608]{0:T(1024)(128)(4,1)} %bitcast.5), calls=%async_computation.1 | async-start | bytes 8388608
  11.2 6.7 %collective-permute-start.1 = (bf16[2,32,4096]{2,1,0:T(8,128)(2,1)S(1)}, bf16[2,32,4096]{2,1,0:T(8,128)(2,1)S(1)}, u32[]{:S(2)}, u32[]{:S(2)}) collective-permute-start(bf16[2,32,4096]{2,1,0:T(8,128)(2,1)S(1)} %stack.1.refs_3_.refs_0_), channel_id=1, source_target_pairs={{0,1},{1,0},{2,3},{3,2},{4,5},{5,4},{6,7},{7,6},{8,9},{9,8},{10,11... | collective-permute-start | bytes 1572872 | tf_op jit(solution)/shard_map/ppermute | solution.py:222
  13.6 4.3 %collective-permute-start.6 = (bf16[32,1024]{1,0:T(8,128)(2,1)S(1)}, bf16[32,1024]{1,0:T(8,128)(2,1)S(1)}, u32[]{:S(2)}, u32[]{:S(2)}) collective-permute-start(bf16[32,1024]{1,0:T(8,128)(2,1)S(1)} %get-tuple-element.30), channel_id=1, source_target_pairs={{0,4},{4,0},{8,12},{12,8},{16,20},{20,16},{24,28},{28,24},{1,5},{5... | collective-permute-start | bytes 196616 | tf_op jit(solution)/shard_map/ppermute | solution.py:225
  18.2 6.1 %collective-permute-start.12 = (f32[2,32,4096]{2,1,0:T(8,128)S(1)}, f32[2,32,4096]{2,1,0:T(8,128)S(1)}, u32[]{:S(2)}, u32[]{:S(2)}) collective-permute-start(f32[2,32,4096]{2,1,0:T(8,128)S(1)} %get-tuple-element.41), channel_id=1, source_target_pairs={{0,1},{1,0},{2,3},{3,2},{4,5},{5,4},{6,7},{7,6},{8,9},{9,8},{10,11... | collective-permute-start | bytes 3145736 | tf_op jit(solution)/shard_map/ppermute | solution.py:222
  18.2 4.0 %collective-permute-start.9 = (f32[32,128]{1,0:T(8,128)S(1)}, f32[32,128]{1,0:T(8,128)S(1)}, u32[]{:S(2)}, u32[]{:S(2)}) collective-permute-start(f32[32,128]{1,0:T(8,128)S(1)} %get-tuple-element.34.refs_3_.refs_0_), channel_id=1, source_target_pairs={{0,3},{1,2},{2,1},{3,0},{4,7},{5,6},{6,5},{7,4},{8,11},{9,10},{10,... | collective-permute-start | bytes 49160 | tf_op jit(solution)/shard_map/ppermute | solution.py:222
  18.7 3.7 %collective-permute-start.8 = (f32[32,128]{1,0:T(8,128)S(1)}, f32[32,128]{1,0:T(8,128)S(1)}, u32[]{:S(2)}, u32[]{:S(2)}) collective-permute-start(f32[32,128]{1,0:T(8,128)S(1)} %get-tuple-element.34.refs_3_.refs_0_), channel_id=1, source_target_pairs={{0,2},{1,3},{2,0},{3,1},{4,6},{5,7},{6,4},{7,5},{8,10},{9,11},{10,... | collective-permute-start | bytes 49160 | tf_op jit(solution)/shard_map/ppermute | solution.py:222
  20.3 2.1 %collective-permute-start.7 = (f32[32,128]{1,0:T(8,128)S(1)}, f32[32,128]{1,0:T(8,128)S(1)}, u32[]{:S(2)}, u32[]{:S(2)}) collective-permute-start(f32[32,128]{1,0:T(8,128)S(1)} %get-tuple-element.34.refs_3_.refs_0_), channel_id=1, source_target_pairs={{0,1},{1,0},{2,3},{3,2},{4,5},{5,4},{6,7},{7,6},{8,9},{9,8},{10,11... | collective-permute-start | bytes 49160 | tf_op jit(solution)/shard_map/ppermute | solution.py:222
  20.3 2.1 %collective-permute-start.10 = (bf16[16,1024]{1,0:T(8,128)(2,1)S(1)}, bf16[16,1024]{1,0:T(8,128)(2,1)S(1)}, u32[]{:S(2)}, u32[]{:S(2)}) collective-permute-start(bf16[16,1024]{1,0:T(8,128)(2,1)S(1)} %get-tuple-element.36), channel_id=1, source_target_pairs={{0,1},{1,0},{2,3},{3,2},{4,5},{5,4},{6,7},{7,6},{8,9},{9,8},{10,11... | collective-permute-start | bytes 98312 | tf_op jit(solution)/shard_map/ppermute | solution.py:222
  22.7 4.3 %collective-permute-start.11 = (bf16[32,1024]{1,0:T(8,128)(2,1)S(1)}, bf16[32,1024]{1,0:T(8,128)(2,1)S(1)}, u32[]{:S(2)}, u32[]{:S(2)}) collective-permute-start(bf16[32,1024]{1,0:T(8,128)(2,1)S(1)} %get-tuple-element.39.refs_1_), channel_id=1, source_target_pairs={{0,4},{4,0},{8,12},{12,8},{16,20},{20,16},{24,28},{28,24},{1,5},{5... | collective-permute-start | bytes 196616 | tf_op jit(solution)/shard_map/ppermute | solution.py:225
  24.8 7.7 %collective-permute-start.13 = (bf16[32,4096]{1,0:T(8,128)(2,1)S(1)}, bf16[32,4096]{1,0:T(8,128)(2,1)S(1)}, u32[]{:S(2)}, u32[]{:S(2)}) collective-permute-start(bf16[32,4096]{1,0:T(8,128)(2,1)S(1)} %get-tuple-element.42.refs_3_), channel_id=1, source_target_pairs={{0,2},{1,3},{2,0},{3,1},{4,6},{5,7},{6,4},{7,5},{8,10},{9,11},{10,... | collective-permute-start | bytes 786440 | tf_op jit(solution)/shard_map/ppermute | solution.py:222
  27.1 6.2 %collective-permute-start.14 = (bf16[32,1024]{1,0:T(8,128)(2,1)S(1)}, bf16[32,1024]{1,0:T(8,128)(2,1)S(1)}, u32[]{:S(2)}, u32[]{:S(2)}) collective-permute-start(bf16[32,1024]{1,0:T(8,128)(2,1)S(1)} %get-tuple-element.46), channel_id=1, source_target_pairs={{0,24},{4,28},{8,16},{12,20},{16,8},{20,12},{24,0},{28,4},{1,25},{... | collective-permute-start | bytes 196616 | tf_op jit(solution)/shard_map/ppermute | solution.py:228
  30.7 5.2 %collective-permute-start.15 = (bf16[32,1024]{1,0:T(8,128)(2,1)S(1)}, bf16[32,1024]{1,0:T(8,128)(2,1)S(1)}, u32[]{:S(2)}, u32[]{:S(2)}) collective-permute-start(bf16[32,1024]{1,0:T(8,128)(2,1)S(1)} %get-tuple-element.47), channel_id=1, source_target_pairs={{0,16},{4,20},{8,24},{12,28},{16,0},{20,4},{24,8},{28,12},{1,17},{... | collective-permute-start | bytes 196616 | tf_op jit(solution)/shard_map/ppermute | solution.py:228
  30.7 5.2 %collective-permute-start.16 = (bf16[32,1024]{1,0:T(8,128)(2,1)S(1)}, bf16[32,1024]{1,0:T(8,128)(2,1)S(1)}, u32[]{:S(2)}, u32[]{:S(2)}) collective-permute-start(bf16[32,1024]{1,0:T(8,128)(2,1)S(1)} %get-tuple-element.48), channel_id=1, source_target_pairs={{0,8},{4,12},{8,0},{12,4},{16,24},{20,28},{24,16},{28,20},{1,9},{5... | collective-permute-start | bytes 196616 | tf_op jit(solution)/shard_map/ppermute | solution.py:228

commit v5 on v4

--- a/solution.py
+++ b/solution.py
@@ -286,6 +286,7 @@
             [vmem()] * (1 + outer),
             flops=flops,
             moved=small_bytes,
+            after=(pieces[1],),
         )
         keep, give = call(
             base_kernel,
@@ -299,6 +300,8 @@
             after=(found[0],),
         )
         found = [found[0]] + [over_inner(found[k], k) for k in range(1, inner)]
+        give, *found[1:] = lax.optimization_barrier((give, *found[1:]))
+        got = over_tensor(give, 1)
 
         both, chosen, columns, chosen_down = call(
             functools.partial(low_kernel, inner, tensor_size),
@@ -325,8 +328,6 @@
             weight_bytes,
             after=(both,),
         )
-        give, both = lax.optimization_barrier((give, both))
-        got = over_tensor(give, 1)
         sibling = over_tensor(chosen_down, 1)
         totals = [both] + [over_tensor(both, k) for k in range(1, tensor_size)]
 

time: 36.7 us -> 36.9 us (level)
  no operation moved by 1% of the time
where the time goes in v5:
time: 36.9 us; the launch traced here: 36.7 us
  starting transfers between devices  20.8 us (56%)
  Pallas kernels  7.42 us (20%)
  waiting for transfers between devices  6.17 us (17%)
  between operations  1.42 us (4%)
  other arithmetic  0.78 us (2%)
    ppermute x6, starting transfers between devices, over_outer(): return lax.ppermute(x, 'dp', [(d, d ^ k * inner) for d in range(dp_size)])  8.84 us
    pallas_call x14, Pallas kernels, call(): pl.pallas_call(run, name=name, out_shape=outs, in_specs=specs + [pl.Block...  7.42 us
    ppermute x8, starting transfers between devices, over_tensor(): return lax.ppermute(x, 'tensor', [(t, t ^ k) for t in range(tensor_size)])  7.35 us
    ppermute x3, starting transfers between devices, over_inner(): return lax.ppermute(x, 'dp', [(d, d ^ k) for d in range(dp_size)])  4.66 us
    ppermute x3, waiting for transfers between devices, over_inner(): return lax.ppermute(x, 'dp', [(d, d ^ k) for d in range(dp_size)])  2.95 us
    ppermute x6, waiting for transfers between devices, over_outer(): return lax.ppermute(x, 'dp', [(d, d ^ k * inner) for d in range(dp_size)])  2.81 us
    concatenate x1, other arithmetic, per_device(): mine = jnp.concatenate([down[0], up[0]], axis=0)  0.78 us
  transfers between devices with their start and end apart: 17, of which 8 were waited for; matrix products, arithmetic and copies ran while one was open for 2% of the time, Pallas kernels for 18%

profile of v5, /device:TPU:0, one launch (start us, length us, event | category | flops | bytes accessed | tf_op | source)
XLA Modules:
  0.0 36.7 jit_solution(16606920627484552648)
XLA Ops:
  0.6 3.0 %collective-permute-start = (bf16[32,4096]{1,0:T(8,128)(2,1)}, bf16[32,4096]{1,0:T(8,128)(2,1)S(1)}, u32[]{:S(2)}, u32[]{:S(2)}) collective-permute-start(bf16[32,4096]{1,0:T(8,128)(2,1)} %refs_0_.1), channel_id=1, source_target_pairs={{0,2},{1,3},{2,0},{3,1},{4,6},{5,7},{6,4},{7,5},{8,10},{9,11},{10,... | collective-permute-start | bytes 786440 | tf_op jit(solution)/shard_map/ppermute | solution.py:222
  3.7 0.8 %pad_maximum_fusion.refs_0_ = bf16[32,1024]{1,0:T(8,128)(2,1)S(1)} fusion(bf16[16,1024]{1,0:T(8,128)(2,1)} %bitcast.8, bf16[16,1024]{1,0:T(8,128)(2,1)} %bitcast.9), kind=kLoop, calls=%fused_computation | loop fusion | flops 131072 | bytes 131072 | tf_op jit(solution)/shard_map/concatenate | solution.py:237
  4.4 3.6 %collective-permute-start.5 = (bf16[32,1024]{1,0:T(8,128)(2,1)S(1)}, bf16[32,1024]{1,0:T(8,128)(2,1)S(1)}, u32[]{:S(2)}, u32[]{:S(2)}) collective-permute-start(bf16[32,1024]{1,0:T(8,128)(2,1)S(1)} %pad_maximum_fusion.refs_0_), channel_id=1, source_target_pairs={{0,24},{4,28},{8,16},{12,20},{16,8},{20,12},{24,0},{28,4},{1,25},{... | collective-permute-start | bytes 196616 | tf_op jit(solution)/shard_map/ppermute | solution.py:228
  8.0 0.0 collective-permute-start.4
  8.0 0.8 %collective-permute-start.3 = (bf16[32,1024]{1,0:T(8,128)(2,1)S(1)}, bf16[32,1024]{1,0:T(8,128)(2,1)S(1)}, u32[]{:S(2)}, u32[]{:S(2)}) collective-permute-start(bf16[32,1024]{1,0:T(8,128)(2,1)S(1)} %pad_maximum_fusion.refs_0_), channel_id=1, source_target_pairs={{0,8},{4,12},{8,0},{12,4},{16,24},{20,28},{24,16},{28,20},{1,9},{5... | collective-permute-start | bytes 196616 | tf_op jit(solution)/shard_map/ppermute | solution.py:228
  9.5 0.0 copy-start
  9.5 1.6 %collective-permute-start.2 = (s32[8,128]{1,0:T(8,128)S(1)}, s32[8,128]{1,0:T(8,128)S(1)}, u32[]{:S(2)}, u32[]{:S(2)}) collective-permute-start(s32[8,128]{1,0:T(8,128)S(1)} %broadcast_in_dim.8.refs_1_), channel_id=1, source_target_pairs={{0,4},{4,0},{8,12},{12,8},{16,20},{20,16},{24,28},{28,24},{1,5},{5... | collective-permute-start | bytes 12296 | tf_op jit(solution)/shard_map/ppermute | solution.py:225
  11.1 0.0 collective-permute-done.refs_1_
  11.1 0.0 copy-done
  11.1 0.0 slice-start
  11.1 0.0 copy-start.1
  11.2 0.0 copy-start.2
  11.2 0.0 slice-start.1
  11.2 0.1 collective-permute-start.1
  11.3 1.9 %collective-permute-done.2.refs_2_ = s32[8,128]{1,0:T(8,128)S(1)} collective-permute-done((s32[8,128]{1,0:T(8,128)S(1)}, s32[8,128]{1,0:T(8,128)S(1)}, u32[]{:S(2)}, u32[]{:S(2)}) %collective-permute-start.2) | collective-permute-done | bytes 4128 | tf_op jit(solution)/shard_map/ppermute | solution.py:225
  13.2 0.0 copy-done.1
  13.2 0.0 copy-done.2
  13.2 0.2 slots.1
  13.3 0.0 collective-permute-done.5.refs_4_
  13.3 0.1 collective-permute-done.4.refs_3_
  13.4 0.1 collective-permute-done.3.refs_2_
  13.5 0.0 collective-permute-done.1.refs_5_.refs_4_.refs_1_
  13.5 0.1 pick.1
  13.6 1.6 %collective-permute-start.6 = (bf16[32,1024]{1,0:T(8,128)(2,1)S(1)}, bf16[32,1024]{1,0:T(8,128)(2,1)S(1)}, u32[]{:S(2)}, u32[]{:S(2)}) collective-permute-start(bf16[32,1024]{1,0:T(8,128)(2,1)S(1)} %get-tuple-element.32), channel_id=1, source_target_pairs={{0,4},{4,0},{8,12},{12,8},{16,20},{20,16},{24,28},{28,24},{1,5},{5... | collective-permute-start | bytes 196616 | tf_op jit(solution)/shard_map/ppermute | solution.py:225
  15.1 0.0 slice-done
  15.1 0.0 slice-done.1
  15.1 2.4 %base.1 = (f32[2,32,4096]{2,1,0:T(8,128)S(1)}, f32[2,32,4096]{2,1,0:T(8,128)S(1)}) custom-call(bf16[128,1024]{1,0:T(8,128)(2,1)S(1)} %get-tuple-element.30.refs_0_.refs_5_, bf16[4096,1024]{1,0:T(8,128)(2,1)S(1)} %bitcast.6, bf16[32,1024]{1,0:T(8,128)(2,1)S(1)} %get-tuple-element.29.refs_2_.refs_1_), custom_call_target="tpu_custom_call" | custom-call | flops 1073741824 | bytes 8388608 | tf_op jit(solution)/shard_map/base/pallas_call | solution.py:36
  17.6 0.3 collective-permute-done.6.refs_2_
  17.9 0.0 collective-permute-start.12
  17.9 0.3 low.1
  18.2 0.7 %collective-permute-start.9 = (f32[32,128]{1,0:T(8,128)S(1)}, f32[32,128]{1,0:T(8,128)S(1)}, u32[]{:S(2)}, u32[]{:S(2)}) collective-permute-start(f32[32,128]{1,0:T(8,128)S(1)} %get-tuple-element.34.refs_3_.refs_0_), channel_id=1, source_target_pairs={{0,3},{1,2},{2,1},{3,0},{4,7},{5,6},{6,5},{7,4},{8,11},{9,10},{10,... | collective-permute-start | bytes 49160 | tf_op jit(solution)/shard_map/ppermute | solution.py:222
  18.8 1.5 %collective-permute-start.8 = (f32[32,128]{1,0:T(8,128)S(1)}, f32[32,128]{1,0:T(8,128)S(1)}, u32[]{:S(2)}, u32[]{:S(2)}) collective-permute-start(f32[32,128]{1,0:T(8,128)S(1)} %get-tuple-element.34.refs_3_.refs_0_), channel_id=1, source_target_pairs={{0,2},{1,3},{2,0},{3,1},{4,6},{5,7},{6,4},{7,5},{8,10},{9,11},{10,... | collective-permute-start | bytes 49160 | tf_op jit(solution)/shard_map/ppermute | solution.py:222
  20.3 0.0 collective-permute-start.7
  20.3 0.5 %collective-permute-start.10 = (bf16[16,1024]{1,0:T(8,128)(2,1)S(1)}, bf16[16,1024]{1,0:T(8,128)(2,1)S(1)}, u32[]{:S(2)}, u32[]{:S(2)}) collective-permute-start(bf16[16,1024]{1,0:T(8,128)(2,1)S(1)} %get-tuple-element.36), channel_id=1, source_target_pairs={{0,1},{1,0},{2,3},{3,2},{4,5},{5,4},{6,7},{7,6},{8,9},{9,8},{10,11... | collective-permute-start | bytes 98312 | tf_op jit(solution)/shard_map/ppermute | solution.py:222
  20.9 1.3 %mixed.1.refs_6_.refs_0_ = f32[128,1024]{1,0:T(8,128)S(1)} custom-call(bf16[2,32,4096]{2,1,0:T(8,128)(2,1)S(1)} %stack.1.refs_3_.refs_0_, bf16[2,32,4096]{2,1,0:T(8,128)(2,1)S(1)} %collective-permute-done.1.refs_5_.refs_4_.refs_1_, bf16[4096,1024]{1,0:T(8,128)(2,1)S(1)} %bitcast.6, f32[32,128]{1,0:T(8,128)S(1)} %get-tuple-element.34.refs_3_.refs_0_), custom_call_target="tpu_custom_call" | custom-call | flops 1073741824 | bytes 8388608 | tf_op jit(solution)/shard_map/mixed/pallas_call | solution.py:36
  22.2 0.0 collective-permute-done.9.refs_3_
  22.2 0.4 %collective-permute-done.8.refs_2_ = f32[32,128]{1,0:T(8,128)S(1)} collective-permute-done((f32[32,128]{1,0:T(8,128)S(1)}, f32[32,128]{1,0:T(8,128)S(1)}, u32[]{:S(2)}, u32[]{:S(2)}) %collective-permute-start.8) | collective-permute-done | bytes 16416 | tf_op jit(solution)/shard_map/ppermute | solution.py:222
  22.6 0.0 collective-permute-done.7.refs_1_
  22.6 0.0 collective-permute-done.10.refs_7_.refs_4_
  22.6 0.2 gradient.1
  22.8 1.5 %collective-permute-start.11 = (bf16[32,1024]{1,0:T(8,128)(2,1)S(1)}, bf16[32,1024]{1,0:T(8,128)(2,1)S(1)}, u32[]{:S(2)}, u32[]{:S(2)}) collective-permute-start(bf16[32,1024]{1,0:T(8,128)(2,1)S(1)} %get-tuple-element.39.refs_1_), channel_id=1, source_target_pairs={{0,4},{4,0},{8,12},{12,8},{16,20},{20,16},{24,28},{28,24},{1,5},{5... | collective-permute-start | bytes 196616 | tf_op jit(solution)/shard_map/ppermute | solution.py:225
  24.3 0.0 collective-permute-done.12.refs_1_
  24.3 0.5 %add.1 = (f32[32,4096]{1,0:T(8,128)S(1)}, bf16[32,4096]{1,0:T(8,128)(2,1)S(1)}) custom-call(f32[2,32,4096]{2,1,0:T(8,128)S(1)} %get-tuple-element.40.refs_0_, f32[2,32,4096]{2,1,0:T(8,128)S(1)} %collective-permute-done.12.refs_1_, bf16[32,128]{1,0:T(8,128)(2,1)S(1)} %get-tuple-element.37.refs_2_.refs_1_, ...), custom_call_target="tpu_custom_call" | custom-call | tf_op jit(solution)/shard_map/add/pallas_call | solution.py:36
  24.8 1.6 %collective-permute-start.13 = (bf16[32,4096]{1,0:T(8,128)(2,1)S(1)}, bf16[32,4096]{1,0:T(8,128)(2,1)S(1)}, u32[]{:S(2)}, u32[]{:S(2)}) collective-permute-start(bf16[32,4096]{1,0:T(8,128)(2,1)S(1)} %get-tuple-element.42.refs_3_), channel_id=1, source_target_pairs={{0,2},{1,3},{2,0},{3,1},{4,6},{5,7},{6,4},{7,5},{8,10},{9,11},{10,... | collective-permute-start | bytes 786440 | tf_op jit(solution)/shard_map/ppermute | solution.py:222
  26.4 0.7 %collective-permute-done.11.refs_2_ = bf16[32,1024]{1,0:T(8,128)(2,1)S(1)} collective-permute-done((bf16[32,1024]{1,0:T(8,128)(2,1)S(1)}, bf16[32,1024]{1,0:T(8,128)(2,1)S(1)}, u32[]{:S(2)}, u32[]{:S(2)}) %collective-permute-start.11) | collective-permute-done | bytes 65568 | tf_op jit(solution)/shard_map/ppermute | solution.py:225
  27.1 0.1 route.1
  27.2 3.7 %collective-permute-start.14 = (bf16[32,1024]{1,0:T(8,128)(2,1)S(1)}, bf16[32,1024]{1,0:T(8,128)(2,1)S(1)}, u32[]{:S(2)}, u32[]{:S(2)}) collective-permute-start(bf16[32,1024]{1,0:T(8,128)(2,1)S(1)} %get-tuple-element.46), channel_id=1, source_target_pairs={{0,24},{4,28},{8,16},{12,20},{16,8},{20,12},{24,0},{28,4},{1,25},{... | collective-permute-start | bytes 196616 | tf_op jit(solution)/shard_map/ppermute | solution.py:228
  30.8 0.0 collective-permute-start.15
  30.8 0.8 %collective-permute-start.16 = (bf16[32,1024]{1,0:T(8,128)(2,1)S(1)}, bf16[32,1024]{1,0:T(8,128)(2,1)S(1)}, u32[]{:S(2)}, u32[]{:S(2)}) collective-permute-start(bf16[32,1024]{1,0:T(8,128)(2,1)S(1)} %get-tuple-element.48), channel_id=1, source_target_pairs={{0,8},{4,12},{8,0},{12,4},{16,24},{20,28},{24,16},{28,20},{1,9},{5... | collective-permute-start | bytes 196616 | tf_op jit(solution)/shard_map/ppermute | solution.py:228
  31.6 1.0 %finish.1 = bf16[128,1024]{1,0:T(8,128)(2,1)} custom-call(f32[128,1024]{1,0:T(8,128)S(1)} %mixed.1.refs_6_.refs_0_, bf16[32,128]{1,0:T(8,128)(2,1)S(1)} %get-tuple-element.37.refs_2_.refs_1_, bf16[32,1024]{1,0:T(8,128)(2,1)S(1)} %get-tuple-element.38.refs_3_.refs_2_, bf16[32,1024]{1,0:T(8,128)(2,1)S(1)} %get-tuple-element.43.refs_3_.refs_0_), custom_call_target="tpu_custom_call" | custom-call | flops 4294967296 | tf_op jit(solution)/shard_map/finish/pallas_call | solution.py:36
  32.6 0.0 collective-permute-done.13.refs_1_
  32.6 0.7 %close.1 = (bf16[32,4096]{1,0:T(8,128)(2,1)}, f32[8,128]{1,0:T(8,128)S(1)}) custom-call(f32[32,4096]{1,0:T(8,128)S(1)} %get-tuple-element.44.refs_0_, bf16[32,4096]{1,0:T(8,128)(2,1)S(1)} %collective-permute-done.13.refs_1_), custom_call_target="tpu_custom_call" | custom-call | tf_op jit(solution)/shard_map/close/pallas_call | solution.py:36
  33.3 0.1 collective-permute-done.14.refs_1_
  33.4 2.6 %collective-permute-done.15.refs_2_ = bf16[32,1024]{1,0:T(8,128)(2,1)S(1)} collective-permute-done((bf16[32,1024]{1,0:T(8,128)(2,1)S(1)}, bf16[32,1024]{1,0:T(8,128)(2,1)S(1)}, u32[]{:S(2)}, u32[]{:S(2)}) %collective-permute-start.15) | collective-permute-done | bytes 65568 | tf_op jit(solution)/shard_map/ppermute | solution.py:228
  36.0 0.0 collective-permute-done.16.refs_3_
  36.0 0.7 %sum.1 = (f32[1,16,1024]{2,1,0:T(8,128)}, f32[1,16,1024]{2,1,0:T(8,128)}) custom-call(bf16[32,1024]{1,0:T(8,128)(2,1)S(1)} %get-tuple-element.43.refs_3_.refs_0_, bf16[32,1024]{1,0:T(8,128)(2,1)S(1)} %collective-permute-done.14.refs_1_, bf16[32,1024]{1,0:T(8,128)(2,1)S(1)} %collective-permute-done.15.refs_2_, ...), custom_call_target="tpu_custom_call" | custom-call | tf_op jit(solution)/shard_map/sum/pallas_call | solution.py:36
  (5 shorter events, 0.1 us)
Async XLA Ops:
  0.6 10.4 %collective-permute-start = (bf16[32,4096]{1,0:T(8,128)(2,1)}, bf16[32,4096]{1,0:T(8,128)(2,1)S(1)}, u32[]{:S(2)}, u32[]{:S(2)}) collective-permute-start(bf16[32,4096]{1,0:T(8,128)(2,1)} %refs_0_.1), channel_id=1, source_target_pairs={{0,2},{1,3},{2,0},{3,1},{4,6},{5,7},{6,4},{7,5},{8,10},{9,11},{10,... | collective-permute-start | bytes 786440 | tf_op jit(solution)/shard_map/ppermute | solution.py:222
  4.4 8.9 %collective-permute-start.5 = (bf16[32,1024]{1,0:T(8,128)(2,1)S(1)}, bf16[32,1024]{1,0:T(8,128)(2,1)S(1)}, u32[]{:S(2)}, u32[]{:S(2)}) collective-permute-start(bf16[32,1024]{1,0:T(8,128)(2,1)S(1)} %pad_maximum_fusion.refs_0_), channel_id=1, source_target_pairs={{0,24},{4,28},{8,16},{12,20},{16,8},{20,12},{24,0},{28,4},{1,25},{... | collective-permute-start | bytes 196616 | tf_op jit(solution)/shard_map/ppermute | solution.py:228
  8.0 5.4 %collective-permute-start.4 = (bf16[32,1024]{1,0:T(8,128)(2,1)S(1)}, bf16[32,1024]{1,0:T(8,128)(2,1)S(1)}, u32[]{:S(2)}, u32[]{:S(2)}) collective-permute-start(bf16[32,1024]{1,0:T(8,128)(2,1)S(1)} %pad_maximum_fusion.refs_0_), channel_id=1, source_target_pairs={{0,16},{4,20},{8,24},{12,28},{16,0},{20,4},{24,8},{28,12},{1,17},{... | collective-permute-start | bytes 196616 | tf_op jit(solution)/shard_map/ppermute | solution.py:228
  8.0 5.4 %collective-permute-start.3 = (bf16[32,1024]{1,0:T(8,128)(2,1)S(1)}, bf16[32,1024]{1,0:T(8,128)(2,1)S(1)}, u32[]{:S(2)}, u32[]{:S(2)}) collective-permute-start(bf16[32,1024]{1,0:T(8,128)(2,1)S(1)} %pad_maximum_fusion.refs_0_), channel_id=1, source_target_pairs={{0,8},{4,12},{8,0},{12,4},{16,24},{20,28},{24,16},{28,20},{1,9},{5... | collective-permute-start | bytes 196616 | tf_op jit(solution)/shard_map/ppermute | solution.py:228
  9.5 1.6 %copy-start = (bf16[32,4096]{1,0:T(8,128)(2,1)S(1)}, bf16[32,4096]{1,0:T(8,128)(2,1)}, u32[]{:S(2)}) copy-start(bf16[32,4096]{1,0:T(8,128)(2,1)} %refs_0_.1) | copy-start | bytes 786436
  9.5 3.7 %collective-permute-start.2 = (s32[8,128]{1,0:T(8,128)S(1)}, s32[8,128]{1,0:T(8,128)S(1)}, u32[]{:S(2)}, u32[]{:S(2)}) collective-permute-start(s32[8,128]{1,0:T(8,128)S(1)} %broadcast_in_dim.8.refs_1_), channel_id=1, source_target_pairs={{0,4},{4,0},{8,12},{12,8},{16,20},{20,16},{24,28},{28,24},{1,5},{5... | collective-permute-start | bytes 12296 | tf_op jit(solution)/shard_map/ppermute | solution.py:225
  11.1 4.0 %slice-start = ((s8[8388608]{0:T(1024)(128)(4,1)}), s8[4194304]{0:T(1024)(128)(4,1)S(1)}, s32[]{:S(2)}) async-start(s8[8388608]{0:T(1024)(128)(4,1)} %bitcast.5), calls=%async_computation | async-start | bytes 8388608
  11.1 2.0 %copy-start.1 = (bf16[128,1024]{1,0:T(8,128)(2,1)S(1)}, bf16[128,1024]{1,0:T(8,128)(2,1)}, u32[]{:S(2)}) copy-start(bf16[128,1024]{1,0:T(8,128)(2,1)} %refs_3_.1) | copy-start | bytes 786436
  11.2 2.0 %copy-start.2 = (s32[8]{0:T(128)S(1)}, s32[8]{0:T(128)}, u32[]{:S(2)}) copy-start(s32[8]{0:T(128)} %param.13) | copy-start | bytes 100
  11.2 4.0 %slice-start.1 = ((s8[8388608]{0:T(1024)(128)(4,1)}), s8[4194304]{0:T(1024)(128)(4,1)S(1)}, s32[]{:S(2)}) async-start(s8[8388608]{0:T(1024)(128)(4,1)} %bitcast.5), calls=%async_computation.1 | async-start | bytes 8388608
  11.2 2.3 %collective-permute-start.1 = (bf16[2,32,4096]{2,1,0:T(8,128)(2,1)S(1)}, bf16[2,32,4096]{2,1,0:T(8,128)(2,1)S(1)}, u32[]{:S(2)}, u32[]{:S(2)}) collective-permute-start(bf16[2,32,4096]{2,1,0:T(8,128)(2,1)S(1)} %stack.1.refs_3_.refs_0_), channel_id=1, source_target_pairs={{0,1},{1,0},{2,3},{3,2},{4,5},{5,4},{6,7},{7,6},{8,9},{9,8},{10,11... | collective-permute-start | bytes 1572872 | tf_op jit(solution)/shard_map/ppermute | solution.py:222
  13.6 4.3 %collective-permute-start.6 = (bf16[32,1024]{1,0:T(8,128)(2,1)S(1)}, bf16[32,1024]{1,0:T(8,128)(2,1)S(1)}, u32[]{:S(2)}, u32[]{:S(2)}) collective-permute-start(bf16[32,1024]{1,0:T(8,128)(2,1)S(1)} %get-tuple-element.32), channel_id=1, source_target_pairs={{0,4},{4,0},{8,12},{12,8},{16,20},{20,16},{24,28},{28,24},{1,5},{5... | collective-permute-start | bytes 196616 | tf_op jit(solution)/shard_map/ppermute | solution.py:225
  17.9 6.4 %collective-permute-start.12 = (f32[2,32,4096]{2,1,0:T(8,128)S(1)}, f32[2,32,4096]{2,1,0:T(8,128)S(1)}, u32[]{:S(2)}, u32[]{:S(2)}) collective-permute-start(f32[2,32,4096]{2,1,0:T(8,128)S(1)} %get-tuple-element.41), channel_id=1, source_target_pairs={{0,1},{1,0},{2,3},{3,2},{4,5},{5,4},{6,7},{7,6},{8,9},{9,8},{10,11... | collective-permute-start | bytes 3145736 | tf_op jit(solution)/shard_map/ppermute | solution.py:222
  18.2 4.0 %collective-permute-start.9 = (f32[32,128]{1,0:T(8,128)S(1)}, f32[32,128]{1,0:T(8,128)S(1)}, u32[]{:S(2)}, u32[]{:S(2)}) collective-permute-start(f32[32,128]{1,0:T(8,128)S(1)} %get-tuple-element.34.refs_3_.refs_0_), channel_id=1, source_target_pairs={{0,3},{1,2},{2,1},{3,0},{4,7},{5,6},{6,5},{7,4},{8,11},{9,10},{10,... | collective-permute-start | bytes 49160 | tf_op jit(solution)/shard_map/ppermute | solution.py:222
  18.8 3.7 %collective-permute-start.8 = (f32[32,128]{1,0:T(8,128)S(1)}, f32[32,128]{1,0:T(8,128)S(1)}, u32[]{:S(2)}, u32[]{:S(2)}) collective-permute-start(f32[32,128]{1,0:T(8,128)S(1)} %get-tuple-element.34.refs_3_.refs_0_), channel_id=1, source_target_pairs={{0,2},{1,3},{2,0},{3,1},{4,6},{5,7},{6,4},{7,5},{8,10},{9,11},{10,... | collective-permute-start | bytes 49160 | tf_op jit(solution)/shard_map/ppermute | solution.py:222
  20.3 2.2 %collective-permute-start.7 = (f32[32,128]{1,0:T(8,128)S(1)}, f32[32,128]{1,0:T(8,128)S(1)}, u32[]{:S(2)}, u32[]{:S(2)}) collective-permute-start(f32[32,128]{1,0:T(8,128)S(1)} %get-tuple-element.34.refs_3_.refs_0_), channel_id=1, source_target_pairs={{0,1},{1,0},{2,3},{3,2},{4,5},{5,4},{6,7},{7,6},{8,9},{9,8},{10,11... | collective-permute-start | bytes 49160 | tf_op jit(solution)/shard_map/ppermute | solution.py:222
  20.3 2.2 %collective-permute-start.10 = (bf16[16,1024]{1,0:T(8,128)(2,1)S(1)}, bf16[16,1024]{1,0:T(8,128)(2,1)S(1)}, u32[]{:S(2)}, u32[]{:S(2)}) collective-permute-start(bf16[16,1024]{1,0:T(8,128)(2,1)S(1)} %get-tuple-element.36), channel_id=1, source_target_pairs={{0,1},{1,0},{2,3},{3,2},{4,5},{5,4},{6,7},{7,6},{8,9},{9,8},{10,11... | collective-permute-start | bytes 98312 | tf_op jit(solution)/shard_map/ppermute | solution.py:222
  22.8 4.3 %collective-permute-start.11 = (bf16[32,1024]{1,0:T(8,128)(2,1)S(1)}, bf16[32,1024]{1,0:T(8,128)(2,1)S(1)}, u32[]{:S(2)}, u32[]{:S(2)}) collective-permute-start(bf16[32,1024]{1,0:T(8,128)(2,1)S(1)} %get-tuple-element.39.refs_1_), channel_id=1, source_target_pairs={{0,4},{4,0},{8,12},{12,8},{16,20},{20,16},{24,28},{28,24},{1,5},{5... | collective-permute-start | bytes 196616 | tf_op jit(solution)/shard_map/ppermute | solution.py:225
  24.8 7.8 %collective-permute-start.13 = (bf16[32,4096]{1,0:T(8,128)(2,1)S(1)}, bf16[32,4096]{1,0:T(8,128)(2,1)S(1)}, u32[]{:S(2)}, u32[]{:S(2)}) collective-permute-start(bf16[32,4096]{1,0:T(8,128)(2,1)S(1)} %get-tuple-element.42.refs_3_), channel_id=1, source_target_pairs={{0,2},{1,3},{2,0},{3,1},{4,6},{5,7},{6,4},{7,5},{8,10},{9,11},{10,... | collective-permute-start | bytes 786440 | tf_op jit(solution)/shard_map/ppermute | solution.py:222
  27.2 6.2 %collective-permute-start.14 = (bf16[32,1024]{1,0:T(8,128)(2,1)S(1)}, bf16[32,1024]{1,0:T(8,128)(2,1)S(1)}, u32[]{:S(2)}, u32[]{:S(2)}) collective-permute-start(bf16[32,1024]{1,0:T(8,128)(2,1)S(1)} %get-tuple-element.46), channel_id=1, source_target_pairs={{0,24},{4,28},{8,16},{12,20},{16,8},{20,12},{24,0},{28,4},{1,25},{... | collective-permute-start | bytes 196616 | tf_op jit(solution)/shard_map/ppermute | solution.py:228
  30.8 5.2 %collective-permute-start.15 = (bf16[32,1024]{1,0:T(8,128)(2,1)S(1)}, bf16[32,1024]{1,0:T(8,128)(2,1)S(1)}, u32[]{:S(2)}, u32[]{:S(2)}) collective-permute-start(bf16[32,1024]{1,0:T(8,128)(2,1)S(1)} %get-tuple-element.47), channel_id=1, source_target_pairs={{0,16},{4,20},{8,24},{12,28},{16,0},{20,4},{24,8},{28,12},{1,17},{... | collective-permute-start | bytes 196616 | tf_op jit(solution)/shard_map/ppermute | solution.py:228
  30.8 5.2 %collective-permute-start.16 = (bf16[32,1024]{1,0:T(8,128)(2,1)S(1)}, bf16[32,1024]{1,0:T(8,128)(2,1)S(1)}, u32[]{:S(2)}, u32[]{:S(2)}) collective-permute-start(bf16[32,1024]{1,0:T(8,128)(2,1)S(1)} %get-tuple-element.48), channel_id=1, source_target_pairs={{0,8},{4,12},{8,0},{12,4},{16,24},{20,28},{24,16},{28,20},{1,9},{5... | collective-permute-start | bytes 196616 | tf_op jit(solution)/shard_map/ppermute | solution.py:228
